TPU v7x, 128 devices: a whole 4x4x4 slice. The times are simulated.
128 devices in a mesh: tm: 128 (over z, y, x, core).
Axes of the slice: x: 4, y: 4, z: 4, core: 2. Of those that a mesh axis runs over, the one named last changes fastest.
Arguments:
- hidden: bfloat16 [49152, 8192], P('tm'), may hold values from -6 to 6
- norm_gain: float32 [8192], replicated, may hold values from 0.1 to 1.9
- w_in: bfloat16 [8192, 768], replicated, may hold values from -0.0625 to 0.0625
- w_short: float32 [768, 7], replicated, may hold values from -2 to 2
- residues: float32 [8, 16], replicated, may hold values from -4 to 4
- rates: float32 [8, 16], replicated, may hold values from 4.06901042e-06 to 0.0333333333, as said below
- skip: float32 [256], replicated, may hold values from -4 to 4
- w_out: bfloat16 [256, 8192], replicated, may hold values from -0.375 to 0.375
Outputs:
- mixed: bfloat16 [49152, 8192], P('tm')
Inputs may be any that keep to these rules, and one draw needn't show every extreme that they name: `rates`: every rate is positive.
All inputs are finite; a program needn't handle non-finite values.
Results may differ from a plain program's by a relative error of at most 0.0088.
Values may be sent and summed in bfloat16 or wider, within the bound.
No kernel may reach another device: no remote copies, remote signals or barrier semaphores. Data moves between devices by JAX's collectives and lax.ppermute only.
A program may use at most 256 MiB of HBM per device.

v0:
```python
import jax
import jax.numpy as jnp
from jax import lax
from jax.sharding import PartitionSpec as P

HIGHEST = lax.Precision.HIGHEST


def shifted(block, axis, distance):
    devices = range(lax.axis_size(axis))
    route = [(i - distance, i) for i in devices if i - distance in devices]
    return lax.ppermute(block, axis, route)


def own_block(fragment, tok_rows, rates, residues):
    weights = residues * jnp.sqrt(2.0 * rates)
    steps_idx = jnp.arange(tok_rows, dtype=jnp.int32)
    lag_matrix = (steps_idx[None, :] - steps_idx[:, None]).astype(jnp.float32)
    decays = jnp.exp(-rates[:, :, None, None] * jnp.maximum(lag_matrix, 0.0)[None, None, :, :])
    toeplitz = jnp.einsum("gm,gmst->gst", weights, decays, precision=HIGHEST)
    toeplitz = jnp.where((lag_matrix >= 0.0)[None, :, :], toeplitz, 0.0)
    return jnp.einsum(
        "gcs,gst->gct", fragment, toeplitz, precision=HIGHEST, preferred_element_type=jnp.float32
    )


def on_device(hidden, norm_gain, w_in, w_short, residues, rates, skip, w_out):
    tok_rows = hidden.shape[0]
    chan_total = w_short.shape[0] // 3
    group_count = rates.shape[0]
    chan_group = chan_total // group_count
    tap_count = w_short.shape[1]
    own_start = lax.axis_index("tm") * tok_rows
    widened = hidden.astype(jnp.float32)
    inv_scale = lax.rsqrt(jnp.mean(widened * widened, axis=1, keepdims=True) + 1e-06)
    normed = (widened * inv_scale * norm_gain).astype(jnp.bfloat16)
    projected = lax.dot_general(
        w_in, normed, (((0,), (1,)), ((), ())), preferred_element_type=jnp.float32
    ).astype(jnp.bfloat16)
    edge_cols = shifted(projected[:, tok_rows - (tap_count - 1) :], "tm", 1)
    extended = jnp.concatenate([edge_cols, projected], axis=1).astype(jnp.float32)
    features = jnp.zeros(projected.shape, jnp.float32)
    for offset_tap in range(tap_count):
        begin = tap_count - 1 - offset_tap
        features = (
            features
            + w_short[:, offset_tap : offset_tap + 1] * extended[:, begin : begin + tok_rows]
        )
    queries = features[:chan_total]
    keyed = features[chan_total : 2 * chan_total]
    valued = features[2 * chan_total :]
    product = (keyed * valued).astype(jnp.bfloat16)
    product_wide = product.astype(jnp.float32).reshape(group_count, chan_group, tok_rows)
    local_part = own_block(product_wide, tok_rows, rates, residues)
    positions = jnp.arange(tok_rows, dtype=jnp.float32)
    fragment = lax.all_gather(product, "tm", axis=1, tiled=True)
    width = fragment.shape[1]
    spots = jnp.arange(width, dtype=jnp.int32)
    distance = (own_start - 1 - spots).astype(jnp.float32)
    factor = jnp.exp(-rates[:, None, :] * jnp.maximum(distance, 0.0)[None, :, None])
    factor = jnp.where((spots < own_start)[None, :, None], factor, 0.0)
    grouped = fragment.astype(jnp.float32).reshape(group_count, chan_group, width)
    states = jnp.einsum(
        "gcw,gwm->gcm", grouped, factor, precision=HIGHEST, preferred_element_type=jnp.float32
    )
    weights = residues * jnp.sqrt(2.0 * rates)
    rising = jnp.exp(-rates[:, :, None] * (positions + 1.0)[None, None, :])
    convolved = local_part + jnp.einsum(
        "gcm,gmt->gct",
        states * weights[:, None, :],
        rising,
        precision=HIGHEST,
        preferred_element_type=jnp.float32,
    )
    convolved = convolved.reshape(chan_total, tok_rows)
    product_flat = product_wide.reshape(chan_total, tok_rows)
    gated = (queries * (convolved + skip[:, None] * product_flat)).astype(jnp.bfloat16)
    mixed = lax.dot_general(
        gated, w_out, (((0,), (0,)), ((), ())), preferred_element_type=jnp.float32
    )
    return mixed.astype(jnp.bfloat16)


def solution(mesh):
    return jax.shard_map(
        on_device,
        mesh=mesh,
        in_specs=(P("tm", None), P(), P(), P(), P(), P(), P(), P()),
        out_specs=P("tm", None),
        check_vma=False,
    )
```

profile of v0, /device:TPU:32, one launch (start us, length us, event | category | flops | bytes accessed | tf_op | source)
XLA Modules:
  0.0 230.6 jit_solution(6560298311716021537)
XLA Ops:
  6.5 0.0 all-gather.2.cloned.1.call-start
  6.5 0.0 copy-start
  6.5 4.3 %fusion.6 = f32[384]{0:T(512)S(1)} fusion(bf16[384,8192]{1,0:T(8,128)(2,1)} %param.8), kind=kLoop, calls=%fused_computation.9 | loop fusion | flops 9436800 | bytes 6292992 | tf_op jit(solution)/shard_map/reduce_sum | solution.py:35
  10.8 0.3 copy-done
  11.1 0.0 copy-start.2
  11.1 8.3 %fusion.24 = bf16[768,384]{0,1:T(8,128)(2,1)S(1)} fusion(bf16[8192,768]{1,0:T(8,128)(2,1)} %param.10, bf16[384,8192]{1,0:T(8,128)(2,1)S(1)} %copy-done, f32[8192]{0:T(1024)} %param.9, f32[384]{0:T(512)S(1)} %add_rsqrt_fusion), kind=kOutput, calls=%fused_computation.26 | convolution fusion | flops 4844716032 | bytes 19498496 | tf_op jit(solution)/shard_map/dot_general | solution.py:37
  19.5 1.9 collective-permute-start
  21.4 0.0 copy-done.2
  21.4 0.1 slice_reduce_fusion.6
  21.5 7.2 %collective-permute-done = bf16[768,6]{0,1:T(8,128)(2,1)S(1)} collective-permute-done((bf16[768,6]{0,1:T(8,128)(2,1)S(1)}, bf16[768,6]{0,1:T(8,128)(2,1)S(1)}, u32[]{:S(2)}, u32[]{:S(2)}) %collective-permute-start) | collective-permute-done | bytes 9248 | tf_op jit(solution)/shard_map/ppermute | solution.py:12
  28.7 0.1 maximum_convert_fusion
  28.8 0.0 copy-start.4
  28.8 0.0 copy-start.5
  28.9 1.0 fusion.27
  29.8 0.7 fusion.36
  30.5 0.0 all-gather.2.cloned.1.call-update
  30.6 0.1 convert_compare_fusion
  30.7 0.1 convert_maximum_fusion
  30.8 0.0 copy-done.4
  30.8 0.0 copy-done.5
  30.9 24.4 %multiply_exponential_fusion = f32[8,16,384,384]{3,2,1,0:T(8,128)} fusion(f32[384,384]{1,0:T(8,128)S(1)} %convert_maximum_fusion, f32[8,16]{1,0:T(8,128)S(1)} %get-tuple-element.12), kind=kLoop, calls=%fused_computation.2 | loop fusion | flops 18874368 | bytes 76087808 | tf_op jit(solution)/shard_map/exp | solution.py:19
  55.3 0.0 copy-start.1
  55.3 98.0 %fusion = f32[8,1,384,384]{3,1,2,0:T(1,128)} fusion(f32[8,16,1,1]{1,2,3,0:T(1,128)S(1)} %bitcast.20, f32[8,16,384,384]{3,2,1,0:T(8,128)} %multiply_exponential_fusion), kind=kOutput, calls=%fused_computation | convolution fusion | flops 226492416 | bytes 80216576 | tf_op jit(solution)/shard_map/gm,gmst->gst/dot_general | solution.py:20
  153.4 0.0 copy-done.1
  153.4 0.2 copy.14
  153.5 4.4 %fusion.17 = f32[8,32,384]{2,1,0:T(8,128)S(1)} fusion(bf16[8,32,384]{2,1,0:T(8,128)(2,1)S(1)} %bitcast.19, f32[8,1,384,384]{3,1,2,0:T(1,128)} %fusion, pred[384,384]{1,0:T(8,128)(4,1)S(1)} %convert_compare_fusion), kind=kOutput, calls=%fused_computation.21 | convolution fusion | flops 454164480 | bytes 5455872 | tf_op jit(solution)/shard_map/gcs,gst->gct/dot_general | solution.py:22
  157.9 0.0 all-gather.2.cloned.1.call-done
  157.9 32.7 %copy.15 = bf16[256,49152]{1,0:T(8,128)(2,1)} copy(bf16[256,49152]{0,1:T(8,128)(2,1)} %all-gather.2.cloned.1.call-done) | data formatting | bytes 50331648 | tf_op jit(solution)/shard_map/all_gather | solution.py:56
  190.6 0.0 copy-start.3
  190.6 25.6 %fusion.33 = f32[8,32,16]{1,2,0:T(8,128)S(1)} fusion(bf16[8,32,49152]{2,1,0:T(8,128)(2,1)} %bitcast.17, f32[49152]{0:T(1024)S(1)} %convert_maximum_fusion.1, f32[8,16]{1,0:T(8,128)S(1)} %get-tuple-element.12, pred[49152]{0:T(1024)(128)(4,1)S(1)} %iota_compare_fusion, f32[8,16]{1,0:T(8,128)S(1)} %get-tuple-element.13), kind=kOutput, calls=%fused_computation.41 | convolution fusion | flops 2428506112 | bytes 25428992 | tf_op jit(solution)/shard_map/gcw,gwm->gcm/dot_general | solution.py:63
  216.3 0.6 convolution_add_fusion
  216.9 0.2 copy.16
  217.0 0.0 copy-done.3
  217.1 6.7 %convolution_convert_fusion = bf16[384,8192]{1,0:T(8,128)(2,1)} fusion(bf16[256,8192]{1,0:T(8,128)(2,1)} %param.15, f32[768,384]{0,1:T(8,128)S(1)} %fusion.27, f32[256,384]{0,1:T(8,128)S(1)} %copy.16, bf16[256,384]{0,1:T(8,128)(2,1)S(1)} %copy-done.1, f32[256]{0:T(256)S(1)} %copy-done.3), kind=kOutput, calls=%fused_computation.16 | convolution fusion | flops 1614249984 | bytes 11469824 | tf_op jit(solution)/shard_map/dot_general | solution.py:78
  (6 shorter events, 0.1 us)
Async XLA Ops:
  6.5 151.4 %all-gather.2.cloned.1.call-start = ((), (), s32[]{:S(2)}) async-start(), calls=%async_computation | async-start | bytes 25362432 | tf_op jit(solution)/shard_map/all_gather | solution.py:56
  6.5 4.6 %copy-start = (bf16[384,8192]{1,0:T(8,128)(2,1)S(1)}, bf16[384,8192]{1,0:T(8,128)(2,1)}, u32[]{:S(2)}) copy-start(bf16[384,8192]{1,0:T(8,128)(2,1)} %param.8) | copy-start | bytes 18874372
  11.1 10.3 %copy-start.2 = (f32[768,7]{0,1:T(8,128)S(1)}, f32[768,7]{0,1:T(8,128)}, u32[]{:S(2)}) copy-start(f32[768,7]{0,1:T(8,128)} %param.11) | copy-start | bytes 64516
  19.5 9.2 %collective-permute-start = (bf16[768,6]{0,1:T(8,128)(2,1)S(1)}, bf16[768,6]{0,1:T(8,128)(2,1)S(1)}, u32[]{:S(2)}, u32[]{:S(2)}) collective-permute-start(bf16[768,6]{0,1:T(8,128)(2,1)S(1)} %slice.72), channel_id=1, source_target_pairs={{0,1},{1,2},{2,3},{3,4},{4,5},{5,6},{6,7},{7,8},{8,9},{9,10},{10,1... | collective-permute-start | bytes 27656 | tf_op jit(solution)/shard_map/ppermute | solution.py:12
  28.8 2.0 copy-start.4
  28.8 2.0 copy-start.5
  55.3 98.0 %copy-start.1 = (bf16[256,384]{0,1:T(8,128)(2,1)S(1)}, bf16[256,384]{0,1:T(8,128)(2,1)}, u32[]{:S(2)}) copy-start(bf16[256,384]{0,1:T(8,128)(2,1)} %fusion.36) | copy-start | bytes 589828
  190.6 26.4 %copy-start.3 = (f32[256]{0:T(256)S(1)}, f32[256]{0:T(256)}, u32[]{:S(2)}) copy-start(f32[256]{0:T(256)} %param.14) | copy-start | bytes 3076
Sparse Core Ops, SparseCore 0:
  30.7 90.2 all-gather.1
where the time goes:
time: 232 us; the launch traced here: 231 us
  matrix products  144 us (62%)
  local copies, waits for them, and re-layouts  33.5 us (14%)
  other arithmetic  30.8 us (13%)
  between operations  13.6 us (6%)
  waiting for transfers between devices  7.26 us (3%)
    dot_general x1, matrix products, own_block(): toeplitz = jnp.einsum('gm,gmst->gst', weights, decays, precision=HIGHEST)  98 us
    all_gather x1, local copies, waits for them, and re-layouts, on_device(): fragment = lax.all_gather(product, 'tm', axis=1, tiled=True)  32.7 us
    dot_general x1, matrix products, on_device(): jnp.einsum('gcw,gwm->gcm', grouped, factor, precision=HIGHEST, preferred_...  25.6 us
    exp x1, other arithmetic, own_block(): jnp.exp(-rates[:, :, None, None] * jnp.maximum(lag_matrix, 0.0)[None, Non...  24.4 us
    dot_general x1, matrix products, on_device(): lax.dot_general(w_in, normed, (((0,), (1,)), ((), ())), preferred_element...  8.31 us
    ppermute x1, waiting for transfers between devices, shifted(): return lax.ppermute(block, axis, route)  7.22 us
    dot_general x1, matrix products, on_device(): lax.dot_general(gated, w_out, (((0,), (0,)), ((), ())), preferred_element...  6.7 us
  transfers between devices with their start and end apart: 2, of which 1 were waited for; matrix products, arithmetic and copies ran while one was open for 55% of the time, Pallas kernels for 0%

commit v1 on v0

v1 whole, which is shorter than its diff:
```python
import jax
import jax.numpy as jnp
from jax import lax
from jax.experimental import pallas as pl
from jax.experimental.pallas import tpu as pltpu
from jax.sharding import PartitionSpec as P

F32 = jnp.float32
BF16 = jnp.bfloat16
HALO = 8
MIB = 1 << 20


def split(value):
    high = value.astype(BF16)
    return high, (value - high.astype(F32)).astype(BF16)


def dot(left, right):
    return jnp.dot(left, right, preferred_element_type=F32)


def project_kernel(hidden_ref, gain_ref, w_ref, out_ref, total, squares):
    step = pl.program_id(0)
    wide = hidden_ref[...].astype(F32)
    part = dot((wide * gain_ref[...]).astype(BF16), w_ref[...])
    power = jnp.sum((wide * wide).reshape(wide.shape[0], -1, 128), axis=1)

    @pl.when(step == 0)
    def _():
        total[...] = part
        squares[...] = power

    @pl.when(step > 0)
    def _():
        total[...] += part
        squares[...] += power

    @pl.when(step == pl.num_programs(0) - 1)
    def _():
        width = hidden_ref.shape[1] * pl.num_programs(0)
        mean = jnp.sum(squares[...], axis=1, keepdims=True) / width
        out_ref[...] = (total[...] * lax.rsqrt(mean + 1e-06)).astype(BF16)


def project(hidden, gain, w_in, block):
    rows, width = hidden.shape
    columns = w_in.shape[1]
    return pl.pallas_call(
        project_kernel,
        grid=(width // block,),
        in_specs=[
            pl.BlockSpec((rows, block), lambda k: (0, k)),
            pl.BlockSpec((1, block), lambda k: (0, k)),
            pl.BlockSpec((block, columns), lambda k: (k, 0)),
        ],
        out_specs=pl.BlockSpec((rows, columns), lambda k: (0, 0)),
        out_shape=jax.ShapeDtypeStruct((rows, columns), BF16),
        scratch_shapes=[pltpu.VMEM((rows, columns), F32), pltpu.VMEM((rows, 128), F32)],
        compiler_params=pltpu.CompilerParams(vmem_limit_bytes=16 * MIB),
        cost_estimate=pl.CostEstimate(
            flops=2 * rows * width * columns,
            bytes_accessed=2 * width * (rows + columns),
            transcendentals=0,
        ),
        name="project",
    )(hidden, gain, w_in)


def features_kernel(
    halo_ref, gain_ref, w_ref, proj_ref, taps_ref, rcol_ref, query_ref, prod_ref, state_ref, ext
):
    wide = halo_ref[...].astype(F32)
    width = wide.shape[1]
    rows, columns = proj_ref.shape
    chan = columns // 3
    inv = lax.rsqrt(jnp.mean(wide * wide, axis=1, keepdims=True) + 1e-06)
    edge = dot((wide * gain_ref[...]).astype(BF16), w_ref[...]) * inv
    ext[0:HALO, :] = edge.astype(BF16).astype(F32)
    ext[HALO : HALO + rows, :] = proj_ref[...].astype(F32)

    def feature(first):
        cols = slice(first, first + chan)
        total = taps_ref[0:1, cols] * ext[HALO : HALO + rows, cols]
        for k in range(1, taps_ref.shape[0]):
            total = total + taps_ref[k : k + 1, cols] * ext[HALO - k : HALO - k + rows, cols]
        return total

    query_ref[...] = feature(0)
    product = (feature(chan) * feature(2 * chan)).astype(BF16)
    prod_ref[...] = product
    spots = lax.broadcasted_iota(jnp.int32, (1, rows), 1)
    left = (rows - 1 - spots).astype(F32)
    high, low = split(jnp.exp(-rcol_ref[...] * left))
    crossed = dot(high, product) + dot(low, product)
    modes = state_ref.shape[0]
    groups = crossed.shape[0] // modes
    owner = lax.broadcasted_iota(jnp.int32, (modes, chan), 1) // (chan // groups)
    state = jnp.zeros((modes, chan), F32)
    for g in range(groups):
        state = jnp.where(owner == g, crossed[g * modes : (g + 1) * modes, :], state)
    state_ref[...] = state


def local_kernel(prod_ref, skip_ref, rcol_ref, wcol_ref, out_ref):
    rows, chan = prod_ref.shape
    block = 128
    blocks = rows // block
    span = (blocks + 1) * block
    modes = rcol_ref.shape[0] // groups_of(prod_ref)
    groups = groups_of(prod_ref)
    per = chan // groups
    top = (blocks - 1) * block
    spots = lax.broadcasted_iota(jnp.int32, (1, span), 1)
    lags = jnp.where(spots <= top, top - spots, top + span - spots)
    used = (spots <= top) | (spots > blocks * block)
    terms = wcol_ref[...] * jnp.exp(-rcol_ref[...] * lags.astype(F32))
    terms = jnp.where(used, terms, 0.0)
    for g in range(groups):
        filt = jnp.sum(terms[g * modes : (g + 1) * modes, :], axis=0, keepdims=True)
        wide = jnp.broadcast_to(filt, (block, span))
        strip = pltpu.roll(wide, 0, 1, stride=1, stride_axis=0)[:, : blocks * block].astype(BF16)
        cols = slice(g * per, (g + 1) * per)
        mine = prod_ref[:, cols]
        for i in range(blocks):
            near = strip[:, (blocks - 1 - i) * block :]
            conv = dot(near, mine[: (i + 1) * block])
            here = slice(i * block, (i + 1) * block)
            out_ref[here, cols] = conv + skip_ref[:, cols] * mine[here].astype(F32)


def groups_of(prod_ref):
    return prod_ref.shape[1] // 32


def prefix_kernel(chip_ref, all_ref, rate_ref, first_ref, mine_ref, next_ref, *, hop):
    count = all_ref.shape[0]
    fall = jnp.exp(-rate_ref[...] * (2.0 * hop))
    chip = chip_ref[0]

    def step(j, total):
        return jnp.where(j < chip, fall * total + all_ref[j].astype(F32), total)

    total = jnp.zeros(rate_ref.shape, F32)
    total = lax.fori_loop(0, count, step, total, unroll=8)
    mine_ref[...] = total
    next_ref[...] = jnp.exp(-rate_ref[...] * hop) * total + first_ref[...]


def mix_kernel(query_ref, base_ref, state_ref, rrow_ref, wrow_ref, w_ref, out_ref, gated):
    step = pl.program_id(0)

    @pl.when(step == 0)
    def _():
        rows, chan = query_ref.shape
        state = state_ref[...]
        modes = state.shape[0]
        groups = rrow_ref.shape[1] // modes
        owner = lax.broadcasted_iota(jnp.int32, (modes, chan), 1) // (chan // groups)
        spread = jnp.concatenate(
            [jnp.where(owner == g, state, 0.0) for g in range(groups)], axis=0
        )
        times = lax.broadcasted_iota(jnp.int32, (rows, 1), 0).astype(F32) + 1.0
        rising = wrow_ref[...] * jnp.exp(-rrow_ref[...] * times)
        rise_high, rise_low = split(rising)
        high, low = split(spread)
        carry = dot(rise_high, high) + dot(rise_low, high) + dot(rise_high, low)
        gated[...] = (query_ref[...] * (base_ref[...] + carry)).astype(BF16)

    out_ref[...] = dot(gated[...], w_ref[...]).astype(BF16)


def on_device(hidden, norm_gain, w_in, w_short, residues, rates, skip, w_out):
    rows, width = hidden.shape
    chan = w_short.shape[0] // 3
    half = chan // 2
    groups, modes = rates.shape
    devices = lax.axis_size("tm")
    here = lax.axis_index("tm")
    core = here % 2
    edge = lax.ppermute(hidden[rows - HALO :], "tm", [(i, i + 1) for i in range(devices - 1)])
    gain = norm_gain[None, :]
    weights = residues * jnp.sqrt(2.0 * rates)
    rcol, wcol = rates.reshape(-1, 1), weights.reshape(-1, 1)
    rrow, wrow = rates.reshape(1, -1), weights.reshape(1, -1)
    taps = w_short.T
    rate_chan = jnp.repeat(rates.T, chan // groups, axis=1)
    rate_half = lax.dynamic_slice_in_dim(rate_chan, core * half, half, axis=1)

    projected = project(hidden, gain, w_in, 1024)
    query, product, state = pl.pallas_call(
        features_kernel,
        out_shape=[
            jax.ShapeDtypeStruct((rows, chan), F32),
            jax.ShapeDtypeStruct((rows, chan), BF16),
            jax.ShapeDtypeStruct((modes, chan), F32),
        ],
        scratch_shapes=[pltpu.VMEM((rows + HALO, 3 * chan), F32)],
        compiler_params=pltpu.CompilerParams(vmem_limit_bytes=32 * MIB),
        cost_estimate=pl.CostEstimate(
            flops=2 * HALO * width * 3 * chan, bytes_accessed=2 * width * 3 * chan, transcendentals=0
        ),
        name="features",
    )(edge, gain, w_in, projected, taps, rcol)

    base = pl.pallas_call(
        local_kernel,
        out_shape=jax.ShapeDtypeStruct((rows, chan), F32),
        compiler_params=pltpu.CompilerParams(vmem_limit_bytes=16 * MIB),
        cost_estimate=pl.CostEstimate(
            flops=2 * rows * rows * chan, bytes_accessed=6 * rows * chan, transcendentals=0
        ),
        name="local",
    )(product, skip[None, :], rcol, wcol)

    pairs = [(i, i ^ 1) for i in range(devices)]
    own = lax.dynamic_slice_in_dim(state, core * half, half, axis=1)
    other = lax.dynamic_slice_in_dim(state, (1 - core) * half, half, axis=1)
    got = lax.ppermute(other, "tm", pairs)
    first = jnp.where(core == 0, own, got)
    second = jnp.where(core == 0, got, own)
    chip_state = (jnp.exp(-rate_half * rows) * first + second).astype(BF16)
    members = [list(range(c, devices, 2)) for c in range(2)]
    spread = lax.all_to_all(
        jnp.broadcast_to(chip_state, (devices // 2,) + chip_state.shape),
        "tm",
        0,
        0,
        tiled=True,
        axis_index_groups=members,
    )
    mine, following = pl.pallas_call(
        lambda *refs: prefix_kernel(*refs, hop=float(rows)),
        in_specs=[pl.BlockSpec(memory_space=pltpu.SMEM)] + [pl.BlockSpec(memory_space=pltpu.VMEM)] * 3,
        out_shape=[jax.ShapeDtypeStruct((modes, half), F32)] * 2,
        compiler_params=pltpu.CompilerParams(vmem_limit_bytes=8 * MIB),
        name="prefix",
    )((here // 2).astype(jnp.int32)[None], spread, rate_half, first)
    back = lax.ppermute(jnp.where(core == 0, following, mine), "tm", pairs)
    keep = jnp.where(core == 0, mine, following)
    before = jnp.where(
        core == 0,
        jnp.concatenate([keep, back], axis=1),
        jnp.concatenate([back, keep], axis=1),
    )

    block = 1024
    out_width = w_out.shape[1]
    return pl.pallas_call(
        mix_kernel,
        grid=(out_width // block,),
        in_specs=[
            pl.BlockSpec((rows, chan), lambda n: (0, 0)),
            pl.BlockSpec((rows, chan), lambda n: (0, 0)),
            pl.BlockSpec((modes, chan), lambda n: (0, 0)),
            pl.BlockSpec((1, groups * modes), lambda n: (0, 0)),
            pl.BlockSpec((1, groups * modes), lambda n: (0, 0)),
            pl.BlockSpec((chan, block), lambda n: (0, n)),
        ],
        out_specs=pl.BlockSpec((rows, block), lambda n: (0, n)),
        out_shape=jax.ShapeDtypeStruct((rows, out_width), BF16),
        scratch_shapes=[pltpu.VMEM((rows, chan), BF16)],
        compiler_params=pltpu.CompilerParams(vmem_limit_bytes=16 * MIB),
        name="mix",
    )(query, base, before, rrow, wrow, w_out)


def solution(mesh):
    return jax.shard_map(
        on_device,
        mesh=mesh,
        in_specs=(P("tm", None), P(), P(), P(), P(), P(), P(), P()),
        out_specs=P("tm", None),
        check_vma=False,
    )
```

time: 232 us -> 70.7 us (0.30)
  the two profiles are of different devices: /device:TPU:32 before, /device:TPU:1 now
where the time goes in v1:
time: 70.7 us; the launch traced here: 70.3 us
  Pallas kernels  25 us (35%)
  local copies, waits for them, and re-layouts  17.1 us (24%)
  starting transfers between devices  16.9 us (24%)
  waiting for transfers between devices  11.1 us (16%)
    unnamed x20, local copies, waits for them, and re-layouts  14.9 us
    pallas_call x1, Pallas kernels, project(): pl.pallas_call(project_kernel, grid=(width // block,), in_specs=[pl.Block...  12.9 us
    all_to_all x1, starting transfers between devices, on_device(): lax.all_to_all(jnp.broadcast_to(chip_state, (devices // 2,) + chip_state....  10.8 us
    all_to_all x1, waiting for transfers between devices, on_device(): lax.all_to_all(jnp.broadcast_to(chip_state, (devices // 2,) + chip_state....  10.2 us
    pallas_call x1, Pallas kernels, on_device(): pl.pallas_call(mix_kernel, grid=(out_width // block,), in_specs=[pl.Block...  5.91 us
    ppermute x1, starting transfers between devices, on_device(): lax.ppermute(hidden[rows - HALO:], 'tm', [(i, i + 1) for i in range(devic...  4.51 us
    pallas_call x1, Pallas kernels, on_device(): pl.pallas_call(features_kernel, out_shape=[jax.ShapeDtypeStruct((rows, ch...  3.1 us
    pallas_call x1, Pallas kernels, on_device(): pl.pallas_call(local_kernel, out_shape=jax.ShapeDtypeStruct((rows, chan),...  2.85 us
  transfers between devices with their start and end apart: 4, of which 2 were waited for; matrix products, arithmetic and copies ran while one was open for 1% of the time, Pallas kernels for 22%

profile of v1, /device:TPU:1, one launch (start us, length us, event | category | flops | bytes accessed | tf_op | source)
XLA Modules:
  0.0 70.3 jit_solution(324367462140234594)
XLA Ops:
  0.0 0.9 %slice.3 = bf16[8,8192]{1,0:T(8,128)(2,1)S(1)} slice(bf16[384,8192]{1,0:T(8,128)(2,1)} %hidden_ref.1), slice={[376:384], [0:8192]} | slice | bytes 262144 | tf_op jit(solution)/shard_map/slice | solution.py:181
  0.9 4.5 %collective-permute-start = (bf16[8,8192]{1,0:T(8,128)(2,1)S(1)}, bf16[8,8192]{1,0:T(8,128)(2,1)S(1)}, u32[]{:S(2)}, u32[]{:S(2)}) collective-permute-start(bf16[8,8192]{1,0:T(8,128)(2,1)S(1)} %slice.3), channel_id=1, source_target_pairs={{0,1},{1,2},{2,3},{3,4},{4,5},{5,6},{6,7},{7,8},{8,9},{9,10},{10,1... | collective-permute-start | bytes 393224 | tf_op jit(solution)/shard_map/ppermute | solution.py:181
  5.4 0.0 copy-start
  5.4 4.6 %copy-done = bf16[8192,768]{1,0:T(8,128)(2,1)S(1)} copy-done((bf16[8192,768]{1,0:T(8,128)(2,1)S(1)}, bf16[8192,768]{1,0:T(8,128)(2,1)}, u32[]{:S(2)}) %copy-start) | copy-done | bytes 12582936
  10.0 0.0 copy-start.2
  10.0 2.8 %copy-done.2 = bf16[384,8192]{1,0:T(8,128)(2,1)S(1)} copy-done((bf16[384,8192]{1,0:T(8,128)(2,1)S(1)}, bf16[384,8192]{1,0:T(8,128)(2,1)}, u32[]{:S(2)}) %copy-start.2) | copy-done | bytes 6291480
  12.8 0.0 copy-start.4
  12.8 0.8 %copy-done.4 = f32[8192]{0:T(1024)S(1)} copy-done((f32[8192]{0:T(1024)S(1)}, f32[8192]{0:T(1024)}, u32[]{:S(2)}) %copy-start.4) | copy-done | bytes 32792
  13.6 0.0 copy-start.8
  13.6 0.0 copy-start.5
  13.6 0.0 copy-start.6
  13.6 12.9 %project.1.proj_ref = bf16[384,768]{1,0:T(8,128)(2,1)S(1)} custom-call(bf16[384,8192]{1,0:T(8,128)(2,1)S(1)} %copy-done.2, f32[1,8192]{1,0:T(1,128)S(1)} %bitcast.5, bf16[8192,768]{1,0:T(8,128)(2,1)S(1)} %copy-done), custom_call_target="tpu_custom_call" | custom-call | flops 4831838208 | bytes 18874368 | tf_op jit(solution)/shard_map/project/pallas_call | solution.py:49
  26.5 0.0 copy-done.8
  26.5 0.1 reshape.20.rcol_ref
  26.6 0.0 collective-permute-done.halo_ref
  26.6 0.0 copy-done.5
  26.6 0.0 copy-done.6
  26.6 0.0 copy-start.1
  26.6 4.6 %copy-done.1 = bf16[8192,768]{1,0:T(8,128)(2,1)S(1)} copy-done((bf16[8192,768]{1,0:T(8,128)(2,1)S(1)}, bf16[8192,768]{1,0:T(8,128)(2,1)}, u32[]{:S(2)}) %copy-start.1) | copy-done | bytes 12582936
  31.2 0.0 copy-start.9
  31.2 0.0 copy-start.7
  31.2 3.1 %features.1 = (f32[384,256]{1,0:T(8,128)S(1)}, bf16[384,256]{1,0:T(8,128)(2,1)S(1)}, f32[16,256]{1,0:T(8,128)S(1)}) custom-call(bf16[8,8192]{1,0:T(8,128)(2,1)S(1)} %collective-permute-done.halo_ref, f32[1,8192]{1,0:T(1,128)S(1)} %bitcast.6, bf16[8192,768]{1,0:T(8,128)(2,1)S(1)} %copy-done.1, bf16[384,768]{1,0:T(8,128)(2,1)S(1)} %project.1.proj_ref, ...), custom_call_target="tpu_custom_call" | custom-call | flops 100663296 | bytes 12582912 | tf_op jit(solution)/shard_map/features/pallas_call | solution.py:191
  34.3 0.1 collective-permute-start.1
  34.4 0.1 copy.12
  34.5 0.1 broadcast_in_dim.18
  34.6 0.1 reshape.17
  34.7 0.9 %collective-permute-done.1 = f32[16,128]{1,0:T(8,128)S(1)} collective-permute-done((f32[16,128]{1,0:T(8,128)S(1)}, f32[16,128]{1,0:T(8,128)S(1)}, u32[]{:S(2)}, u32[]{:S(2)}) %collective-permute-start.1) | collective-permute-done | bytes 8224 | tf_op jit(solution)/shard_map/ppermute | solution.py:219
  35.6 0.7 %broadcast_in_dim.19 = bf16[64,16,128]{2,1,0:T(8,128)(2,1)} broadcast(bf16[16,128]{1,0:T(8,128)(2,1)S(1)} %get-tuple-element.16), dimensions={1,2} | broadcast | bytes 266240 | tf_op jit(solution)/shard_map/broadcast_in_dim | solution.py:225
  36.4 10.8 %all-to-all-start = ((bf16[64,16,128]{2,1,0:T(8,128)(2,1)}), bf16[64,16,128]{2,1,0:T(8,128)(2,1)S(1)}, u32[]{:S(2)}, u32[]{:S(2)}) async-start(bf16[64,16,128]{2,1,0:T(8,128)(2,1)} %broadcast_in_dim.19), calls=%async_computation | async-start | bytes 524288 | tf_op jit(solution)/shard_map/all_to_all | solution.py:224
  47.2 10.2 %all-to-all-done.refs_1_ = bf16[64,16,128]{2,1,0:T(8,128)(2,1)S(1)} async-done(((bf16[64,16,128]{2,1,0:T(8,128)(2,1)}), bf16[64,16,128]{2,1,0:T(8,128)(2,1)S(1)}, u32[]{:S(2)}, u32[]{:S(2)}) %all-to-all-start) | async-done | bytes 262176 | tf_op jit(solution)/shard_map/all_to_all | solution.py:224
  57.4 0.2 prefix.1
  57.6 1.5 %collective-permute-start.2 = (f32[16,128]{1,0:T(8,128)S(1)}, f32[16,128]{1,0:T(8,128)S(1)}, u32[]{:S(2)}, u32[]{:S(2)}) collective-permute-start(f32[16,128]{1,0:T(8,128)S(1)} %get-tuple-element.19), channel_id=1, source_target_pairs={{0,1},{1,0},{2,3},{3,2},{4,5},{5,4},{6,7},{7,6},{8,9},{9,8},{10,11... | collective-permute-start | bytes 24584 | tf_op jit(solution)/shard_map/ppermute | solution.py:239
  59.0 0.0 copy-done.9
  59.1 0.1 reshape.18.rrow_ref
  59.1 0.1 reshape.19.wrow_ref
  59.2 0.1 reshape.21.wcol_ref
  59.3 0.0 copy-done.7
  59.3 2.9 %local.1.base_ref = f32[384,256]{1,0:T(8,128)S(1)} custom-call(bf16[384,256]{1,0:T(8,128)(2,1)S(1)} %get-tuple-element.11.prod_ref, f32[1,256]{1,0:T(1,128)S(1)} %bitcast.8, f32[128,1]{1,0:T(8,128)S(1)} %reshape.20.rcol_ref, f32[128,1]{1,0:T(8,128)S(1)} %reshape.21.wcol_ref), custom_call_target="tpu_custom_call" | custom-call | flops 75497472 | bytes 589824 | tf_op jit(solution)/shard_map/local/pallas_call | solution.py:206
  62.2 0.0 collective-permute-done.2
  62.2 0.0 copy-start.3
  62.2 2.2 %copy-done.3 = bf16[256,8192]{1,0:T(8,128)(2,1)S(1)} copy-done((bf16[256,8192]{1,0:T(8,128)(2,1)S(1)}, bf16[256,8192]{1,0:T(8,128)(2,1)}, u32[]{:S(2)}) %copy-start.3) | copy-done | bytes 4194328
  64.4 5.9 %mix.1 = bf16[384,8192]{1,0:T(8,128)(2,1)} custom-call(f32[384,256]{1,0:T(8,128)S(1)} %get-tuple-element.10.query_ref, f32[384,256]{1,0:T(8,128)S(1)} %local.1.base_ref, f32[16,256]{1,0:T(8,128)S(1)} %maximum_select_fusion.state_ref, f32[1,128]{1,0:T(1,128)S(1)} %reshape.18.rrow_ref, f32[1,128]{1,0:T(1,128)S(1)} %reshape.19.wrow_ref, ...), custom_call_target="tpu_custom_call" | custom-call | tf_op jit(solution)/shard_map/mix/pallas_call | solution.py:249
  (5 shorter events, 0.0 us)
Async XLA Ops:
  0.9 25.7 %collective-permute-start = (bf16[8,8192]{1,0:T(8,128)(2,1)S(1)}, bf16[8,8192]{1,0:T(8,128)(2,1)S(1)}, u32[]{:S(2)}, u32[]{:S(2)}) collective-permute-start(bf16[8,8192]{1,0:T(8,128)(2,1)S(1)} %slice.3), channel_id=1, source_target_pairs={{0,1},{1,2},{2,3},{3,4},{4,5},{5,6},{6,7},{7,8},{8,9},{9,10},{10,1... | collective-permute-start | bytes 393224 | tf_op jit(solution)/shard_map/ppermute | solution.py:181
  5.4 4.6 %copy-start = (bf16[8192,768]{1,0:T(8,128)(2,1)S(1)}, bf16[8192,768]{1,0:T(8,128)(2,1)}, u32[]{:S(2)}) copy-start(bf16[8192,768]{1,0:T(8,128)(2,1)} %w_ref.4) | copy-start | bytes 37748740
  10.0 2.8 %copy-start.2 = (bf16[384,8192]{1,0:T(8,128)(2,1)S(1)}, bf16[384,8192]{1,0:T(8,128)(2,1)}, u32[]{:S(2)}) copy-start(bf16[384,8192]{1,0:T(8,128)(2,1)} %hidden_ref.1) | copy-start | bytes 18874372
  12.8 0.8 %copy-start.4 = (f32[8192]{0:T(1024)S(1)}, f32[8192]{0:T(1024)}, u32[]{:S(2)}) copy-start(f32[8192]{0:T(1024)} %param.9) | copy-start | bytes 98308
  13.6 12.9 %copy-start.8 = (f32[8,16]{1,0:T(8,128)S(1)}, f32[8,16]{1,0:T(8,128)}, u32[]{:S(2)}) copy-start(f32[8,16]{1,0:T(8,128)} %param.13) | copy-start | bytes 1540
  13.6 13.1 %copy-start.5 = (f32[8192]{0:T(1024)S(1)}, f32[8192]{0:T(1024)}, u32[]{:S(2)}) copy-start(f32[8192]{0:T(1024)} %param.9) | copy-start | bytes 98308
  13.6 13.1 %copy-start.6 = (f32[768,7]{0,1:T(8,128)S(1)}, f32[768,7]{0,1:T(8,128)}, u32[]{:S(2)}) copy-start(f32[768,7]{0,1:T(8,128)} %param.11) | copy-start | bytes 64516
  26.6 4.6 %copy-start.1 = (bf16[8192,768]{1,0:T(8,128)(2,1)S(1)}, bf16[8192,768]{1,0:T(8,128)(2,1)}, u32[]{:S(2)}) copy-start(bf16[8192,768]{1,0:T(8,128)(2,1)} %w_ref.4) | copy-start | bytes 37748740
  31.2 27.8 %copy-start.9 = (f32[8,16]{1,0:T(8,128)S(1)}, f32[8,16]{1,0:T(8,128)}, u32[]{:S(2)}) copy-start(f32[8,16]{1,0:T(8,128)} %param.12) | copy-start | bytes 1540
  31.2 28.1 %copy-start.7 = (f32[256]{0:T(256)S(1)}, f32[256]{0:T(256)}, u32[]{:S(2)}) copy-start(f32[256]{0:T(256)} %param.14) | copy-start | bytes 3076
  34.3 1.3 %collective-permute-start.1 = (f32[16,128]{1,0:T(8,128)S(1)}, f32[16,128]{1,0:T(8,128)S(1)}, u32[]{:S(2)}, u32[]{:S(2)}) collective-permute-start(f32[16,128]{1,0:T(8,128)S(1)} %constant_dynamic-slice_fusion), channel_id=1, source_target_pairs={{0,1},{1,0},{2,3},{3,2},{4,5},{5,4},{6,7},{7,6},{8,9},{9,8},{10,11... | collective-permute-start | bytes 24584 | tf_op jit(solution)/shard_map/ppermute | solution.py:219
  36.4 21.0 %all-to-all-start = ((bf16[64,16,128]{2,1,0:T(8,128)(2,1)}), bf16[64,16,128]{2,1,0:T(8,128)(2,1)S(1)}, u32[]{:S(2)}, u32[]{:S(2)}) async-start(bf16[64,16,128]{2,1,0:T(8,128)(2,1)} %broadcast_in_dim.19), calls=%async_computation | async-start | bytes 524288 | tf_op jit(solution)/shard_map/all_to_all | solution.py:224
  57.6 4.6 %collective-permute-start.2 = (f32[16,128]{1,0:T(8,128)S(1)}, f32[16,128]{1,0:T(8,128)S(1)}, u32[]{:S(2)}, u32[]{:S(2)}) collective-permute-start(f32[16,128]{1,0:T(8,128)S(1)} %get-tuple-element.19), channel_id=1, source_target_pairs={{0,1},{1,0},{2,3},{3,2},{4,5},{5,4},{6,7},{7,6},{8,9},{9,8},{10,11... | collective-permute-start | bytes 24584 | tf_op jit(solution)/shard_map/ppermute | solution.py:239
  62.2 2.2 %copy-start.3 = (bf16[256,8192]{1,0:T(8,128)(2,1)S(1)}, bf16[256,8192]{1,0:T(8,128)(2,1)}, u32[]{:S(2)}) copy-start(bf16[256,8192]{1,0:T(8,128)(2,1)} %w_ref.5) | copy-start | bytes 12582916

commit v2 on v0

v2 whole, which is shorter than its diff:
```python
import functools

import jax
import jax.numpy as jnp
from jax import lax
from jax.experimental import pallas as pl
from jax.experimental.pallas import tpu as pltpu
from jax.sharding import PartitionSpec as P

F32 = jnp.float32
BF16 = jnp.bfloat16
HALO = 8
MIB = 1 << 20


def split(value):
    high = value.astype(BF16)
    return high, (value - high.astype(F32)).astype(BF16)


def dot(left, right):
    return jnp.dot(left, right, preferred_element_type=F32)


def spot(axis, count):
    shape = (1, count) if axis else (count, 1)
    return lax.broadcasted_iota(jnp.int32, shape, axis)


def copies(source, target, axis, count, sems):
    size = source.shape[axis] // count
    made = []
    for k in range(count):
        part = pl.ds(k * size, size)
        index = (part, slice(None)) if axis == 0 else (slice(None), part)
        made.append(pltpu.make_async_copy(source.at[index], target.at[index], sems.at[k]))
    return made


def column(table):
    groups, modes = table.shape
    rows = jnp.concatenate(
        [jnp.broadcast_to(table[g : g + 1, :], (modes, modes)) for g in range(groups)], axis=0
    )
    mine = spot(1, modes) == lax.rem(spot(0, groups * modes), modes)
    return jnp.sum(jnp.where(mine, rows, 0.0), axis=1, keepdims=True)


def fold(stacked, modes, per):
    width = stacked.shape[1]
    owner = spot(1, width) // per
    total = jnp.zeros((modes, width), F32)
    for g in range(stacked.shape[0] // modes):
        total = jnp.where(owner == g, stacked[g * modes : (g + 1) * modes, :], total)
    return total


def by_channel(col, modes, per, width):
    return fold(jnp.broadcast_to(col, (col.shape[0], width)), modes, per)


def feature(taps, ext, rows, first, width, at=0):
    cols = slice(at, at + width)
    wide = slice(first, first + width)
    total = taps[0:1, wide] * ext[HALO : HALO + rows, cols]
    for k in range(1, taps.shape[0]):
        total = total + taps[k : k + 1, wide] * ext[HALO - k : HALO - k + rows, cols]
    return total


def multiply(hidden, inv, gain, near, total, weights, store):
    rows = hidden.shape[0]
    count = len(weights)
    block = near.shape[0] // count
    part = rows // 3
    for k in range(count):
        weights[k].wait()
        cols = slice(k * block, (k + 1) * block)
        for first in range(0, rows, part):
            here = slice(first, first + part)
            scale = jnp.concatenate([inv[here, :]] * (block // 128), axis=1)
            normed = (hidden[here, cols].astype(F32) * scale * gain[:, cols]).astype(BF16)
            made = dot(normed, near[cols, :])
            if k == 0:
                total[here, :] = made
            elif k + 1 < count:
                total[here, :] += made
            else:
                store(here, (total[here, :] + made).astype(BF16))


def state_kernel(
    place_ref, hidden_hbm, gain_hbm, w_hbm, taps_hbm, rates_hbm,
    prod_ref, inv_ref, edge_ref, own_ref, other_ref,
    hidden, near, gain, taps, rates, total, ext, little, sems,
):
    rows, width = hidden.shape
    chan = prod_ref.shape[1]
    reach = taps.shape[0] - 1
    small = [
        pltpu.make_async_copy(source, target, sems.at[2, k])
        for k, (source, target) in enumerate(
            ((gain_hbm, gain), (taps_hbm, taps), (rates_hbm, rates))
        )
    ]
    lines = copies(hidden_hbm, hidden, 1, 4, sems.at[0])
    weights = copies(w_hbm.at[:, pl.ds(chan, 2 * chan)], near, 0, 8, sems.at[1])
    for copy in lines + small:
        copy.start()
    inv_ref[...] = jnp.zeros_like(inv_ref)
    block = width // len(lines)
    for k, copy in enumerate(lines):
        copy.wait()
        weights[2 * k].start()
        weights[2 * k + 1].start()

        def add(i, _, k=k):
            cols = pl.ds(pl.multiple_of(k * block + i * 256, 256), 256)
            wide = hidden[:, cols].astype(F32)
            square = wide * wide
            inv_ref[...] += square[:, :128] + square[:, 128:]
            return 0

        lax.fori_loop(0, block // 256, add, 0)
    inv = lax.rsqrt(jnp.sum(inv_ref[...], axis=1, keepdims=True) / width + 1e-06)
    inv_ref[...] = jnp.broadcast_to(inv, inv_ref.shape)
    for copy in small:
        copy.wait()

    def store(here, value):
        ext[HALO + here.start : HALO + here.stop, :] = value.astype(F32)

    ext[0:HALO, :] = jnp.zeros((HALO, 2 * chan), F32)
    multiply(hidden, inv_ref, gain, near, total, weights, store)

    head_k = feature(taps, ext, rows, chan, chan, 0)
    head_v = feature(taps, ext, rows, 2 * chan, chan, chan)
    later = spot(0, rows) >= reach
    product = jnp.where(later, head_k * head_v, 0.0).astype(BF16)
    prod_ref[...] = product
    edge_ref[0:HALO, :] = ext[HALO : 2 * HALO, :]
    edge_ref[HALO:, :] = ext[rows : rows + HALO, :]
    little[0:HALO, :] = ext[rows : rows + HALO, :]
    little[HALO:, :] = jnp.zeros((HALO, 2 * chan), F32)
    tail_k = feature(taps, little, HALO, chan, chan, 0)
    tail_v = feature(taps, little, HALO, 2 * chan, chan, chan)
    early = spot(0, HALO) < reach
    head_k = jnp.where(early, head_k[0:HALO, :], 0.0)
    head_v = jnp.where(early, head_v[0:HALO, :], 0.0)

    modes = rates.shape[1]
    left = (rows - 1 - spot(1, rows)).astype(F32)
    high, low = split(jnp.exp(-column(rates[...]) * left))
    state = fold(dot(high, product) + dot(low, product), modes, chan // rates.shape[0])
    packed = jnp.concatenate([state, head_k, head_v, tail_k, tail_v], axis=0)
    first, second = packed[:, : chan // 2], packed[:, chan // 2 :]
    zero = place_ref[0] == 0
    own_ref[...] = jnp.where(zero, first, second)
    other_ref[...] = jnp.where(zero, second, first)


def half_column(place_ref, rates_ref):
    col = column(rates_ref[...])
    middle = col.shape[0] // 2
    return jnp.where(place_ref[0] == 0, col[:middle], col[middle:])


def joined(tail_k, head_k, tail_v, head_v):
    return ((tail_k + head_k) * (tail_v + head_v)).astype(BF16).astype(F32)


def chip_kernel(place_ref, own_ref, got_ref, rates_ref, first_ref, spread_ref, *, hop, reach, per):
    zero = place_ref[0] == 0
    own, got = own_ref[...], got_ref[...]
    first = jnp.where(zero, own, got)
    second = jnp.where(zero, got, own)
    modes, width = first_ref.shape
    rate = by_channel(half_column(place_ref, rates_ref), modes, per, width)

    def part(value, k):
        return value[modes + k * HALO : modes + (k + 1) * HALO]

    seam = joined(part(first, 2), part(second, 0), part(first, 3), part(second, 1))
    chip = jnp.exp(-rate * hop) * first[:modes] + second[:modes]
    for s in range(reach):
        chip += jnp.exp(-rate * (hop - 1.0 - s)) * seam[s : s + 1]
    first_ref[...] = first[:modes]
    pieces = [chip] + [part(first, k)[:reach] for k in (0, 1)] + [part(second, k)[:reach] for k in (2, 3)]
    packed = jnp.concatenate(pieces, axis=0).astype(BF16)
    spread_ref[...] = jnp.broadcast_to(packed[None], spread_ref.shape)


def query_kernel(
    after_ref, hidden_hbm, gain_ref, w_hbm, taps_ref, inv_ref, edge_ref,
    query_ref, head_ref, tail_ref, hidden, near, total, ext, sems,
):
    rows, _ = hidden.shape
    chan = query_ref.shape[1]
    lines = copies(hidden_hbm, hidden, 1, 8, sems.at[0])
    weights = copies(w_hbm.at[:, pl.ds(0, chan)], near, 0, 8, sems.at[1])
    for line, weight in zip(lines, weights):
        line.start()
        weight.start()
    for line in lines:
        line.wait()

    def store(here, value):
        ext[HALO + here.start : HALO + here.stop, :] = value.astype(F32)

    ext[0:HALO, :] = jnp.zeros((HALO, chan), F32)
    multiply(hidden, inv_ref, gain_ref, near, total, weights, store)
    query_ref[...] = feature(taps_ref, ext, rows, 0, chan, 0)
    head_ref[:, :chan] = ext[HALO : 2 * HALO, :]
    head_ref[:, chan:] = edge_ref[0:HALO, :]
    tail = jnp.concatenate([ext[rows : rows + HALO, :], edge_ref[HALO:, :]], axis=1)
    tail_ref[...] = tail.astype(BF16)


def local_kernel(
    after_ref, prod_ref, skip_ref, rates_ref, residues_ref, rrow_ref, wrow_ref,
    base_ref, high_ref, low_ref,
):
    rows, chan = prod_ref.shape
    groups, modes = rates_ref.shape
    times = spot(0, rows).astype(F32) + 1.0
    high, low = split(wrow_ref[...] * jnp.exp(-rrow_ref[...] * times))
    high_ref[...] = high
    low_ref[...] = low
    rcol = column(rates_ref[...])
    wcol = column(residues_ref[...]) * jnp.sqrt(2.0 * rcol)
    block = 128
    blocks = rows // block
    span = (blocks + 1) * block
    per = chan // groups
    top = (blocks - 1) * block
    spots = spot(1, span)
    lags = jnp.where(spots <= top, top - spots, top + span - spots)
    used = (spots <= top) | (spots > blocks * block)
    terms = wcol * jnp.exp(-rcol * lags.astype(F32))
    terms = jnp.where(used, terms, 0.0)
    for g in range(groups):
        filt = jnp.sum(terms[g * modes : (g + 1) * modes, :], axis=0, keepdims=True)
        wide = jnp.broadcast_to(filt, (block, span))
        strip = pltpu.roll(wide, 0, 1, stride=1, stride_axis=0)[:, : blocks * block].astype(BF16)
        cols = slice(g * per, (g + 1) * per)
        mine = prod_ref[:, cols]
        for i in range(blocks):
            conv = dot(strip[:, (blocks - 1 - i) * block :], mine[: (i + 1) * block])
            here = slice(i * block, (i + 1) * block)
            base_ref[here, cols] = conv + skip_ref[:, cols] * mine[here].astype(F32)


def prefix_kernel(
    place_ref, all_ref, rates_ref, first_ref, after_ref, keep_ref, send_ref, seams, *, hop, reach, per
):
    count = all_ref.shape[0]
    modes, width = keep_ref.shape
    chip, zero = place_ref[1], place_ref[0] == 0
    col = half_column(place_ref, rates_ref)
    rate = by_channel(col, modes, per, width)
    fall = jnp.exp(-rate * (2.0 * hop))
    wide = all_ref[...].astype(F32)

    def part(k):
        return wide[:, modes + k * reach : modes + (k + 1) * reach, :]

    def before(k):
        value = part(k)
        return jnp.concatenate([jnp.zeros_like(value[:1]), value[:-1]], axis=0)

    seams[...] = jnp.zeros_like(seams)
    seams[:, 0:reach, :] = joined(before(2), part(0), before(3), part(1))
    total = jnp.zeros((modes, width), F32)
    for j in range(count):
        total = jnp.where(j < chip, fall * total + wide[j, :modes, :], total)
    index = spot(1, count * HALO)
    place, step = index // HALO, lax.rem(index, HALO)
    lag = 2.0 * hop * (chip - 1 - place).astype(F32) + (2.0 * hop - 1.0) - step.astype(F32)
    fade = jnp.where(place < chip, jnp.exp(-col * jnp.maximum(lag, 0.0)), 0.0)
    high, low = split(fade)
    products = seams[...].reshape(count * HALO, width).astype(BF16)
    total += fold(dot(high, products) + dot(low, products), modes, per)
    following = jnp.exp(-rate * hop) * total + first_ref[...]
    seam = seams[chip]
    for s in range(reach):
        following += jnp.exp(-rate * (hop - 1.0 - s)) * seam[s : s + 1, :]
    keep_ref[...] = jnp.where(zero, total, following)
    send_ref[...] = jnp.where(zero, following, total)


def mix_kernel(
    place_ref, query_ref, base_ref, keep_ref, back_ref, high_ref, low_ref, head_ref, halo_ref,
    taps_ref, skip_ref, rates_ref, residues_ref, w_hbm,
    out_hbm, w_ref, staged, gated, ext, shift, sums, sems,
):
    steps = sems.shape[1]
    weights = copies(w_hbm, w_ref, 1, steps, sems.at[0])
    for copy in weights:
        copy.start()
    rows, chan = query_ref.shape
    groups, modes = rates_ref.shape
    per = chan // groups
    reach = taps_ref.shape[0] - 1
    ext[0:HALO, :] = halo_ref[...].astype(F32)
    ext[HALO:, :] = head_ref[...]
    query, key, value = [feature(taps_ref, ext, HALO, n * chan, chan, n * chan) for n in range(3)]
    product = jnp.where(spot(0, HALO) < reach, key * value, 0.0).astype(BF16).astype(F32)
    shift[0:HALO, :] = product
    shift[HALO:, :] = jnp.zeros((HALO, chan), F32)
    rcol = column(rates_ref[...])
    wcol = column(residues_ref[...]) * jnp.sqrt(2.0 * rcol)
    rate = by_channel(rcol, modes, per, chan)
    weight = by_channel(wcol, modes, per, chan)

    zero = place_ref[0] == 0
    keep, back = keep_ref[...], back_ref[...]
    state = jnp.concatenate([jnp.where(zero, keep, back), jnp.where(zero, back, keep)], axis=1)
    for s in range(reach):
        state += jnp.exp(rate * (s + 1.0)) * product[s : s + 1, :]
    owner = spot(1, chan) // per
    spread = jnp.concatenate([jnp.where(owner == g, state, 0.0) for g in range(groups)], axis=0)
    high, low = split(spread)
    rise = high_ref[...]
    sums[...] = base_ref[...] + (dot(rise, high) + dot(low_ref[...], high) + dot(rise, low))
    start = sums[0:HALO, :] + skip_ref[...] * product
    for ahead in range(1, reach):
        above = jnp.sum(weight * jnp.exp(rate * float(ahead)), axis=0, keepdims=True)
        start -= above * shift[ahead : ahead + HALO, :]
    sums[...] = query_ref[...] * sums[...]
    sums[0:HALO, :] = query * start
    gated[...] = sums[...].astype(BF16)

    block = w_ref.shape[1] // steps
    sent = copies(staged, out_hbm, 1, steps, sems.at[1])
    for k in range(steps):
        cols = slice(k * block, (k + 1) * block)
        weights[k].wait()
        staged[:, cols] = dot(gated[...], w_ref[:, cols]).astype(BF16)
        sent[k].start()
    for copy in sent:
        copy.wait()


VMEM = pl.BlockSpec(memory_space=pltpu.VMEM)
SMEM = pl.BlockSpec(memory_space=pltpu.SMEM)
ANY = pl.BlockSpec(memory_space=pl.ANY)


def call(kernel, name, specs, outs, scratch=(), limit=40, flops=0, size=0, out_specs=None):
    return pl.pallas_call(
        kernel,
        in_specs=specs,
        out_specs=out_specs or [VMEM] * len(outs),
        out_shape=outs,
        scratch_shapes=list(scratch),
        compiler_params=pltpu.CompilerParams(vmem_limit_bytes=limit * MIB),
        cost_estimate=pl.CostEstimate(flops=flops, bytes_accessed=size, transcendentals=0),
        name=name,
    )


def in_hbm(value):
    return pltpu.with_memory_space_constraint(value, pltpu.HBM)


def on_device(hidden, norm_gain, w_in, w_short, residues, rates, skip, w_out):
    rows, width = hidden.shape
    columns = w_in.shape[1]
    chan = columns // 3
    half = chan // 2
    groups, modes = rates.shape
    per = chan // groups
    reach = w_short.shape[1] - 1
    devices = lax.axis_size("tm")
    here = lax.axis_index("tm")
    place = jnp.stack([here % 2, here // 2]).astype(jnp.int32)
    gain = norm_gain[None, :]
    taps = w_short.T
    skips = skip[None, :]
    vmem, sem = pltpu.VMEM, pltpu.SemaphoreType.DMA

    product, inv, edges, own, other = call(
        state_kernel,
        "state",
        [SMEM] + [ANY] * 5,
        [
            vmem((rows, chan), BF16),
            vmem((rows, 128), F32),
            vmem((2 * HALO, 2 * chan), F32),
            vmem((modes + 4 * HALO, half), F32),
            vmem((modes + 4 * HALO, half), F32),
        ],
        [
            vmem((rows, width), BF16),
            vmem((width, 2 * chan), BF16),
            vmem((1, width), F32),
            vmem((reach + 1, columns), F32),
            vmem((groups, modes), F32),
            vmem((rows, 2 * chan), F32),
            vmem((HALO + rows, 2 * chan), F32),
            vmem((2 * HALO, 2 * chan), F32),
            sem((3, 8)),
        ],
        flops=4 * rows * width * chan,
        size=2 * width * (rows + 2 * chan),
    )(place, in_hbm(hidden), in_hbm(gain), in_hbm(w_in), in_hbm(taps), in_hbm(rates))

    pairs = [(i, i ^ 1) for i in range(devices)]
    got = lax.ppermute(other, "tm", pairs)
    first, spread = call(
        functools.partial(chip_kernel, hop=float(rows), reach=reach, per=per),
        "chip",
        [SMEM] + [VMEM] * 3,
        [
            vmem((modes, half), F32),
            jax.ShapeDtypeStruct((devices // 2, modes + 4 * reach, half), BF16),
        ],
    )(place, own, got, rates)
    members = [list(range(c, devices, 2)) for c in range(2)]
    gathered = lax.all_to_all(spread, "tm", 0, 0, tiled=True, axis_index_groups=members)

    query, head, tail = call(
        query_kernel,
        "query",
        [VMEM, ANY, VMEM, ANY] + [VMEM] * 3,
        [vmem((rows, chan), F32), vmem((HALO, columns), F32), vmem((HALO, columns), BF16)],
        [
            vmem((rows, width), BF16),
            vmem((width, chan), BF16),
            vmem((rows, chan), F32),
            vmem((HALO + rows, chan), F32),
            sem((2, 8)),
        ],
        flops=2 * rows * width * chan,
        size=2 * width * (rows + chan),
    )(first, in_hbm(hidden), gain, in_hbm(w_in), taps, inv, edges)
    halo = lax.ppermute(tail, "tm", [(i, i + 1) for i in range(devices - 1)])

    weights = residues * jnp.sqrt(2.0 * rates)
    base, high, low = call(
        local_kernel,
        "local",
        [VMEM] * 7,
        [
            vmem((rows, chan), F32),
            vmem((rows, groups * modes), BF16),
            vmem((rows, groups * modes), BF16),
        ],
        flops=2 * rows * rows * chan,
        size=6 * rows * chan,
    )(tail, product, skips, rates, residues, rates.reshape(1, -1), weights.reshape(1, -1))

    keep, send = call(
        functools.partial(prefix_kernel, hop=float(rows), reach=reach, per=per),
        "prefix",
        [SMEM] + [VMEM] * 4,
        [vmem((modes, half), F32)] * 2,
        [vmem((devices // 2, HALO, half), F32)],
    )(place, gathered, rates, first, low)
    back = lax.ppermute(send, "tm", pairs)

    return call(
        mix_kernel,
        "mix",
        [SMEM] + [VMEM] * 12 + [ANY],
        jax.ShapeDtypeStruct((rows, w_out.shape[1]), BF16),
        [
            vmem(w_out.shape, BF16),
            vmem((rows, w_out.shape[1]), BF16),
            vmem((rows, chan), BF16),
            vmem((2 * HALO, columns), F32),
            vmem((2 * HALO, chan), F32),
            vmem((rows, chan), F32),
            sem((2, 8)),
        ],
        out_specs=ANY,
    )(
        place, query, base, keep, back, high, low, head, halo, taps, skips, rates, residues,
        in_hbm(w_out),
    )


def solution(mesh):
    return jax.shard_map(
        on_device,
        mesh=mesh,
        in_specs=(P("tm", None), P(), P(), P(), P(), P(), P(), P()),
        out_specs=P("tm", None),
        check_vma=False,
    )
```

time: 232 us -> 49.2 us (0.21)
  the two profiles are of different devices: /device:TPU:32 before, /device:TPU:1 now
where the time goes in v2:
time: 49.2 us; the launch traced here: 49 us
  Pallas kernels  28.5 us (58%)
  starting transfers between devices  18.3 us (37%)
  waiting for transfers between devices  1.68 us (3%)
    all_to_all x1, starting transfers between devices, on_device(): lax.all_to_all(spread, 'tm', 0, 0, tiled=True, axis_index_groups=members)  11.2 us
    pallas_call x1, Pallas kernels, on_device(): call(state_kernel, 'state', [SMEM] + [ANY] * 5, [vmem((rows, chan), BF16)...  10.2 us
    pallas_call x1, Pallas kernels, on_device(): call(query_kernel, 'query', [VMEM, ANY, VMEM, ANY] + [VMEM] * 3, [vmem((r...  7.28 us
    pallas_call x1, Pallas kernels, on_device(): call(mix_kernel, 'mix', [SMEM] + [VMEM] * 12 + [ANY], jax.ShapeDtypeStruc...  5.68 us
    ppermute x1, starting transfers between devices, on_device(): halo = lax.ppermute(tail, 'tm', [(i, i + 1) for i in range(devices - 1)])  3.71 us
    pallas_call x1, Pallas kernels, on_device(): call(local_kernel, 'local', [VMEM] * 7, [vmem((rows, chan), F32), vmem((r...  2.9 us
    ppermute x1, starting transfers between devices, on_device(): back = lax.ppermute(send, 'tm', pairs)  1.83 us
    pallas_call x1, Pallas kernels, on_device(): call(functools.partial(chip_kernel, hop=float(rows), reach=reach, per=per...  1.51 us
  transfers between devices with their start and end apart: 4, of which 2 were waited for; matrix products, arithmetic and copies ran while one was open for 0% of the time, Pallas kernels for 23%

profile of v2, /device:TPU:1, one launch (start us, length us, event | category | flops | bytes accessed | tf_op | source)
XLA Modules:
  0.0 49.0 jit_solution(13231639788677664184)
XLA Ops:
  0.0 0.1 pad_add_fusion.place_ref
  0.1 0.0 copy-start.1
  0.1 0.0 copy-start.3
  0.1 0.0 copy-start
  0.1 0.0 copy-start.2
  0.1 10.2 %state.1 = (bf16[384,256]{1,0:T(8,128)(2,1)S(1)}, f32[384,128]{1,0:T(8,128)S(1)}, f32[16,512]{1,0:T(8,128)S(1)}, f32[48,128]{1,0:T(8,128)S(1)}, f32[48,128]{1,0:T(8,128)S(1)}) custom-call(s32[2]{0:T(128)S(1)} %pad_add_fusion.place_ref, bf16[384,8192]{1,0:T(8,128)(2,1)} %hidden_hbm.3, f32[1,8192]{1,0:T(1,128)} %bitcast.8, bf16[8192,768]{1,0:T(8,128)(2,1)} %w_hbm.4, ...), custom_call_target="tpu_custom_call" | custom-call | flops 3221225472 | bytes 14680064 | tf_op jit(solution)/shard_map/state/pallas_call | solution.py:382
  10.3 1.5 %collective-permute-start = (f32[48,128]{1,0:T(8,128)S(1)}, f32[48,128]{1,0:T(8,128)S(1)}, u32[]{:S(2)}, u32[]{:S(2)}) collective-permute-start(f32[48,128]{1,0:T(8,128)S(1)} %get-tuple-element.21), channel_id=1, source_target_pairs={{0,1},{1,0},{2,3},{3,2},{4,5},{5,4},{6,7},{7,6},{8,9},{9,8},{10,11... | collective-permute-start | bytes 73736 | tf_op jit(solution)/shard_map/ppermute | solution.py:409
  11.8 0.8 %collective-permute-done.got_ref = f32[48,128]{1,0:T(8,128)S(1)} collective-permute-done((f32[48,128]{1,0:T(8,128)S(1)}, f32[48,128]{1,0:T(8,128)S(1)}, u32[]{:S(2)}, u32[]{:S(2)}) %collective-permute-start) | collective-permute-done | bytes 24608 | tf_op jit(solution)/shard_map/ppermute | solution.py:409
  12.6 0.0 copy-done.1
  12.6 1.5 %chip.1 = (f32[16,128]{1,0:T(8,128)S(1)}, bf16[64,40,128]{2,1,0:T(8,128)(2,1)}) custom-call(s32[2]{0:T(128)S(1)} %pad_add_fusion.place_ref, f32[48,128]{1,0:T(8,128)S(1)} %get-tuple-element.20.own_ref, f32[48,128]{1,0:T(8,128)S(1)} %collective-permute-done.got_ref, f32[8,16]{1,0:T(8,128)S(1)} %copy-done.1), custom_call_target="tpu_custom_call" | custom-call | tf_op jit(solution)/shard_map/chip/pallas_call | solution.py:410
  14.2 11.2 %all-to-all-start = ((bf16[64,40,128]{2,1,0:T(8,128)(2,1)}), bf16[64,40,128]{2,1,0:T(8,128)(2,1)S(1)}, u32[]{:S(2)}, u32[]{:S(2)}) async-start(bf16[64,40,128]{2,1,0:T(8,128)(2,1)} %get-tuple-element.29), calls=%async_computation | async-start | bytes 1310720 | tf_op jit(solution)/shard_map/all_to_all | solution.py:420
  25.4 0.1 reshape.6.rrow_ref
  25.5 0.0 copy-done.3
  25.5 0.1 reshape.7.wrow_ref
  25.6 0.0 copy-done
  25.6 0.0 copy-done.2
  25.6 0.0 copy-start.4
  25.6 7.3 %query.1 = (f32[384,256]{1,0:T(8,128)S(1)}, f32[8,768]{1,0:T(8,128)S(1)}, bf16[8,768]{1,0:T(8,128)(2,1)S(1)}) custom-call(f32[16,128]{1,0:T(8,128)S(1)} %get-tuple-element.22.after_ref.first_ref, bf16[384,8192]{1,0:T(8,128)(2,1)} %hidden_hbm.3, f32[1,8192]{1,0:T(1,128)S(1)} %bitcast.9, bf16[8192,768]{1,0:T(8,128)(2,1)} %w_hbm.4, f32[7,768]{1,0:T(8,128)S(1)} %bitcast.6, ...), custom_call_target="tpu_custom_call" | custom-call | flops 1610612736 | bytes 10485760 | tf_op jit(solution)/shard_map/query/pallas_call | solution.py:422
  32.9 3.7 %collective-permute-start.2 = (bf16[8,768]{1,0:T(8,128)(2,1)S(1)}, bf16[8,768]{1,0:T(8,128)(2,1)S(1)}, u32[]{:S(2)}, u32[]{:S(2)}) collective-permute-start(bf16[8,768]{1,0:T(8,128)(2,1)S(1)} %get-tuple-element.26.after_ref), channel_id=1, source_target_pairs={{0,1},{1,2},{2,3},{3,4},{4,5},{5,6},{6,7},{7,8},{8,9},{9,10},{10,1... | collective-permute-start | bytes 36872 | tf_op jit(solution)/shard_map/ppermute | solution.py:437
  36.6 0.0 copy-done.4
  36.6 2.9 %local.1 = (f32[384,256]{1,0:T(8,128)S(1)}, bf16[384,128]{1,0:T(8,128)(2,1)S(1)}, bf16[384,128]{1,0:T(8,128)(2,1)S(1)}) custom-call(bf16[8,768]{1,0:T(8,128)(2,1)S(1)} %get-tuple-element.26.after_ref, bf16[384,256]{1,0:T(8,128)(2,1)S(1)} %get-tuple-element.27.prod_ref, f32[1,256]{1,0:T(1,128)S(1)} %bitcast.10, f32[8,16]{1,0:T(8,128)S(1)} %copy-done.1, ...), custom_call_target="tpu_custom_call" | custom-call | flops 75497472 | bytes 589824 | tf_op jit(solution)/shard_map/local/pallas_call | solution.py:440
  39.5 0.0 all-to-all-done.all_ref
  39.5 1.0 %prefix.1 = (f32[16,128]{1,0:T(8,128)S(1)}, f32[16,128]{1,0:T(8,128)S(1)}) custom-call(s32[2]{0:T(128)S(1)} %pad_add_fusion.place_ref, bf16[64,40,128]{2,1,0:T(8,128)(2,1)S(1)} %all-to-all-done.all_ref, f32[8,16]{1,0:T(8,128)S(1)} %copy-done.1, f32[16,128]{1,0:T(8,128)S(1)} %get-tuple-element.22.after_ref.first_ref, ...), custom_call_target="tpu_custom_call" | custom-call | tf_op jit(solution)/shard_map/prefix/pallas_call | solution.py:453
  40.5 1.8 %collective-permute-start.1 = (f32[16,128]{1,0:T(8,128)S(1)}, f32[16,128]{1,0:T(8,128)S(1)}, u32[]{:S(2)}, u32[]{:S(2)}) collective-permute-start(f32[16,128]{1,0:T(8,128)S(1)} %get-tuple-element.32), channel_id=1, source_target_pairs={{0,1},{1,0},{2,3},{3,2},{4,5},{5,4},{6,7},{7,6},{8,9},{9,8},{10,11... | collective-permute-start | bytes 24584 | tf_op jit(solution)/shard_map/ppermute | solution.py:460
  42.3 0.0 collective-permute-done.2.halo_ref
  42.3 0.8 %collective-permute-done.1.back_ref = f32[16,128]{1,0:T(8,128)S(1)} collective-permute-done((f32[16,128]{1,0:T(8,128)S(1)}, f32[16,128]{1,0:T(8,128)S(1)}, u32[]{:S(2)}, u32[]{:S(2)}) %collective-permute-start.1) | collective-permute-done | bytes 8224 | tf_op jit(solution)/shard_map/ppermute | solution.py:460
  43.1 5.7 %mix.1 = bf16[384,8192]{1,0:T(8,128)(2,1)} custom-call(s32[2]{0:T(128)S(1)} %pad_add_fusion.place_ref, f32[384,256]{1,0:T(8,128)S(1)} %get-tuple-element.25.query_ref, f32[384,256]{1,0:T(8,128)S(1)} %get-tuple-element.28.base_ref, f32[16,128]{1,0:T(8,128)S(1)} %get-tuple-element.31.keep_ref, f32[16,128]{1,0:T(8,128)S(1)} %collective-permute-done.1.back_ref, ...), custom_call_target="tpu_custom_call" | custom-call | tf_op jit(solution)/shard_map/mix/pallas_call | solution.py:462
  (1 shorter events, 0.0 us)
Async XLA Ops:
  0.1 12.6 %copy-start.1 = (f32[8,16]{1,0:T(8,128)S(1)}, f32[8,16]{1,0:T(8,128)}, u32[]{:S(2)}) copy-start(f32[8,16]{1,0:T(8,128)} %rates_ref.7) | copy-start | bytes 1540
  0.1 25.4 %copy-start.3 = (f32[8,16]{1,0:T(8,128)S(1)}, f32[8,16]{1,0:T(8,128)}, u32[]{:S(2)}) copy-start(f32[8,16]{1,0:T(8,128)} %residues_ref.3) | copy-start | bytes 1540
  0.1 25.5 %copy-start = (f32[768,7]{0,1:T(8,128)S(1)}, f32[768,7]{0,1:T(8,128)}, u32[]{:S(2)}) copy-start(f32[768,7]{0,1:T(8,128)} %param.11) | copy-start | bytes 64516
  0.1 25.5 %copy-start.2 = (f32[8192]{0:T(1024)S(1)}, f32[8192]{0:T(1024)}, u32[]{:S(2)}) copy-start(f32[8192]{0:T(1024)} %param.9) | copy-start | bytes 98308
  10.3 2.4 %collective-permute-start = (f32[48,128]{1,0:T(8,128)S(1)}, f32[48,128]{1,0:T(8,128)S(1)}, u32[]{:S(2)}, u32[]{:S(2)}) collective-permute-start(f32[48,128]{1,0:T(8,128)S(1)} %get-tuple-element.21), channel_id=1, source_target_pairs={{0,1},{1,0},{2,3},{3,2},{4,5},{5,4},{6,7},{7,6},{8,9},{9,8},{10,11... | collective-permute-start | bytes 73736 | tf_op jit(solution)/shard_map/ppermute | solution.py:409
  14.2 25.3 %all-to-all-start = ((bf16[64,40,128]{2,1,0:T(8,128)(2,1)}), bf16[64,40,128]{2,1,0:T(8,128)(2,1)S(1)}, u32[]{:S(2)}, u32[]{:S(2)}) async-start(bf16[64,40,128]{2,1,0:T(8,128)(2,1)} %get-tuple-element.29), calls=%async_computation | async-start | bytes 1310720 | tf_op jit(solution)/shard_map/all_to_all | solution.py:420
  25.6 11.0 %copy-start.4 = (f32[256]{0:T(256)S(1)}, f32[256]{0:T(256)}, u32[]{:S(2)}) copy-start(f32[256]{0:T(256)} %param.14) | copy-start | bytes 3076
  32.9 9.4 %collective-permute-start.2 = (bf16[8,768]{1,0:T(8,128)(2,1)S(1)}, bf16[8,768]{1,0:T(8,128)(2,1)S(1)}, u32[]{:S(2)}, u32[]{:S(2)}) collective-permute-start(bf16[8,768]{1,0:T(8,128)(2,1)S(1)} %get-tuple-element.26.after_ref), channel_id=1, source_target_pairs={{0,1},{1,2},{2,3},{3,4},{4,5},{5,6},{6,7},{7,8},{8,9},{9,10},{10,1... | collective-permute-start | bytes 36872 | tf_op jit(solution)/shard_map/ppermute | solution.py:437
  40.5 2.7 %collective-permute-start.1 = (f32[16,128]{1,0:T(8,128)S(1)}, f32[16,128]{1,0:T(8,128)S(1)}, u32[]{:S(2)}, u32[]{:S(2)}) collective-permute-start(f32[16,128]{1,0:T(8,128)S(1)} %get-tuple-element.32), channel_id=1, source_target_pairs={{0,1},{1,0},{2,3},{3,2},{4,5},{5,4},{6,7},{7,6},{8,9},{9,8},{10,11... | collective-permute-start | bytes 24584 | tf_op jit(solution)/shard_map/ppermute | solution.py:460

commit v3 on v2

--- a/solution.py
+++ b/solution.py
@@ -59,34 +59,51 @@
     return fold(jnp.broadcast_to(col, (col.shape[0], width)), modes, per)
 
 
-def feature(taps, ext, rows, first, width, at=0):
+def feature(taps, ext, here, first, width, at=0):
     cols = slice(at, at + width)
     wide = slice(first, first + width)
-    total = taps[0:1, wide] * ext[HALO : HALO + rows, cols]
+    total = taps[0:1, wide] * ext[HALO + here.start : HALO + here.stop, cols]
     for k in range(1, taps.shape[0]):
-        total = total + taps[k : k + 1, wide] * ext[HALO - k : HALO - k + rows, cols]
+        near = ext[HALO + here.start - k : HALO + here.stop - k, cols]
+        total = total + taps[k : k + 1, wide] * near
     return total
 
 
-def multiply(hidden, inv, gain, near, total, weights, store):
+EDGE = slice(0, HALO)
+
+
+def multiply(hidden, inv, gain, near, total, weights, store, lines=(), late=1):
     rows = hidden.shape[0]
     count = len(weights)
     block = near.shape[0] // count
     part = rows // 3
-    for k in range(count):
+    parts = [slice(first, first + part) for first in range(0, rows, part)]
+
+    def made(here, k):
+        cols = slice(k * block, (k + 1) * block)
+        scale = jnp.concatenate([inv[here, :]] * (block // 128), axis=1)
+        normed = (hidden[here, cols].astype(F32) * scale * gain[:, cols]).astype(BF16)
+        return dot(normed, near[cols, :])
+
+    def arrive(k):
+        for copy in lines[k : k + 1]:
+            copy.wait()
         weights[k].wait()
-        cols = slice(k * block, (k + 1) * block)
-        for first in range(0, rows, part):
-            here = slice(first, first + part)
-            scale = jnp.concatenate([inv[here, :]] * (block // 128), axis=1)
-            normed = (hidden[here, cols].astype(F32) * scale * gain[:, cols]).astype(BF16)
-            made = dot(normed, near[cols, :])
+
+    for k in range(count - late):
+        arrive(k)
+        for here in parts:
             if k == 0:
-                total[here, :] = made
-            elif k + 1 < count:
-                total[here, :] += made
+                total[here, :] = made(here, k)
             else:
-                store(here, (total[here, :] + made).astype(BF16))
+                total[here, :] += made(here, k)
+    for here in parts:
+        value = total[here, :]
+        for k in range(count - late, count):
+            if here.start == 0:
+                arrive(k)
+            value += made(here, k)
+        store(here, value.astype(BF16))
 
 
 def state_kernel(
@@ -103,16 +120,21 @@
             ((gain_hbm, gain), (taps_hbm, taps), (rates_hbm, rates))
         )
     ]
-    lines = copies(hidden_hbm, hidden, 1, 4, sems.at[0])
+    lines = copies(hidden_hbm, hidden, 1, 8, sems.at[0])
     weights = copies(w_hbm.at[:, pl.ds(chan, 2 * chan)], near, 0, 8, sems.at[1])
-    for copy in lines + small:
+    for copy in small + lines:
         copy.start()
     inv_ref[...] = jnp.zeros_like(inv_ref)
+    ext[0:HALO, :] = jnp.zeros((HALO, 2 * chan), F32)
+    for copy in small:
+        copy.wait()
+    modes = rates.shape[1]
+    left = (rows - 1 - spot(1, rows)).astype(F32)
+    high, low = split(jnp.exp(-column(rates[...]) * left))
     block = width // len(lines)
     for k, copy in enumerate(lines):
         copy.wait()
-        weights[2 * k].start()
-        weights[2 * k + 1].start()
+        weights[k].start()
 
         def add(i, _, k=k):
             cols = pl.ds(pl.multiple_of(k * block + i * 256, 256), 256)
@@ -124,35 +146,31 @@
         lax.fori_loop(0, block // 256, add, 0)
     inv = lax.rsqrt(jnp.sum(inv_ref[...], axis=1, keepdims=True) / width + 1e-06)
     inv_ref[...] = jnp.broadcast_to(inv, inv_ref.shape)
-    for copy in small:
-        copy.wait()
+    crossed, heads = [], []
 
     def store(here, value):
         ext[HALO + here.start : HALO + here.stop, :] = value.astype(F32)
-
-    ext[0:HALO, :] = jnp.zeros((HALO, 2 * chan), F32)
-    multiply(hidden, inv_ref, gain, near, total, weights, store)
-
-    head_k = feature(taps, ext, rows, chan, chan, 0)
-    head_v = feature(taps, ext, rows, 2 * chan, chan, chan)
-    later = spot(0, rows) >= reach
-    product = jnp.where(later, head_k * head_v, 0.0).astype(BF16)
-    prod_ref[...] = product
+        key = feature(taps, ext, here, chan, chan, 0)
+        value = feature(taps, ext, here, 2 * chan, chan, chan)
+        product = key * value
+        if here.start == 0:
+            early = spot(0, HALO) < reach
+            heads.extend(jnp.where(early, kind[0:HALO, :], 0.0) for kind in (key, value))
+            product = jnp.where(spot(0, here.stop) >= reach, product, 0.0)
+        product = product.astype(BF16)
+        prod_ref[here, :] = product
+        crossed.append(dot(high[:, here], product) + dot(low[:, here], product))
+
+    multiply(hidden, inv_ref, gain, near, total, weights, store, late=4)
+
     edge_ref[0:HALO, :] = ext[HALO : 2 * HALO, :]
     edge_ref[HALO:, :] = ext[rows : rows + HALO, :]
     little[0:HALO, :] = ext[rows : rows + HALO, :]
     little[HALO:, :] = jnp.zeros((HALO, 2 * chan), F32)
-    tail_k = feature(taps, little, HALO, chan, chan, 0)
-    tail_v = feature(taps, little, HALO, 2 * chan, chan, chan)
-    early = spot(0, HALO) < reach
-    head_k = jnp.where(early, head_k[0:HALO, :], 0.0)
-    head_v = jnp.where(early, head_v[0:HALO, :], 0.0)
-
-    modes = rates.shape[1]
-    left = (rows - 1 - spot(1, rows)).astype(F32)
-    high, low = split(jnp.exp(-column(rates[...]) * left))
-    state = fold(dot(high, product) + dot(low, product), modes, chan // rates.shape[0])
-    packed = jnp.concatenate([state, head_k, head_v, tail_k, tail_v], axis=0)
+    tail_k = feature(taps, little, EDGE, chan, chan, 0)
+    tail_v = feature(taps, little, EDGE, 2 * chan, chan, chan)
+    state = fold(sum(crossed[1:], crossed[0]), modes, chan // rates.shape[0])
+    packed = jnp.concatenate([state] + heads + [tail_k, tail_v], axis=0)
     first, second = packed[:, : chan // 2], packed[:, chan // 2 :]
     zero = place_ref[0] == 0
     own_ref[...] = jnp.where(zero, first, second)
@@ -201,15 +219,13 @@
     for line, weight in zip(lines, weights):
         line.start()
         weight.start()
-    for line in lines:
-        line.wait()
 
     def store(here, value):
         ext[HALO + here.start : HALO + here.stop, :] = value.astype(F32)
+        query_ref[here, :] = feature(taps_ref, ext, here, 0, chan, 0)
 
     ext[0:HALO, :] = jnp.zeros((HALO, chan), F32)
-    multiply(hidden, inv_ref, gain_ref, near, total, weights, store)
-    query_ref[...] = feature(taps_ref, ext, rows, 0, chan, 0)
+    multiply(hidden, inv_ref, gain_ref, near, total, weights, store, lines)
     head_ref[:, :chan] = ext[HALO : 2 * HALO, :]
     head_ref[:, chan:] = edge_ref[0:HALO, :]
     tail = jnp.concatenate([ext[rows : rows + HALO, :], edge_ref[HALO:, :]], axis=1)
@@ -217,9 +233,11 @@
 
 
 def local_kernel(
-    after_ref, prod_ref, skip_ref, rates_ref, residues_ref, rrow_ref, wrow_ref,
-    base_ref, high_ref, low_ref,
+    after_ref, prod_ref, skip_ref, rates_ref, residues_ref, rrow_ref, wrow_ref, w_hbm,
+    base_ref, high_ref, low_ref, near_ref, sem,
 ):
+    fetch = pltpu.make_async_copy(w_hbm.at[:, pl.ds(0, near_ref.shape[1])], near_ref, sem)
+    fetch.start()
     rows, chan = prod_ref.shape
     groups, modes = rates_ref.shape
     times = spot(0, rows).astype(F32) + 1.0
@@ -248,6 +266,7 @@
             conv = dot(strip[:, (blocks - 1 - i) * block :], mine[: (i + 1) * block])
             here = slice(i * block, (i + 1) * block)
             base_ref[here, cols] = conv + skip_ref[:, cols] * mine[here].astype(F32)
+    fetch.wait()
 
 
 def prefix_kernel(
@@ -290,11 +309,14 @@
 
 def mix_kernel(
     place_ref, query_ref, base_ref, keep_ref, back_ref, high_ref, low_ref, head_ref, halo_ref,
-    taps_ref, skip_ref, rates_ref, residues_ref, w_hbm,
+    taps_ref, skip_ref, rates_ref, residues_ref, near_ref, w_hbm,
     out_hbm, w_ref, staged, gated, ext, shift, sums, sems,
 ):
     steps = sems.shape[1]
-    weights = copies(w_hbm, w_ref, 1, steps, sems.at[0])
+    kept = near_ref.shape[1]
+    block = out_hbm.shape[1] // steps
+    rest = w_ref.shape[1]
+    weights = copies(w_hbm.at[:, pl.ds(kept, rest)], w_ref, 1, rest // block, sems.at[0])
     for copy in weights:
         copy.start()
     rows, chan = query_ref.shape
@@ -303,7 +325,7 @@
     reach = taps_ref.shape[0] - 1
     ext[0:HALO, :] = halo_ref[...].astype(F32)
     ext[HALO:, :] = head_ref[...]
-    query, key, value = [feature(taps_ref, ext, HALO, n * chan, chan, n * chan) for n in range(3)]
+    query, key, value = [feature(taps_ref, ext, EDGE, n * chan, chan, n * chan) for n in range(3)]
     product = jnp.where(spot(0, HALO) < reach, key * value, 0.0).astype(BF16).astype(F32)
     shift[0:HALO, :] = product
     shift[HALO:, :] = jnp.zeros((HALO, chan), F32)
@@ -330,12 +352,14 @@
     sums[0:HALO, :] = query * start
     gated[...] = sums[...].astype(BF16)
 
-    block = w_ref.shape[1] // steps
     sent = copies(staged, out_hbm, 1, steps, sems.at[1])
     for k in range(steps):
-        cols = slice(k * block, (k + 1) * block)
-        weights[k].wait()
-        staged[:, cols] = dot(gated[...], w_ref[:, cols]).astype(BF16)
+        source, first = near_ref, k * block
+        if first >= kept:
+            source, first = w_ref, first - kept
+            weights[first // block].wait()
+        made = dot(gated[...], source[:, first : first + block])
+        staged[:, k * block : (k + 1) * block] = made.astype(BF16)
         sent[k].start()
     for copy in sent:
         copy.wait()
@@ -437,18 +461,24 @@
     halo = lax.ppermute(tail, "tm", [(i, i + 1) for i in range(devices - 1)])
 
     weights = residues * jnp.sqrt(2.0 * rates)
-    base, high, low = call(
+    kept = w_out.shape[1] * 3 // 8
+    base, high, low, w_near = call(
         local_kernel,
         "local",
-        [VMEM] * 7,
+        [VMEM] * 7 + [ANY],
         [
             vmem((rows, chan), F32),
             vmem((rows, groups * modes), BF16),
             vmem((rows, groups * modes), BF16),
+            vmem((chan, kept), BF16),
         ],
+        [sem],
         flops=2 * rows * rows * chan,
         size=6 * rows * chan,
-    )(tail, product, skips, rates, residues, rates.reshape(1, -1), weights.reshape(1, -1))
+    )(
+        tail, product, skips, rates, residues, rates.reshape(1, -1), weights.reshape(1, -1),
+        in_hbm(w_out),
+    )
 
     keep, send = call(
         functools.partial(prefix_kernel, hop=float(rows), reach=reach, per=per),
@@ -462,10 +492,10 @@
     return call(
         mix_kernel,
         "mix",
-        [SMEM] + [VMEM] * 12 + [ANY],
+        [SMEM] + [VMEM] * 13 + [ANY],
         jax.ShapeDtypeStruct((rows, w_out.shape[1]), BF16),
         [
-            vmem(w_out.shape, BF16),
+            vmem((chan, w_out.shape[1] - kept), BF16),
             vmem((rows, w_out.shape[1]), BF16),
             vmem((rows, chan), BF16),
             vmem((2 * HALO, columns), F32),
@@ -476,7 +506,7 @@
         out_specs=ANY,
     )(
         place, query, base, keep, back, high, low, head, halo, taps, skips, rates, residues,
-        in_hbm(w_out),
+        w_near, in_hbm(w_out),
     )
 
 

time: 49.2 us -> 47.7 us (0.970)
  Pallas kernels: 28.5 us -> 25.7 us
  waiting for transfers between devices: 1.68 us -> 2.7 us
    pallas_call x1, Pallas kernels: 7.28 us -> 4.88 us  [on_device(): call(query_kernel, 'query', [VMEM, ANY, VMEM, ANY] + [VMEM] * 3, [vmem((r...]
    all_to_all x1, waiting for transfers between devices: 0.01 us -> 1.02 us  [on_device(): lax.all_to_all(spread, 'tm', 0, 0, tiled=True, axis_index_groups=members)]
    pallas_call x1, Pallas kernels: 10.2 us -> 9.23 us  [on_device(): call(state_kernel, 'state', [SMEM] + [ANY] * 5, [vmem((rows, chan), BF16)...]
    pallas_call x2, Pallas kernels: 8.58 us -> 9.14 us  [the longest x1 5.28 us: on_device(): call(mix_kernel, 'mix', [SMEM] + [VMEM] * 13 + [ANY], jax.ShapeDtypeStruc...]
  transfers between devices with their start and end apart: 4 -> 4, of which waited for: 2 -> 3; matrix products, arithmetic and copies ran while one was open for 0% -> 0% of each run, Pallas kernels for 23% -> 20%
where the time goes in v3:
time: 47.7 us; the launch traced here: 47.4 us
  Pallas kernels  25.7 us (54%)
  starting transfers between devices  18.5 us (39%)
  waiting for transfers between devices  2.7 us (6%)
    all_to_all x1, starting transfers between devices, on_device(): lax.all_to_all(spread, 'tm', 0, 0, tiled=True, axis_index_groups=members)  11.2 us
    pallas_call x1, Pallas kernels, on_device(): call(state_kernel, 'state', [SMEM] + [ANY] * 5, [vmem((rows, chan), BF16)...  9.23 us
    pallas_call x1, Pallas kernels, on_device(): call(mix_kernel, 'mix', [SMEM] + [VMEM] * 13 + [ANY], jax.ShapeDtypeStruc...  5.28 us
    pallas_call x1, Pallas kernels, on_device(): call(query_kernel, 'query', [VMEM, ANY, VMEM, ANY] + [VMEM] * 3, [vmem((r...  4.88 us
    ppermute x1, starting transfers between devices, on_device(): halo = lax.ppermute(tail, 'tm', [(i, i + 1) for i in range(devices - 1)])  3.89 us
    pallas_call x1, Pallas kernels, on_device(): call(local_kernel, 'local', [VMEM] * 7 + [ANY], [vmem((rows, chan), F32),...  3.86 us
    ppermute x1, starting transfers between devices, on_device(): back = lax.ppermute(send, 'tm', pairs)  1.89 us
    pallas_call x1, Pallas kernels, on_device(): call(functools.partial(chip_kernel, hop=float(rows), reach=reach, per=per...  1.51 us
  transfers between devices with their start and end apart: 4, of which 3 were waited for; matrix products, arithmetic and copies ran while one was open for 0% of the time, Pallas kernels for 20%

profile of v3, /device:TPU:1, one launch (start us, length us, event | category | flops | bytes accessed | tf_op | source)
XLA Modules:
  0.0 47.4 jit_solution(6938157733228290561)
XLA Ops:
  0.0 0.1 pad_add_fusion.place_ref
  0.1 0.0 copy-start.1
  0.1 0.0 copy-start.3
  0.1 0.0 copy-start
  0.1 0.0 copy-start.2
  0.1 9.2 %state.1 = (bf16[384,256]{1,0:T(8,128)(2,1)S(1)}, f32[384,128]{1,0:T(8,128)S(1)}, f32[16,512]{1,0:T(8,128)S(1)}, f32[48,128]{1,0:T(8,128)S(1)}, f32[48,128]{1,0:T(8,128)S(1)}) custom-call(s32[2]{0:T(128)S(1)} %pad_add_fusion.place_ref, bf16[384,8192]{1,0:T(8,128)(2,1)} %hidden_hbm.3, f32[1,8192]{1,0:T(1,128)} %bitcast.8, bf16[8192,768]{1,0:T(8,128)(2,1)} %w_hbm.5, ...), custom_call_target="tpu_custom_call" | custom-call | flops 3221225472 | bytes 14680064 | tf_op jit(solution)/shard_map/state/pallas_call | solution.py:406
  9.3 1.5 %collective-permute-start = (f32[48,128]{1,0:T(8,128)S(1)}, f32[48,128]{1,0:T(8,128)S(1)}, u32[]{:S(2)}, u32[]{:S(2)}) collective-permute-start(f32[48,128]{1,0:T(8,128)S(1)} %get-tuple-element.22), channel_id=1, source_target_pairs={{0,1},{1,0},{2,3},{3,2},{4,5},{5,4},{6,7},{7,6},{8,9},{9,8},{10,11... | collective-permute-start | bytes 73736 | tf_op jit(solution)/shard_map/ppermute | solution.py:433
  10.8 0.8 %collective-permute-done.got_ref = f32[48,128]{1,0:T(8,128)S(1)} collective-permute-done((f32[48,128]{1,0:T(8,128)S(1)}, f32[48,128]{1,0:T(8,128)S(1)}, u32[]{:S(2)}, u32[]{:S(2)}) %collective-permute-start) | collective-permute-done | bytes 24608 | tf_op jit(solution)/shard_map/ppermute | solution.py:433
  11.7 0.0 copy-done.1
  11.7 1.5 %chip.1 = (f32[16,128]{1,0:T(8,128)S(1)}, bf16[64,40,128]{2,1,0:T(8,128)(2,1)}) custom-call(s32[2]{0:T(128)S(1)} %pad_add_fusion.place_ref, f32[48,128]{1,0:T(8,128)S(1)} %get-tuple-element.21.own_ref, f32[48,128]{1,0:T(8,128)S(1)} %collective-permute-done.got_ref, f32[8,16]{1,0:T(8,128)S(1)} %copy-done.1), custom_call_target="tpu_custom_call" | custom-call | tf_op jit(solution)/shard_map/chip/pallas_call | solution.py:434
  13.2 11.2 %all-to-all-start = ((bf16[64,40,128]{2,1,0:T(8,128)(2,1)}), bf16[64,40,128]{2,1,0:T(8,128)(2,1)S(1)}, u32[]{:S(2)}, u32[]{:S(2)}) async-start(bf16[64,40,128]{2,1,0:T(8,128)(2,1)} %get-tuple-element.30), calls=%async_computation | async-start | bytes 1310720 | tf_op jit(solution)/shard_map/all_to_all | solution.py:444
  24.4 0.1 reshape.6.rrow_ref
  24.5 0.0 copy-done.3
  24.5 0.1 reshape.7.wrow_ref
  24.6 0.0 copy-done
  24.6 0.0 copy-done.2
  24.6 0.0 copy-start.4
  24.6 4.9 %query.1 = (f32[384,256]{1,0:T(8,128)S(1)}, f32[8,768]{1,0:T(8,128)S(1)}, bf16[8,768]{1,0:T(8,128)(2,1)S(1)}) custom-call(f32[16,128]{1,0:T(8,128)S(1)} %get-tuple-element.23.after_ref.first_ref, bf16[384,8192]{1,0:T(8,128)(2,1)} %hidden_hbm.3, f32[1,8192]{1,0:T(1,128)S(1)} %bitcast.9, bf16[8192,768]{1,0:T(8,128)(2,1)} %w_hbm.5, f32[7,768]{1,0:T(8,128)S(1)} %bitcast.6, ...), custom_call_target="tpu_custom_call" | custom-call | flops 1610612736 | bytes 10485760 | tf_op jit(solution)/shard_map/query/pallas_call | solution.py:446
  29.5 3.9 %collective-permute-start.2 = (bf16[8,768]{1,0:T(8,128)(2,1)S(1)}, bf16[8,768]{1,0:T(8,128)(2,1)S(1)}, u32[]{:S(2)}, u32[]{:S(2)}) collective-permute-start(bf16[8,768]{1,0:T(8,128)(2,1)S(1)} %get-tuple-element.27.after_ref), channel_id=1, source_target_pairs={{0,1},{1,2},{2,3},{3,4},{4,5},{5,6},{6,7},{7,8},{8,9},{9,10},{10,1... | collective-permute-start | bytes 36872 | tf_op jit(solution)/shard_map/ppermute | solution.py:461
  33.4 0.0 copy-done.4
  33.4 3.9 %local.1 = (f32[384,256]{1,0:T(8,128)S(1)}, bf16[384,128]{1,0:T(8,128)(2,1)S(1)}, bf16[384,128]{1,0:T(8,128)(2,1)S(1)}, bf16[256,3072]{1,0:T(8,128)(2,1)S(1)}) custom-call(bf16[8,768]{1,0:T(8,128)(2,1)S(1)} %get-tuple-element.27.after_ref, bf16[384,256]{1,0:T(8,128)(2,1)S(1)} %get-tuple-element.28.prod_ref, f32[1,256]{1,0:T(1,128)S(1)} %bitcast.10, ...), custom_call_target="tpu_custom_call" | custom-call | flops 75497472 | bytes 589824 | tf_op jit(solution)/shard_map/local/pallas_call | solution.py:465
  37.3 1.0 %all-to-all-done.all_ref = bf16[64,40,128]{2,1,0:T(8,128)(2,1)S(1)} async-done(((bf16[64,40,128]{2,1,0:T(8,128)(2,1)}), bf16[64,40,128]{2,1,0:T(8,128)(2,1)S(1)}, u32[]{:S(2)}, u32[]{:S(2)}) %all-to-all-start) | async-done | bytes 655392 | tf_op jit(solution)/shard_map/all_to_all | solution.py:444
  38.3 1.0 %prefix.1 = (f32[16,128]{1,0:T(8,128)S(1)}, f32[16,128]{1,0:T(8,128)S(1)}) custom-call(s32[2]{0:T(128)S(1)} %pad_add_fusion.place_ref, bf16[64,40,128]{2,1,0:T(8,128)(2,1)S(1)} %all-to-all-done.all_ref, f32[8,16]{1,0:T(8,128)S(1)} %copy-done.1, f32[16,128]{1,0:T(8,128)S(1)} %get-tuple-element.23.after_ref.first_ref, ...), custom_call_target="tpu_custom_call" | custom-call | tf_op jit(solution)/shard_map/prefix/pallas_call | solution.py:483
  39.3 1.9 %collective-permute-start.1 = (f32[16,128]{1,0:T(8,128)S(1)}, f32[16,128]{1,0:T(8,128)S(1)}, u32[]{:S(2)}, u32[]{:S(2)}) collective-permute-start(f32[16,128]{1,0:T(8,128)S(1)} %get-tuple-element.33), channel_id=1, source_target_pairs={{0,1},{1,0},{2,3},{3,2},{4,5},{5,4},{6,7},{7,6},{8,9},{9,8},{10,11... | collective-permute-start | bytes 24584 | tf_op jit(solution)/shard_map/ppermute | solution.py:490
  41.2 0.0 collective-permute-done.2.halo_ref
  41.2 0.8 %collective-permute-done.1.back_ref = f32[16,128]{1,0:T(8,128)S(1)} collective-permute-done((f32[16,128]{1,0:T(8,128)S(1)}, f32[16,128]{1,0:T(8,128)S(1)}, u32[]{:S(2)}, u32[]{:S(2)}) %collective-permute-start.1) | collective-permute-done | bytes 8224 | tf_op jit(solution)/shard_map/ppermute | solution.py:490
  42.0 5.3 %mix.1 = bf16[384,8192]{1,0:T(8,128)(2,1)} custom-call(s32[2]{0:T(128)S(1)} %pad_add_fusion.place_ref, f32[384,256]{1,0:T(8,128)S(1)} %get-tuple-element.26.query_ref, f32[384,256]{1,0:T(8,128)S(1)} %get-tuple-element.29.base_ref, f32[16,128]{1,0:T(8,128)S(1)} %get-tuple-element.32.keep_ref, f32[16,128]{1,0:T(8,128)S(1)} %collective-permute-done.1.back_ref, ...), custom_call_target="tpu_custom_call" | custom-call | tf_op jit(solution)/shard_map/mix/pallas_call | solution.py:492
  (1 shorter events, 0.0 us)
Async XLA Ops:
  0.1 11.6 %copy-start.1 = (f32[8,16]{1,0:T(8,128)S(1)}, f32[8,16]{1,0:T(8,128)}, u32[]{:S(2)}) copy-start(f32[8,16]{1,0:T(8,128)} %rates_ref.7) | copy-start | bytes 1540
  0.1 24.4 %copy-start.3 = (f32[8,16]{1,0:T(8,128)S(1)}, f32[8,16]{1,0:T(8,128)}, u32[]{:S(2)}) copy-start(f32[8,16]{1,0:T(8,128)} %residues_ref.3) | copy-start | bytes 1540
  0.1 24.5 %copy-start = (f32[768,7]{0,1:T(8,128)S(1)}, f32[768,7]{0,1:T(8,128)}, u32[]{:S(2)}) copy-start(f32[768,7]{0,1:T(8,128)} %param.11) | copy-start | bytes 64516
  0.1 24.5 %copy-start.2 = (f32[8192]{0:T(1024)S(1)}, f32[8192]{0:T(1024)}, u32[]{:S(2)}) copy-start(f32[8192]{0:T(1024)} %param.9) | copy-start | bytes 98308
  9.3 2.3 %collective-permute-start = (f32[48,128]{1,0:T(8,128)S(1)}, f32[48,128]{1,0:T(8,128)S(1)}, u32[]{:S(2)}, u32[]{:S(2)}) collective-permute-start(f32[48,128]{1,0:T(8,128)S(1)} %get-tuple-element.22), channel_id=1, source_target_pairs={{0,1},{1,0},{2,3},{3,2},{4,5},{5,4},{6,7},{7,6},{8,9},{9,8},{10,11... | collective-permute-start | bytes 73736 | tf_op jit(solution)/shard_map/ppermute | solution.py:433
  13.2 25.1 %all-to-all-start = ((bf16[64,40,128]{2,1,0:T(8,128)(2,1)}), bf16[64,40,128]{2,1,0:T(8,128)(2,1)S(1)}, u32[]{:S(2)}, u32[]{:S(2)}) async-start(bf16[64,40,128]{2,1,0:T(8,128)(2,1)} %get-tuple-element.30), calls=%async_computation | async-start | bytes 1310720 | tf_op jit(solution)/shard_map/all_to_all | solution.py:444
  24.6 8.8 %copy-start.4 = (f32[256]{0:T(256)S(1)}, f32[256]{0:T(256)}, u32[]{:S(2)}) copy-start(f32[256]{0:T(256)} %param.14) | copy-start | bytes 3076
  29.5 11.7 %collective-permute-start.2 = (bf16[8,768]{1,0:T(8,128)(2,1)S(1)}, bf16[8,768]{1,0:T(8,128)(2,1)S(1)}, u32[]{:S(2)}, u32[]{:S(2)}) collective-permute-start(bf16[8,768]{1,0:T(8,128)(2,1)S(1)} %get-tuple-element.27.after_ref), channel_id=1, source_target_pairs={{0,1},{1,2},{2,3},{3,4},{4,5},{5,6},{6,7},{7,8},{8,9},{9,10},{10,1... | collective-permute-start | bytes 36872 | tf_op jit(solution)/shard_map/ppermute | solution.py:461
  39.3 2.7 %collective-permute-start.1 = (f32[16,128]{1,0:T(8,128)S(1)}, f32[16,128]{1,0:T(8,128)S(1)}, u32[]{:S(2)}, u32[]{:S(2)}) collective-permute-start(f32[16,128]{1,0:T(8,128)S(1)} %get-tuple-element.33), channel_id=1, source_target_pairs={{0,1},{1,0},{2,3},{3,2},{4,5},{5,4},{6,7},{7,6},{8,9},{9,8},{10,11... | collective-permute-start | bytes 24584 | tf_op jit(solution)/shard_map/ppermute | solution.py:490

commit v4 on v3

--- a/solution.py
+++ b/solution.py
@@ -187,23 +187,60 @@
     return ((tail_k + head_k) * (tail_v + head_v)).astype(BF16).astype(F32)
 
 
-def chip_kernel(place_ref, own_ref, got_ref, rates_ref, first_ref, spread_ref, *, hop, reach, per):
+def part(value, modes, k):
+    return value[modes + k * HALO : modes + (k + 1) * HALO]
+
+
+def merge(left, right, rate, length):
+    modes = rate.shape[0]
+    seam = joined(*[part(v, modes, k) for v, k in ((left, 2), (right, 0), (left, 3), (right, 1))])
+    state = jnp.exp(-rate * length) * left[:modes] + right[:modes] + entering(seam, rate, length)
+    return jnp.concatenate(
+        [state, left[modes : modes + 2 * HALO], right[modes + 2 * HALO :]], axis=0
+    )
+
+
+def entering(seam, rate, length):
+    total = jnp.zeros(rate.shape, F32)
+    for s in range(HALO - 2):
+        total += jnp.exp(-rate * (length - 1.0 - s)) * seam[s : s + 1]
+    return total
+
+
+def chip_kernel(place_ref, own_ref, got_ref, rates_ref, first_ref, chip_ref, *, hop, per):
     zero = place_ref[0] == 0
     own, got = own_ref[...], got_ref[...]
     first = jnp.where(zero, own, got)
     second = jnp.where(zero, got, own)
     modes, width = first_ref.shape
     rate = by_channel(half_column(place_ref, rates_ref), modes, per, width)
-
-    def part(value, k):
-        return value[modes + k * HALO : modes + (k + 1) * HALO]
-
-    seam = joined(part(first, 2), part(second, 0), part(first, 3), part(second, 1))
-    chip = jnp.exp(-rate * hop) * first[:modes] + second[:modes]
-    for s in range(reach):
-        chip += jnp.exp(-rate * (hop - 1.0 - s)) * seam[s : s + 1]
     first_ref[...] = first[:modes]
-    pieces = [chip] + [part(first, k)[:reach] for k in (0, 1)] + [part(second, k)[:reach] for k in (2, 3)]
+    chip_ref[...] = merge(first, second, rate, hop)
+
+
+def line_kernel(place_ref, own_ref, *refs, hop, reach, per, along):
+    got_refs, (rates_ref, tail_ref, spread_ref, inner_ref, early_ref, sent_ref) = (
+        refs[: along - 1], refs[along - 1 :]
+    )
+    sent_ref[...] = tail_ref[...]
+    own = own_ref[...]
+    modes = rates_ref.shape[1]
+    rate = by_channel(half_column(place_ref, rates_ref), modes, per, own.shape[1])
+    spot_x = place_ref[1]
+    chips = []
+    for j in range(along):
+        chip = own
+        for m in range(1, along):
+            chip = jnp.where(spot_x == (j ^ m), got_refs[m - 1][...], chip)
+        chips.append(chip)
+    total = chips[0]
+    before = jnp.zeros_like(total)
+    for j in range(1, along):
+        before = jnp.where(spot_x == j, total, before)
+        total = merge(total, chips[j], rate, 2.0 * hop)
+    inner_ref[...] = before
+    early_ref[...] = own[modes : modes + 2 * HALO]
+    pieces = [total[:modes]] + [part(total, modes, k)[:reach] for k in range(4)]
     packed = jnp.concatenate(pieces, axis=0).astype(BF16)
     spread_ref[...] = jnp.broadcast_to(packed[None], spread_ref.shape)
 
@@ -247,62 +284,90 @@
     rcol = column(rates_ref[...])
     wcol = column(residues_ref[...]) * jnp.sqrt(2.0 * rcol)
     block = 128
-    blocks = rows // block
-    span = (blocks + 1) * block
     per = chan // groups
-    top = (blocks - 1) * block
+    places = [slice(first, first + block) for first in range(0, rows, block)]
+    for here in places:
+        base_ref[here, :] = skip_ref[...] * prod_ref[here, :].astype(F32)
+
+    keep = spot(1, chan) // per == spot(0, groups * modes) // modes
+    leave_high, leave_low = split(jnp.exp(-rcol * (block - 1 - spot(1, block)).astype(F32)))
+    fall = jnp.exp(-rcol * float(block))
+    state = jnp.zeros((groups * modes, chan), F32)
+    for here, following in zip(places, places[1:]):
+        mine = prod_ref[here, :]
+        state = fall * state + (dot(leave_high, mine) + dot(leave_low, mine))
+        near_high, near_low = split(jnp.where(keep, state, 0.0))
+        rise = high[:block, :]
+        base_ref[following, :] += (
+            dot(rise, near_high) + dot(low[:block, :], near_high) + dot(rise, near_low)
+        )
+
+    span = 2 * block
     spots = spot(1, span)
-    lags = jnp.where(spots <= top, top - spots, top + span - spots)
-    used = (spots <= top) | (spots > blocks * block)
+    lags = jnp.where(spots == 0, 0, span - spots)
     terms = wcol * jnp.exp(-rcol * lags.astype(F32))
-    terms = jnp.where(used, terms, 0.0)
+    terms = jnp.where((spots == 0) | (spots > block), terms, 0.0)
     for g in range(groups):
         filt = jnp.sum(terms[g * modes : (g + 1) * modes, :], axis=0, keepdims=True)
         wide = jnp.broadcast_to(filt, (block, span))
-        strip = pltpu.roll(wide, 0, 1, stride=1, stride_axis=0)[:, : blocks * block].astype(BF16)
+        square = pltpu.roll(wide, 0, 1, stride=1, stride_axis=0)[:, :block].astype(BF16)
         cols = slice(g * per, (g + 1) * per)
-        mine = prod_ref[:, cols]
-        for i in range(blocks):
-            conv = dot(strip[:, (blocks - 1 - i) * block :], mine[: (i + 1) * block])
-            here = slice(i * block, (i + 1) * block)
-            base_ref[here, cols] = conv + skip_ref[:, cols] * mine[here].astype(F32)
+        for here in places:
+            base_ref[here, cols] += dot(square, prod_ref[here, cols])
     fetch.wait()
 
 
 def prefix_kernel(
-    place_ref, all_ref, rates_ref, first_ref, after_ref, keep_ref, send_ref, seams, *, hop, reach, per
+    place_ref, all_ref, rates_ref, first_ref, inner_ref, early_ref, after_ref,
+    keep_ref, send_ref, seams, tails, *, hop, reach, per, along,
 ):
     count = all_ref.shape[0]
     modes, width = keep_ref.shape
-    chip, zero = place_ref[1], place_ref[0] == 0
+    zero, spot_x, line = place_ref[0] == 0, place_ref[1], place_ref[2]
     col = half_column(place_ref, rates_ref)
     rate = by_channel(col, modes, per, width)
-    fall = jnp.exp(-rate * (2.0 * hop))
+    span = 2.0 * hop * along
+    fall = jnp.exp(-rate * span)
     wide = all_ref[...].astype(F32)
 
-    def part(k):
+    def piece(k):
         return wide[:, modes + k * reach : modes + (k + 1) * reach, :]
 
     def before(k):
-        value = part(k)
+        value = piece(k)
         return jnp.concatenate([jnp.zeros_like(value[:1]), value[:-1]], axis=0)
 
     seams[...] = jnp.zeros_like(seams)
-    seams[:, 0:reach, :] = joined(before(2), part(0), before(3), part(1))
+    tails[...] = jnp.zeros_like(tails)
+    tail_k, tail_v = before(2), before(3)
+    tails[:, 0:reach, :] = tail_k
+    tails[:, HALO : HALO + reach, :] = tail_v
+    seams[:, 0:reach, :] = joined(tail_k, piece(0), tail_v, piece(1))
     total = jnp.zeros((modes, width), F32)
     for j in range(count):
-        total = jnp.where(j < chip, fall * total + wide[j, :modes, :], total)
+        total = jnp.where(j < line, fall * total + wide[j, :modes, :], total)
     index = spot(1, count * HALO)
     place, step = index // HALO, lax.rem(index, HALO)
-    lag = 2.0 * hop * (chip - 1 - place).astype(F32) + (2.0 * hop - 1.0) - step.astype(F32)
-    fade = jnp.where(place < chip, jnp.exp(-col * jnp.maximum(lag, 0.0)), 0.0)
+    lag = span * (line - 1 - place).astype(F32) + (span - 1.0) - step.astype(F32)
+    fade = jnp.where(place < line, jnp.exp(-col * jnp.maximum(lag, 0.0)), 0.0)
     high, low = split(fade)
     products = seams[...].reshape(count * HALO, width).astype(BF16)
     total += fold(dot(high, products) + dot(low, products), modes, per)
-    following = jnp.exp(-rate * hop) * total + first_ref[...]
-    seam = seams[chip]
+
+    inner, early = inner_ref[...], early_ref[...]
+    outer = tails[line]
+    heads = [part(inner, modes, k) for k in (0, 1)]
+    seam = joined(outer[:HALO], heads[0], outer[HALO:], heads[1])
+    length = 2.0 * hop * spot_x.astype(F32)
+    within = jnp.exp(-rate * length) * total + inner[:modes]
     for s in range(reach):
-        following += jnp.exp(-rate * (hop - 1.0 - s)) * seam[s : s + 1, :]
+        within += jnp.exp(-rate * jnp.maximum(length - 1.0 - s, 0.0)) * seam[s : s + 1]
+    starts = spot_x == 0
+    total = jnp.where(starts, total, within)
+    last_k = jnp.where(starts, outer[:HALO], part(inner, modes, 2))
+    last_v = jnp.where(starts, outer[HALO:], part(inner, modes, 3))
+    seam = joined(last_k, early[:HALO], last_v, early[HALO:])
+    following = jnp.exp(-rate * hop) * total + first_ref[...] + entering(seam, rate, hop)
     keep_ref[...] = jnp.where(zero, total, following)
     send_ref[...] = jnp.where(zero, following, total)
 
@@ -397,7 +462,8 @@
     reach = w_short.shape[1] - 1
     devices = lax.axis_size("tm")
     here = lax.axis_index("tm")
-    place = jnp.stack([here % 2, here // 2]).astype(jnp.int32)
+    along = 4
+    place = jnp.stack([here % 2, here // 2 % along, here // (2 * along)]).astype(jnp.int32)
     gain = norm_gain[None, :]
     taps = w_short.T
     skips = skip[None, :]
@@ -431,17 +497,16 @@
 
     pairs = [(i, i ^ 1) for i in range(devices)]
     got = lax.ppermute(other, "tm", pairs)
-    first, spread = call(
-        functools.partial(chip_kernel, hop=float(rows), reach=reach, per=per),
+    first, chip = call(
+        functools.partial(chip_kernel, hop=float(rows), per=per),
         "chip",
         [SMEM] + [VMEM] * 3,
-        [
-            vmem((modes, half), F32),
-            jax.ShapeDtypeStruct((devices // 2, modes + 4 * reach, half), BF16),
-        ],
+        [vmem((modes, half), F32), vmem((modes + 4 * HALO, half), F32)],
     )(place, own, got, rates)
-    members = [list(range(c, devices, 2)) for c in range(2)]
-    gathered = lax.all_to_all(spread, "tm", 0, 0, tiled=True, axis_index_groups=members)
+    lines = [
+        lax.ppermute(chip, "tm", [(i, i ^ (2 * m)) for i in range(devices)])
+        for m in range(1, along)
+    ]
 
     query, head, tail = call(
         query_kernel,
@@ -458,6 +523,19 @@
         flops=2 * rows * width * chan,
         size=2 * width * (rows + chan),
     )(first, in_hbm(hidden), gain, in_hbm(w_in), taps, inv, edges)
+    spread, inner, early, tail = call(
+        functools.partial(line_kernel, hop=float(rows), reach=reach, per=per, along=along),
+        "line",
+        [SMEM] + [VMEM] * (along + 2),
+        [
+            jax.ShapeDtypeStruct((devices // 2 // along, modes + 4 * reach, half), BF16),
+            vmem((modes + 4 * HALO, half), F32),
+            vmem((2 * HALO, half), F32),
+            vmem((HALO, columns), BF16),
+        ],
+    )(place, chip, *lines, rates, tail)
+    members = [list(range(c, devices, 2 * along)) for c in range(2 * along)]
+    gathered = lax.all_to_all(spread, "tm", 0, 0, tiled=True, axis_index_groups=members)
     halo = lax.ppermute(tail, "tm", [(i, i + 1) for i in range(devices - 1)])
 
     weights = residues * jnp.sqrt(2.0 * rates)
@@ -481,12 +559,15 @@
     )
 
     keep, send = call(
-        functools.partial(prefix_kernel, hop=float(rows), reach=reach, per=per),
+        functools.partial(prefix_kernel, hop=float(rows), reach=reach, per=per, along=along),
         "prefix",
-        [SMEM] + [VMEM] * 4,
+        [SMEM] + [VMEM] * 6,
         [vmem((modes, half), F32)] * 2,
-        [vmem((devices // 2, HALO, half), F32)],
-    )(place, gathered, rates, first, low)
+        [
+            vmem((devices // 2 // along, HALO, half), F32),
+            vmem((devices // 2 // along, 2 * HALO, half), F32),
+        ],
+    )(place, gathered, rates, first, inner, early, low)
     back = lax.ppermute(send, "tm", pairs)
 
     return call(

time: 47.7 us -> 47 us (0.985)
  Pallas kernels: 25.7 us -> 24.1 us
  starting transfers between devices: 18.5 us -> 19.9 us
    all_to_all x1, starting transfers between devices: 11.2 us -> 7.84 us  [on_device(): lax.all_to_all(spread, 'tm', 0, 0, tiled=True, axis_index_groups=members)]
    ppermute x0 -> x3, starting transfers between devices: none -> 3.33 us  [on_device(): lax.ppermute(chip, 'tm', [(i, i ^ 2 * m) for i in range(devices)])]
    pallas_call x1, Pallas kernels: 3.86 us -> 1.87 us  [on_device(): call(local_kernel, 'local', [VMEM] * 7 + [ANY], [vmem((rows, chan), F32),...]
    ppermute x1, starting transfers between devices: 1.89 us -> 2.78 us  [on_device(): back = lax.ppermute(send, 'tm', pairs)]
    ppermute x1, starting transfers between devices: 3.89 us -> 4.48 us  [on_device(): halo = lax.ppermute(tail, 'tm', [(i, i + 1) for i in range(devices - 1)])]
    pallas_call x1 -> x2, Pallas kernels: 1.51 us -> 1.99 us  [the longest x1 1.34 us: on_device(): call(functools.partial(line_kernel, hop=float(rows), reach=reach, per=per...]
  transfers between devices with their start and end apart: 4 -> 7, of which waited for: 3 -> 3; matrix products, arithmetic and copies ran while one was open for 0% -> 0% of each run, Pallas kernels for 20% -> 16%
where the time goes in v4:
time: 47 us; the launch traced here: 46.8 us
  Pallas kernels  24.1 us (51%)
  starting transfers between devices  19.9 us (42%)
  waiting for transfers between devices  2.23 us (5%)
    pallas_call x1, Pallas kernels, on_device(): call(state_kernel, 'state', [SMEM] + [ANY] * 5, [vmem((rows, chan), BF16)...  9.24 us
    all_to_all x1, starting transfers between devices, on_device(): lax.all_to_all(spread, 'tm', 0, 0, tiled=True, axis_index_groups=members)  7.84 us
    pallas_call x1, Pallas kernels, on_device(): call(mix_kernel, 'mix', [SMEM] + [VMEM] * 13 + [ANY], jax.ShapeDtypeStruc...  5.28 us
    pallas_call x1, Pallas kernels, on_device(): call(query_kernel, 'query', [VMEM, ANY, VMEM, ANY] + [VMEM] * 3, [vmem((r...  4.9 us
    ppermute x1, starting transfers between devices, on_device(): halo = lax.ppermute(tail, 'tm', [(i, i + 1) for i in range(devices - 1)])  4.48 us
    ppermute x3, starting transfers between devices, on_device(): lax.ppermute(chip, 'tm', [(i, i ^ 2 * m) for i in range(devices)])  3.33 us
    ppermute x1, starting transfers between devices, on_device(): back = lax.ppermute(send, 'tm', pairs)  2.78 us
    pallas_call x1, Pallas kernels, on_device(): call(local_kernel, 'local', [VMEM] * 7 + [ANY], [vmem((rows, chan), F32),...  1.87 us
  transfers between devices with their start and end apart: 7, of which 3 were waited for; matrix products, arithmetic and copies ran while one was open for 0% of the time, Pallas kernels for 16%

profile of v4, /device:TPU:1, one launch (start us, length us, event | category | flops | bytes accessed | tf_op | source)
XLA Modules:
  0.0 46.8 jit_solution(10281125640695912884)
XLA Ops:
  0.0 0.1 pad_add_fusion.place_ref
  0.1 0.0 copy-start
  0.1 0.0 copy-start.1
  0.1 0.0 copy-start.2
  0.1 9.2 %state.1 = (bf16[384,256]{1,0:T(8,128)(2,1)S(1)}, f32[384,128]{1,0:T(8,128)S(1)}, f32[16,512]{1,0:T(8,128)S(1)}, f32[48,128]{1,0:T(8,128)S(1)}, f32[48,128]{1,0:T(8,128)S(1)}) custom-call(s32[3]{0:T(128)S(1)} %pad_add_fusion.place_ref, bf16[384,8192]{1,0:T(8,128)(2,1)} %hidden_hbm.3, f32[1,8192]{1,0:T(1,128)} %bitcast.9, bf16[8192,768]{1,0:T(8,128)(2,1)} %w_hbm.5, ...), custom_call_target="tpu_custom_call" | custom-call | flops 3221225472 | bytes 14680064 | tf_op jit(solution)/shard_map/state/pallas_call | solution.py:472
  9.3 1.5 %collective-permute-start = (f32[48,128]{1,0:T(8,128)S(1)}, f32[48,128]{1,0:T(8,128)S(1)}, u32[]{:S(2)}, u32[]{:S(2)}) collective-permute-start(f32[48,128]{1,0:T(8,128)S(1)} %get-tuple-element.26), channel_id=1, source_target_pairs={{0,1},{1,0},{2,3},{3,2},{4,5},{5,4},{6,7},{7,6},{8,9},{9,8},{10,11... | collective-permute-start | bytes 73736 | tf_op jit(solution)/shard_map/ppermute | solution.py:499
  10.8 0.0 copy-done
  10.8 0.1 reshape.6.rrow_ref
  10.9 0.8 %collective-permute-done.got_ref = f32[48,128]{1,0:T(8,128)S(1)} collective-permute-done((f32[48,128]{1,0:T(8,128)S(1)}, f32[48,128]{1,0:T(8,128)S(1)}, u32[]{:S(2)}, u32[]{:S(2)}) %collective-permute-start) | collective-permute-done | bytes 24608 | tf_op jit(solution)/shard_map/ppermute | solution.py:499
  11.7 0.7 %chip.1 = (f32[16,128]{1,0:T(8,128)S(1)}, f32[48,128]{1,0:T(8,128)S(1)}) custom-call(s32[3]{0:T(128)S(1)} %pad_add_fusion.place_ref, f32[48,128]{1,0:T(8,128)S(1)} %get-tuple-element.25.own_ref, f32[48,128]{1,0:T(8,128)S(1)} %collective-permute-done.got_ref, f32[8,16]{1,0:T(8,128)S(1)} %copy-done), custom_call_target="tpu_custom_call" | custom-call | tf_op jit(solution)/shard_map/chip/pallas_call | solution.py:500
  12.3 2.6 %collective-permute-start.3 = (f32[48,128]{1,0:T(8,128)S(1)}, f32[48,128]{1,0:T(8,128)S(1)}, u32[]{:S(2)}, u32[]{:S(2)}) collective-permute-start(f32[48,128]{1,0:T(8,128)S(1)} %get-tuple-element.31.own_ref), channel_id=1, source_target_pairs={{0,6},{1,7},{2,4},{3,5},{4,2},{5,3},{6,0},{7,1},{8,14},{9,15},{10,... | collective-permute-start | bytes 73736 | tf_op jit(solution)/shard_map/ppermute | solution.py:507
  15.0 0.5 %collective-permute-start.2 = (f32[48,128]{1,0:T(8,128)S(1)}, f32[48,128]{1,0:T(8,128)S(1)}, u32[]{:S(2)}, u32[]{:S(2)}) collective-permute-start(f32[48,128]{1,0:T(8,128)S(1)} %get-tuple-element.31.own_ref), channel_id=1, source_target_pairs={{0,4},{1,5},{2,6},{3,7},{4,0},{5,1},{6,2},{7,3},{8,12},{9,13},{10,... | collective-permute-start | bytes 73736 | tf_op jit(solution)/shard_map/ppermute | solution.py:507
  15.5 0.2 collective-permute-start.1
  15.7 0.0 copy-done.1
  15.7 0.0 copy-done.2
  15.7 0.0 copy-start.3
  15.7 0.0 copy-start.4
  15.7 4.9 %query.1 = (f32[384,256]{1,0:T(8,128)S(1)}, f32[8,768]{1,0:T(8,128)S(1)}, bf16[8,768]{1,0:T(8,128)(2,1)S(1)}) custom-call(f32[16,128]{1,0:T(8,128)S(1)} %get-tuple-element.27.after_ref.first_ref, bf16[384,8192]{1,0:T(8,128)(2,1)} %hidden_hbm.3, f32[1,8192]{1,0:T(1,128)S(1)} %bitcast.10, bf16[8192,768]{1,0:T(8,128)(2,1)} %w_hbm.5, f32[7,768]{1,0:T(8,128)S(1)} %bitcast.7, ...), custom_call_target="tpu_custom_call" | custom-call | flops 1610612736 | bytes 10485760 | tf_op jit(solution)/shard_map/query/pallas_call | solution.py:511
  20.6 0.0 collective-permute-done.3.refs_2_
  20.6 0.0 collective-permute-done.2.refs_1_
  20.6 0.0 collective-permute-done.1.refs_0_
  20.6 1.3 %line.1 = (bf16[16,40,128]{2,1,0:T(8,128)(2,1)}, f32[48,128]{1,0:T(8,128)S(1)}, f32[16,128]{1,0:T(8,128)S(1)}, bf16[8,768]{1,0:T(8,128)(2,1)S(1)}) custom-call(s32[3]{0:T(128)S(1)} %pad_add_fusion.place_ref, f32[48,128]{1,0:T(8,128)S(1)} %get-tuple-element.31.own_ref, f32[48,128]{1,0:T(8,128)S(1)} %collective-permute-done.1.refs_0_, ...), custom_call_target="tpu_custom_call" | custom-call | tf_op jit(solution)/shard_map/line/pallas_call | solution.py:526
  22.0 7.8 %all-to-all-start = ((bf16[16,40,128]{2,1,0:T(8,128)(2,1)}), bf16[16,40,128]{2,1,0:T(8,128)(2,1)S(1)}, u32[]{:S(2)}, u32[]{:S(2)}) async-start(bf16[16,40,128]{2,1,0:T(8,128)(2,1)} %get-tuple-element.36), calls=%async_computation | async-start | bytes 327680 | tf_op jit(solution)/shard_map/all_to_all | solution.py:538
  29.8 0.0 copy-done.3
  29.8 0.1 reshape.7.wrow_ref
  29.9 4.5 %collective-permute-start.5 = (bf16[8,768]{1,0:T(8,128)(2,1)S(1)}, bf16[8,768]{1,0:T(8,128)(2,1)S(1)}, u32[]{:S(2)}, u32[]{:S(2)}) collective-permute-start(bf16[8,768]{1,0:T(8,128)(2,1)S(1)} %get-tuple-element.33.after_ref), channel_id=1, source_target_pairs={{0,1},{1,2},{2,3},{3,4},{4,5},{5,6},{6,7},{7,8},{8,9},{9,10},{10,1... | collective-permute-start | bytes 36872 | tf_op jit(solution)/shard_map/ppermute | solution.py:539
  34.4 0.0 copy-done.4
  34.4 1.9 %local.1 = (f32[384,256]{1,0:T(8,128)S(1)}, bf16[384,128]{1,0:T(8,128)(2,1)S(1)}, bf16[384,128]{1,0:T(8,128)(2,1)S(1)}, bf16[256,3072]{1,0:T(8,128)(2,1)S(1)}) custom-call(bf16[8,768]{1,0:T(8,128)(2,1)S(1)} %get-tuple-element.33.after_ref, bf16[384,256]{1,0:T(8,128)(2,1)S(1)} %get-tuple-element.34.prod_ref, f32[1,256]{1,0:T(1,128)S(1)} %bitcast.11, ...), custom_call_target="tpu_custom_call" | custom-call | flops 75497472 | bytes 589824 | tf_op jit(solution)/shard_map/local/pallas_call | solution.py:543
  36.3 0.6 %all-to-all-done.all_ref = bf16[16,40,128]{2,1,0:T(8,128)(2,1)S(1)} async-done(((bf16[16,40,128]{2,1,0:T(8,128)(2,1)}), bf16[16,40,128]{2,1,0:T(8,128)(2,1)S(1)}, u32[]{:S(2)}, u32[]{:S(2)}) %all-to-all-start) | async-done | bytes 163872 | tf_op jit(solution)/shard_map/all_to_all | solution.py:538
  36.9 0.8 %prefix.1 = (f32[16,128]{1,0:T(8,128)S(1)}, f32[16,128]{1,0:T(8,128)S(1)}) custom-call(s32[3]{0:T(128)S(1)} %pad_add_fusion.place_ref, bf16[16,40,128]{2,1,0:T(8,128)(2,1)S(1)} %all-to-all-done.all_ref, f32[8,16]{1,0:T(8,128)S(1)} %copy-done, f32[16,128]{1,0:T(8,128)S(1)} %get-tuple-element.27.after_ref.first_ref, ...), custom_call_target="tpu_custom_call" | custom-call | tf_op jit(solution)/shard_map/prefix/pallas_call | solution.py:561
  37.7 2.8 %collective-permute-start.4 = (f32[16,128]{1,0:T(8,128)S(1)}, f32[16,128]{1,0:T(8,128)S(1)}, u32[]{:S(2)}, u32[]{:S(2)}) collective-permute-start(f32[16,128]{1,0:T(8,128)S(1)} %get-tuple-element.41), channel_id=1, source_target_pairs={{0,1},{1,0},{2,3},{3,2},{4,5},{5,4},{6,7},{7,6},{8,9},{9,8},{10,11... | collective-permute-start | bytes 24584 | tf_op jit(solution)/shard_map/ppermute | solution.py:571
  40.5 0.0 collective-permute-done.5.halo_ref
  40.5 0.8 %collective-permute-done.4.back_ref = f32[16,128]{1,0:T(8,128)S(1)} collective-permute-done((f32[16,128]{1,0:T(8,128)S(1)}, f32[16,128]{1,0:T(8,128)S(1)}, u32[]{:S(2)}, u32[]{:S(2)}) %collective-permute-start.4) | collective-permute-done | bytes 8224 | tf_op jit(solution)/shard_map/ppermute | solution.py:571
  41.3 5.3 %mix.1 = bf16[384,8192]{1,0:T(8,128)(2,1)} custom-call(s32[3]{0:T(128)S(1)} %pad_add_fusion.place_ref, f32[384,256]{1,0:T(8,128)S(1)} %get-tuple-element.30.query_ref, f32[384,256]{1,0:T(8,128)S(1)} %get-tuple-element.35.base_ref, f32[16,128]{1,0:T(8,128)S(1)} %get-tuple-element.40.keep_ref, f32[16,128]{1,0:T(8,128)S(1)} %collective-permute-done.4.back_ref, ...), custom_call_target="tpu_custom_call" | custom-call | tf_op jit(solution)/shard_map/mix/pallas_call | solution.py:573
  (1 shorter events, 0.0 us)
Async XLA Ops:
  0.1 10.8 %copy-start = (f32[8,16]{1,0:T(8,128)S(1)}, f32[8,16]{1,0:T(8,128)}, u32[]{:S(2)}) copy-start(f32[8,16]{1,0:T(8,128)} %rates_ref.7) | copy-start | bytes 1540
  0.1 15.6 %copy-start.1 = (f32[768,7]{0,1:T(8,128)S(1)}, f32[768,7]{0,1:T(8,128)}, u32[]{:S(2)}) copy-start(f32[768,7]{0,1:T(8,128)} %param.11) | copy-start | bytes 64516
  0.1 15.6 %copy-start.2 = (f32[8192]{0:T(1024)S(1)}, f32[8192]{0:T(1024)}, u32[]{:S(2)}) copy-start(f32[8192]{0:T(1024)} %param.9) | copy-start | bytes 98308
  9.3 2.4 %collective-permute-start = (f32[48,128]{1,0:T(8,128)S(1)}, f32[48,128]{1,0:T(8,128)S(1)}, u32[]{:S(2)}, u32[]{:S(2)}) collective-permute-start(f32[48,128]{1,0:T(8,128)S(1)} %get-tuple-element.26), channel_id=1, source_target_pairs={{0,1},{1,0},{2,3},{3,2},{4,5},{5,4},{6,7},{7,6},{8,9},{9,8},{10,11... | collective-permute-start | bytes 73736 | tf_op jit(solution)/shard_map/ppermute | solution.py:499
  12.3 8.3 %collective-permute-start.3 = (f32[48,128]{1,0:T(8,128)S(1)}, f32[48,128]{1,0:T(8,128)S(1)}, u32[]{:S(2)}, u32[]{:S(2)}) collective-permute-start(f32[48,128]{1,0:T(8,128)S(1)} %get-tuple-element.31.own_ref), channel_id=1, source_target_pairs={{0,6},{1,7},{2,4},{3,5},{4,2},{5,3},{6,0},{7,1},{8,14},{9,15},{10,... | collective-permute-start | bytes 73736 | tf_op jit(solution)/shard_map/ppermute | solution.py:507
  15.0 5.7 %collective-permute-start.2 = (f32[48,128]{1,0:T(8,128)S(1)}, f32[48,128]{1,0:T(8,128)S(1)}, u32[]{:S(2)}, u32[]{:S(2)}) collective-permute-start(f32[48,128]{1,0:T(8,128)S(1)} %get-tuple-element.31.own_ref), channel_id=1, source_target_pairs={{0,4},{1,5},{2,6},{3,7},{4,0},{5,1},{6,2},{7,3},{8,12},{9,13},{10,... | collective-permute-start | bytes 73736 | tf_op jit(solution)/shard_map/ppermute | solution.py:507
  15.5 5.1 %collective-permute-start.1 = (f32[48,128]{1,0:T(8,128)S(1)}, f32[48,128]{1,0:T(8,128)S(1)}, u32[]{:S(2)}, u32[]{:S(2)}) collective-permute-start(f32[48,128]{1,0:T(8,128)S(1)} %get-tuple-element.31.own_ref), channel_id=1, source_target_pairs={{0,2},{1,3},{2,0},{3,1},{4,6},{5,7},{6,4},{7,5},{8,10},{9,11},{10,... | collective-permute-start | bytes 73736 | tf_op jit(solution)/shard_map/ppermute | solution.py:507
  15.7 14.1 %copy-start.3 = (f32[8,16]{1,0:T(8,128)S(1)}, f32[8,16]{1,0:T(8,128)}, u32[]{:S(2)}) copy-start(f32[8,16]{1,0:T(8,128)} %residues_ref.3) | copy-start | bytes 1540
  15.7 18.7 %copy-start.4 = (f32[256]{0:T(256)S(1)}, f32[256]{0:T(256)}, u32[]{:S(2)}) copy-start(f32[256]{0:T(256)} %param.14) | copy-start | bytes 3076
  22.0 15.0 %all-to-all-start = ((bf16[16,40,128]{2,1,0:T(8,128)(2,1)}), bf16[16,40,128]{2,1,0:T(8,128)(2,1)S(1)}, u32[]{:S(2)}, u32[]{:S(2)}) async-start(bf16[16,40,128]{2,1,0:T(8,128)(2,1)} %get-tuple-element.36), calls=%async_computation | async-start | bytes 327680 | tf_op jit(solution)/shard_map/all_to_all | solution.py:538
  29.9 10.6 %collective-permute-start.5 = (bf16[8,768]{1,0:T(8,128)(2,1)S(1)}, bf16[8,768]{1,0:T(8,128)(2,1)S(1)}, u32[]{:S(2)}, u32[]{:S(2)}) collective-permute-start(bf16[8,768]{1,0:T(8,128)(2,1)S(1)} %get-tuple-element.33.after_ref), channel_id=1, source_target_pairs={{0,1},{1,2},{2,3},{3,4},{4,5},{5,6},{6,7},{7,8},{8,9},{9,10},{10,1... | collective-permute-start | bytes 36872 | tf_op jit(solution)/shard_map/ppermute | solution.py:539
  37.7 3.6 %collective-permute-start.4 = (f32[16,128]{1,0:T(8,128)S(1)}, f32[16,128]{1,0:T(8,128)S(1)}, u32[]{:S(2)}, u32[]{:S(2)}) collective-permute-start(f32[16,128]{1,0:T(8,128)S(1)} %get-tuple-element.41), channel_id=1, source_target_pairs={{0,1},{1,0},{2,3},{3,2},{4,5},{5,4},{6,7},{7,6},{8,9},{9,8},{10,11... | collective-permute-start | bytes 24584 | tf_op jit(solution)/shard_map/ppermute | solution.py:571

commit v5 on v4

--- a/solution.py
+++ b/solution.py
@@ -107,8 +107,8 @@
 
 
 def state_kernel(
-    place_ref, hidden_hbm, gain_hbm, w_hbm, taps_hbm, rates_hbm,
-    prod_ref, inv_ref, edge_ref, own_ref, other_ref,
+    hidden_hbm, gain_hbm, w_hbm, taps_hbm, rates_hbm,
+    prod_ref, inv_ref, edge_ref, own_ref,
     hidden, near, gain, taps, rates, total, ext, little, sems,
 ):
     rows, width = hidden.shape
@@ -170,17 +170,7 @@
     tail_k = feature(taps, little, EDGE, chan, chan, 0)
     tail_v = feature(taps, little, EDGE, 2 * chan, chan, chan)
     state = fold(sum(crossed[1:], crossed[0]), modes, chan // rates.shape[0])
-    packed = jnp.concatenate([state] + heads + [tail_k, tail_v], axis=0)
-    first, second = packed[:, : chan // 2], packed[:, chan // 2 :]
-    zero = place_ref[0] == 0
-    own_ref[...] = jnp.where(zero, first, second)
-    other_ref[...] = jnp.where(zero, second, first)
-
-
-def half_column(place_ref, rates_ref):
-    col = column(rates_ref[...])
-    middle = col.shape[0] // 2
-    return jnp.where(place_ref[0] == 0, col[:middle], col[middle:])
+    own_ref[...] = jnp.concatenate([state] + heads + [tail_k, tail_v], axis=0)
 
 
 def joined(tail_k, head_k, tail_v, head_v):
@@ -208,12 +198,12 @@
 
 
 def chip_kernel(place_ref, own_ref, got_ref, rates_ref, first_ref, chip_ref, *, hop, per):
-    zero = place_ref[0] == 0
+    zero = place_ref[0:1, :] == 0
     own, got = own_ref[...], got_ref[...]
     first = jnp.where(zero, own, got)
     second = jnp.where(zero, got, own)
     modes, width = first_ref.shape
-    rate = by_channel(half_column(place_ref, rates_ref), modes, per, width)
+    rate = by_channel(column(rates_ref[...]), modes, per, width)
     first_ref[...] = first[:modes]
     chip_ref[...] = merge(first, second, rate, hop)
 
@@ -225,8 +215,8 @@
     sent_ref[...] = tail_ref[...]
     own = own_ref[...]
     modes = rates_ref.shape[1]
-    rate = by_channel(half_column(place_ref, rates_ref), modes, per, own.shape[1])
-    spot_x = place_ref[1]
+    rate = by_channel(column(rates_ref[...]), modes, per, own.shape[1])
+    spot_x = place_ref[1:2, :]
     chips = []
     for j in range(along):
         chip = own
@@ -319,12 +309,12 @@
 
 def prefix_kernel(
     place_ref, all_ref, rates_ref, first_ref, inner_ref, early_ref, after_ref,
-    keep_ref, send_ref, seams, tails, *, hop, reach, per, along,
+    state_ref, seams, tails, *, hop, reach, per, along,
 ):
     count = all_ref.shape[0]
-    modes, width = keep_ref.shape
-    zero, spot_x, line = place_ref[0] == 0, place_ref[1], place_ref[2]
-    col = half_column(place_ref, rates_ref)
+    modes, width = state_ref.shape
+    zero, spot_x, line = place_ref[0:1, :] == 0, place_ref[1:2, :], place_ref[2:3, :]
+    col = column(rates_ref[...])
     rate = by_channel(col, modes, per, width)
     span = 2.0 * hop * along
     fall = jnp.exp(-rate * span)
@@ -348,14 +338,17 @@
         total = jnp.where(j < line, fall * total + wide[j, :modes, :], total)
     index = spot(1, count * HALO)
     place, step = index // HALO, lax.rem(index, HALO)
-    lag = span * (line - 1 - place).astype(F32) + (span - 1.0) - step.astype(F32)
-    fade = jnp.where(place < line, jnp.exp(-col * jnp.maximum(lag, 0.0)), 0.0)
+    level = line[:, : count * HALO]
+    lag = span * (level - 1 - place).astype(F32) + (span - 1.0) - step.astype(F32)
+    fade = jnp.where(place < level, jnp.exp(-col * jnp.maximum(lag, 0.0)), 0.0)
     high, low = split(fade)
     products = seams[...].reshape(count * HALO, width).astype(BF16)
     total += fold(dot(high, products) + dot(low, products), modes, per)
 
     inner, early = inner_ref[...], early_ref[...]
-    outer = tails[line]
+    outer = tails[0]
+    for j in range(1, count):
+        outer = jnp.where(line == j, tails[j], outer)
     heads = [part(inner, modes, k) for k in (0, 1)]
     seam = joined(outer[:HALO], heads[0], outer[HALO:], heads[1])
     length = 2.0 * hop * spot_x.astype(F32)
@@ -368,12 +361,11 @@
     last_v = jnp.where(starts, outer[HALO:], part(inner, modes, 3))
     seam = joined(last_k, early[:HALO], last_v, early[HALO:])
     following = jnp.exp(-rate * hop) * total + first_ref[...] + entering(seam, rate, hop)
-    keep_ref[...] = jnp.where(zero, total, following)
-    send_ref[...] = jnp.where(zero, following, total)
+    state_ref[...] = jnp.where(zero, total, following)
 
 
 def mix_kernel(
-    place_ref, query_ref, base_ref, keep_ref, back_ref, high_ref, low_ref, head_ref, halo_ref,
+    query_ref, base_ref, state_ref, high_ref, low_ref, head_ref, halo_ref,
     taps_ref, skip_ref, rates_ref, residues_ref, near_ref, w_hbm,
     out_hbm, w_ref, staged, gated, ext, shift, sums, sems,
 ):
@@ -399,9 +391,7 @@
     rate = by_channel(rcol, modes, per, chan)
     weight = by_channel(wcol, modes, per, chan)
 
-    zero = place_ref[0] == 0
-    keep, back = keep_ref[...], back_ref[...]
-    state = jnp.concatenate([jnp.where(zero, keep, back), jnp.where(zero, back, keep)], axis=1)
+    state = state_ref[...]
     for s in range(reach):
         state += jnp.exp(rate * (s + 1.0)) * product[s : s + 1, :]
     owner = spot(1, chan) // per
@@ -431,7 +421,6 @@
 
 
 VMEM = pl.BlockSpec(memory_space=pltpu.VMEM)
-SMEM = pl.BlockSpec(memory_space=pltpu.SMEM)
 ANY = pl.BlockSpec(memory_space=pl.ANY)
 
 
@@ -456,7 +445,6 @@
     rows, width = hidden.shape
     columns = w_in.shape[1]
     chan = columns // 3
-    half = chan // 2
     groups, modes = rates.shape
     per = chan // groups
     reach = w_short.shape[1] - 1
@@ -464,21 +452,21 @@
     here = lax.axis_index("tm")
     along = 4
     place = jnp.stack([here % 2, here // 2 % along, here // (2 * along)]).astype(jnp.int32)
+    place = jnp.broadcast_to(place[:, None], (3, chan))
     gain = norm_gain[None, :]
     taps = w_short.T
     skips = skip[None, :]
     vmem, sem = pltpu.VMEM, pltpu.SemaphoreType.DMA
 
-    product, inv, edges, own, other = call(
+    product, inv, edges, own = call(
         state_kernel,
         "state",
-        [SMEM] + [ANY] * 5,
+        [ANY] * 5,
         [
             vmem((rows, chan), BF16),
             vmem((rows, 128), F32),
             vmem((2 * HALO, 2 * chan), F32),
-            vmem((modes + 4 * HALO, half), F32),
-            vmem((modes + 4 * HALO, half), F32),
+            vmem((modes + 4 * HALO, chan), F32),
         ],
         [
             vmem((rows, width), BF16),
@@ -493,15 +481,15 @@
         ],
         flops=4 * rows * width * chan,
         size=2 * width * (rows + 2 * chan),
-    )(place, in_hbm(hidden), in_hbm(gain), in_hbm(w_in), in_hbm(taps), in_hbm(rates))
+    )(in_hbm(hidden), in_hbm(gain), in_hbm(w_in), in_hbm(taps), in_hbm(rates))
 
     pairs = [(i, i ^ 1) for i in range(devices)]
-    got = lax.ppermute(other, "tm", pairs)
+    got = lax.ppermute(own, "tm", pairs)
     first, chip = call(
         functools.partial(chip_kernel, hop=float(rows), per=per),
         "chip",
-        [SMEM] + [VMEM] * 3,
-        [vmem((modes, half), F32), vmem((modes + 4 * HALO, half), F32)],
+        [VMEM] + [VMEM] * 3,
+        [vmem((modes, chan), F32), vmem((modes + 4 * HALO, chan), F32)],
     )(place, own, got, rates)
     lines = [
         lax.ppermute(chip, "tm", [(i, i ^ (2 * m)) for i in range(devices)])
@@ -526,11 +514,11 @@
     spread, inner, early, tail = call(
         functools.partial(line_kernel, hop=float(rows), reach=reach, per=per, along=along),
         "line",
-        [SMEM] + [VMEM] * (along + 2),
-        [
-            jax.ShapeDtypeStruct((devices // 2 // along, modes + 4 * reach, half), BF16),
-            vmem((modes + 4 * HALO, half), F32),
-            vmem((2 * HALO, half), F32),
+        [VMEM] + [VMEM] * (along + 2),
+        [
+            jax.ShapeDtypeStruct((devices // 2 // along, modes + 4 * reach, chan), BF16),
+            vmem((modes + 4 * HALO, chan), F32),
+            vmem((2 * HALO, chan), F32),
             vmem((HALO, columns), BF16),
         ],
     )(place, chip, *lines, rates, tail)
@@ -558,22 +546,21 @@
         in_hbm(w_out),
     )
 
-    keep, send = call(
+    state, = call(
         functools.partial(prefix_kernel, hop=float(rows), reach=reach, per=per, along=along),
         "prefix",
-        [SMEM] + [VMEM] * 6,
-        [vmem((modes, half), F32)] * 2,
-        [
-            vmem((devices // 2 // along, HALO, half), F32),
-            vmem((devices // 2 // along, 2 * HALO, half), F32),
+        [VMEM] + [VMEM] * 6,
+        [vmem((modes, chan), F32)],
+        [
+            vmem((devices // 2 // along, HALO, chan), F32),
+            vmem((devices // 2 // along, 2 * HALO, chan), F32),
         ],
     )(place, gathered, rates, first, inner, early, low)
-    back = lax.ppermute(send, "tm", pairs)
 
     return call(
         mix_kernel,
         "mix",
-        [SMEM] + [VMEM] * 13 + [ANY],
+        [VMEM] * 12 + [ANY],
         jax.ShapeDtypeStruct((rows, w_out.shape[1]), BF16),
         [
             vmem((chan, w_out.shape[1] - kept), BF16),
@@ -586,7 +573,7 @@
         ],
         out_specs=ANY,
     )(
-        place, query, base, keep, back, high, low, head, halo, taps, skips, rates, residues,
+        query, base, state, high, low, head, halo, taps, skips, rates, residues,
         w_near, in_hbm(w_out),
     )
 

time: 47 us -> 42.9 us (0.913)
  the two profiles are of different devices: /device:TPU:1 before, /device:TPU:0 now
where the time goes in v5:
time: 42.9 us; the launch traced here: 42.7 us
  Pallas kernels  21.5 us (50%)
  starting transfers between devices  13.9 us (32%)
  waiting for transfers between devices  6.6 us (15%)
    pallas_call x1, Pallas kernels, on_device(): call(state_kernel, 'state', [ANY] * 5, [vmem((rows, chan), BF16), vmem((r...  8.7 us
    all_to_all x1, starting transfers between devices, on_device(): lax.all_to_all(spread, 'tm', 0, 0, tiled=True, axis_index_groups=members)  8.15 us
    all_to_all x1, waiting for transfers between devices, on_device(): lax.all_to_all(spread, 'tm', 0, 0, tiled=True, axis_index_groups=members)  5.49 us
    pallas_call x1, Pallas kernels, on_device(): call(query_kernel, 'query', [VMEM, ANY, VMEM, ANY] + [VMEM] * 3, [vmem((r...  4.9 us
    pallas_call x1, Pallas kernels, on_device(): call(mix_kernel, 'mix', [VMEM] * 12 + [ANY], jax.ShapeDtypeStruct((rows,...  4.75 us
    ppermute x3, starting transfers between devices, on_device(): lax.ppermute(chip, 'tm', [(i, i ^ 2 * m) for i in range(devices)])  4.17 us
    pallas_call x1, Pallas kernels, on_device(): call(local_kernel, 'local', [VMEM] * 7 + [ANY], [vmem((rows, chan), F32),...  1.88 us
    ppermute x1, starting transfers between devices, on_device(): halo = lax.ppermute(tail, 'tm', [(i, i + 1) for i in range(devices - 1)])  1.47 us
  transfers between devices with their start and end apart: 6, of which 2 were waited for; matrix products, arithmetic and copies ran while one was open for 1% of the time, Pallas kernels for 17%

profile of v5, /device:TPU:0, one launch (start us, length us, event | category | flops | bytes accessed | tf_op | source)
XLA Modules:
  0.0 42.7 jit_solution(16551266899822327185)
XLA Ops:
  0.0 0.0 copy-start
  0.0 0.0 copy-start.1
  0.0 0.0 copy-start.2
  0.0 8.7 %state.1 = (bf16[384,256]{1,0:T(8,128)(2,1)S(1)}, f32[384,128]{1,0:T(8,128)S(1)}, f32[16,512]{1,0:T(8,128)S(1)}, f32[48,256]{1,0:T(8,128)S(1)}) custom-call(bf16[384,8192]{1,0:T(8,128)(2,1)} %hidden_hbm.3, f32[1,8192]{1,0:T(1,128)} %bitcast.9, bf16[8192,768]{1,0:T(8,128)(2,1)} %w_hbm.5, f32[7,768]{1,0:T(8,128)} %bitcast.6, f32[8,16]{1,0:T(8,128)} %rates_ref.7), custom_call_target="tpu_custom_call" | custom-call | flops 3221225472 | bytes 14680064 | tf_op jit(solution)/shard_map/state/pallas_call | solution.py:461
  8.7 0.1 collective-permute-start
  8.9 0.1 pad_add_fusion
  8.9 1.1 %collective-permute-done.got_ref = f32[48,256]{1,0:T(8,128)S(1)} collective-permute-done((f32[48,256]{1,0:T(8,128)S(1)}, f32[48,256]{1,0:T(8,128)S(1)}, u32[]{:S(2)}, u32[]{:S(2)}) %collective-permute-start) | collective-permute-done | bytes 49184 | tf_op jit(solution)/shard_map/ppermute | solution.py:487
  10.0 0.1 broadcast_in_dim.12.place_ref
  10.1 0.0 copy-done
  10.1 0.1 chip.1
  10.2 2.9 %collective-permute-start.3 = (f32[48,256]{1,0:T(8,128)S(1)}, f32[48,256]{1,0:T(8,128)S(1)}, u32[]{:S(2)}, u32[]{:S(2)}) collective-permute-start(f32[48,256]{1,0:T(8,128)S(1)} %get-tuple-element.27.own_ref), channel_id=1, source_target_pairs={{0,6},{1,7},{2,4},{3,5},{4,2},{5,3},{6,0},{7,1},{8,14},{9,15},{10,... | collective-permute-start | bytes 147464 | tf_op jit(solution)/shard_map/ppermute | solution.py:495
  13.2 0.8 %collective-permute-start.2 = (f32[48,256]{1,0:T(8,128)S(1)}, f32[48,256]{1,0:T(8,128)S(1)}, u32[]{:S(2)}, u32[]{:S(2)}) collective-permute-start(f32[48,256]{1,0:T(8,128)S(1)} %get-tuple-element.27.own_ref), channel_id=1, source_target_pairs={{0,4},{1,5},{2,6},{3,7},{4,0},{5,1},{6,2},{7,3},{8,12},{9,13},{10,... | collective-permute-start | bytes 147464 | tf_op jit(solution)/shard_map/ppermute | solution.py:495
  14.0 0.4 %collective-permute-start.1 = (f32[48,256]{1,0:T(8,128)S(1)}, f32[48,256]{1,0:T(8,128)S(1)}, u32[]{:S(2)}, u32[]{:S(2)}) collective-permute-start(f32[48,256]{1,0:T(8,128)S(1)} %get-tuple-element.27.own_ref), channel_id=1, source_target_pairs={{0,2},{1,3},{2,0},{3,1},{4,6},{5,7},{6,4},{7,5},{8,10},{9,11},{10,... | collective-permute-start | bytes 147464 | tf_op jit(solution)/shard_map/ppermute | solution.py:495
  14.4 0.0 copy-done.1
  14.4 0.0 copy-done.2
  14.4 0.0 copy-start.3
  14.4 0.0 copy-start.4
  14.4 4.9 %query.1 = (f32[384,256]{1,0:T(8,128)S(1)}, f32[8,768]{1,0:T(8,128)S(1)}, bf16[8,768]{1,0:T(8,128)(2,1)S(1)}) custom-call(f32[16,256]{1,0:T(8,128)S(1)} %get-tuple-element.23.after_ref.first_ref, bf16[384,8192]{1,0:T(8,128)(2,1)} %hidden_hbm.3, f32[1,8192]{1,0:T(1,128)S(1)} %bitcast.10, bf16[8192,768]{1,0:T(8,128)(2,1)} %w_hbm.5, f32[7,768]{1,0:T(8,128)S(1)} %bitcast.7, ...), custom_call_target="tpu_custom_call" | custom-call | flops 1610612736 | bytes 10485760 | tf_op jit(solution)/shard_map/query/pallas_call | solution.py:499
  19.3 0.0 collective-permute-done.3.refs_2_
  19.3 0.0 collective-permute-done.2.refs_1_
  19.3 0.0 collective-permute-done.1.refs_0_
  19.4 0.9 %line.1 = (bf16[16,40,256]{2,1,0:T(8,128)(2,1)}, f32[48,256]{1,0:T(8,128)S(1)}, f32[16,256]{1,0:T(8,128)S(1)}, bf16[8,768]{1,0:T(8,128)(2,1)S(1)}) custom-call(s32[3,256]{1,0:T(4,128)S(1)} %broadcast_in_dim.12.place_ref, f32[48,256]{1,0:T(8,128)S(1)} %get-tuple-element.27.own_ref, f32[48,256]{1,0:T(8,128)S(1)} %collective-permute-done.1.refs_0_, ...), custom_call_target="tpu_custom_call" | custom-call | tf_op jit(solution)/shard_map/line/pallas_call | solution.py:514
  20.2 8.1 %all-to-all-start = ((bf16[16,40,256]{2,1,0:T(8,128)(2,1)}), bf16[16,40,256]{2,1,0:T(8,128)(2,1)S(1)}, u32[]{:S(2)}, u32[]{:S(2)}) async-start(bf16[16,40,256]{2,1,0:T(8,128)(2,1)} %get-tuple-element.32), calls=%async_computation | async-start | bytes 655360 | tf_op jit(solution)/shard_map/all_to_all | solution.py:526
  28.4 1.5 %collective-permute-start.4 = (bf16[8,768]{1,0:T(8,128)(2,1)S(1)}, bf16[8,768]{1,0:T(8,128)(2,1)S(1)}, u32[]{:S(2)}, u32[]{:S(2)}) collective-permute-start(bf16[8,768]{1,0:T(8,128)(2,1)S(1)} %get-tuple-element.29.after_ref), channel_id=1, source_target_pairs={{0,1},{1,2},{2,3},{3,4},{4,5},{5,6},{6,7},{7,8},{8,9},{9,10},{10,1... | collective-permute-start | bytes 36872 | tf_op jit(solution)/shard_map/ppermute | solution.py:527
  29.9 0.0 copy-done.3
  29.9 0.1 reshape.7.rrow_ref
  30.0 0.1 reshape.8.wrow_ref
  30.1 0.0 copy-done.4
  30.1 1.9 %local.1 = (f32[384,256]{1,0:T(8,128)S(1)}, bf16[384,128]{1,0:T(8,128)(2,1)S(1)}, bf16[384,128]{1,0:T(8,128)(2,1)S(1)}, bf16[256,3072]{1,0:T(8,128)(2,1)S(1)}) custom-call(bf16[8,768]{1,0:T(8,128)(2,1)S(1)} %get-tuple-element.29.after_ref, bf16[384,256]{1,0:T(8,128)(2,1)S(1)} %get-tuple-element.30.prod_ref, f32[1,256]{1,0:T(1,128)S(1)} %bitcast.11, ...), custom_call_target="tpu_custom_call" | custom-call | flops 75497472 | bytes 589824 | tf_op jit(solution)/shard_map/local/pallas_call | solution.py:531
  31.9 5.5 %all-to-all-done.all_ref = bf16[16,40,256]{2,1,0:T(8,128)(2,1)S(1)} async-done(((bf16[16,40,256]{2,1,0:T(8,128)(2,1)}), bf16[16,40,256]{2,1,0:T(8,128)(2,1)S(1)}, u32[]{:S(2)}, u32[]{:S(2)}) %all-to-all-start) | async-done | bytes 327712 | tf_op jit(solution)/shard_map/all_to_all | solution.py:526
  37.4 0.3 prefix.1.state_ref
  37.7 0.0 collective-permute-done.4.halo_ref
  37.8 4.8 %mix.1 = bf16[384,8192]{1,0:T(8,128)(2,1)} custom-call(f32[384,256]{1,0:T(8,128)S(1)} %get-tuple-element.26.query_ref, f32[384,256]{1,0:T(8,128)S(1)} %get-tuple-element.31.base_ref, f32[16,256]{1,0:T(8,128)S(1)} %prefix.1.state_ref, bf16[384,128]{1,0:T(8,128)(2,1)S(1)} %get-tuple-element.36.high_ref, ...), custom_call_target="tpu_custom_call" | custom-call | tf_op jit(solution)/shard_map/mix/pallas_call | solution.py:560
  (1 shorter events, 0.0 us)
Async XLA Ops:
  0.0 10.1 %copy-start = (f32[8,16]{1,0:T(8,128)S(1)}, f32[8,16]{1,0:T(8,128)}, u32[]{:S(2)}) copy-start(f32[8,16]{1,0:T(8,128)} %rates_ref.7) | copy-start | bytes 1540
  0.0 14.4 %copy-start.1 = (f32[768,7]{0,1:T(8,128)S(1)}, f32[768,7]{0,1:T(8,128)}, u32[]{:S(2)}) copy-start(f32[768,7]{0,1:T(8,128)} %param.11) | copy-start | bytes 64516
  0.0 14.4 %copy-start.2 = (f32[8192]{0:T(1024)S(1)}, f32[8192]{0:T(1024)}, u32[]{:S(2)}) copy-start(f32[8192]{0:T(1024)} %param.9) | copy-start | bytes 98308
  8.7 1.3 %collective-permute-start = (f32[48,256]{1,0:T(8,128)S(1)}, f32[48,256]{1,0:T(8,128)S(1)}, u32[]{:S(2)}, u32[]{:S(2)}) collective-permute-start(f32[48,256]{1,0:T(8,128)S(1)} %get-tuple-element.22.own_ref), channel_id=1, source_target_pairs={{0,1},{1,0},{2,3},{3,2},{4,5},{5,4},{6,7},{7,6},{8,9},{9,8},{10,11... | collective-permute-start | bytes 147464 | tf_op jit(solution)/shard_map/ppermute | solution.py:487
  10.2 9.1 %collective-permute-start.3 = (f32[48,256]{1,0:T(8,128)S(1)}, f32[48,256]{1,0:T(8,128)S(1)}, u32[]{:S(2)}, u32[]{:S(2)}) collective-permute-start(f32[48,256]{1,0:T(8,128)S(1)} %get-tuple-element.27.own_ref), channel_id=1, source_target_pairs={{0,6},{1,7},{2,4},{3,5},{4,2},{5,3},{6,0},{7,1},{8,14},{9,15},{10,... | collective-permute-start | bytes 147464 | tf_op jit(solution)/shard_map/ppermute | solution.py:495
  13.2 6.2 %collective-permute-start.2 = (f32[48,256]{1,0:T(8,128)S(1)}, f32[48,256]{1,0:T(8,128)S(1)}, u32[]{:S(2)}, u32[]{:S(2)}) collective-permute-start(f32[48,256]{1,0:T(8,128)S(1)} %get-tuple-element.27.own_ref), channel_id=1, source_target_pairs={{0,4},{1,5},{2,6},{3,7},{4,0},{5,1},{6,2},{7,3},{8,12},{9,13},{10,... | collective-permute-start | bytes 147464 | tf_op jit(solution)/shard_map/ppermute | solution.py:495
  14.0 5.4 %collective-permute-start.1 = (f32[48,256]{1,0:T(8,128)S(1)}, f32[48,256]{1,0:T(8,128)S(1)}, u32[]{:S(2)}, u32[]{:S(2)}) collective-permute-start(f32[48,256]{1,0:T(8,128)S(1)} %get-tuple-element.27.own_ref), channel_id=1, source_target_pairs={{0,2},{1,3},{2,0},{3,1},{4,6},{5,7},{6,4},{7,5},{8,10},{9,11},{10,... | collective-permute-start | bytes 147464 | tf_op jit(solution)/shard_map/ppermute | solution.py:495
  14.4 15.5 %copy-start.3 = (f32[8,16]{1,0:T(8,128)S(1)}, f32[8,16]{1,0:T(8,128)}, u32[]{:S(2)}) copy-start(f32[8,16]{1,0:T(8,128)} %residues_ref.3) | copy-start | bytes 1540
  14.4 15.6 %copy-start.4 = (f32[256]{0:T(256)S(1)}, f32[256]{0:T(256)}, u32[]{:S(2)}) copy-start(f32[256]{0:T(256)} %param.14) | copy-start | bytes 3076
  20.2 17.2 %all-to-all-start = ((bf16[16,40,256]{2,1,0:T(8,128)(2,1)}), bf16[16,40,256]{2,1,0:T(8,128)(2,1)S(1)}, u32[]{:S(2)}, u32[]{:S(2)}) async-start(bf16[16,40,256]{2,1,0:T(8,128)(2,1)} %get-tuple-element.32), calls=%async_computation | async-start | bytes 655360 | tf_op jit(solution)/shard_map/all_to_all | solution.py:526
  28.4 9.4 %collective-permute-start.4 = (bf16[8,768]{1,0:T(8,128)(2,1)S(1)}, bf16[8,768]{1,0:T(8,128)(2,1)S(1)}, u32[]{:S(2)}, u32[]{:S(2)}) collective-permute-start(bf16[8,768]{1,0:T(8,128)(2,1)S(1)} %get-tuple-element.29.after_ref), channel_id=1, source_target_pairs={{0,1},{1,2},{2,3},{3,4},{4,5},{5,6},{6,7},{7,8},{8,9},{9,10},{10,1... | collective-permute-start | bytes 36872 | tf_op jit(solution)/shard_map/ppermute | solution.py:527

commit v6 on v5

--- a/solution.py
+++ b/solution.py
@@ -72,10 +72,9 @@
 EDGE = slice(0, HALO)
 
 
-def multiply(hidden, inv, gain, near, total, weights, store, lines=(), late=1):
-    rows = hidden.shape[0]
-    count = len(weights)
-    block = near.shape[0] // count
+def multiply(hidden, inv, gain, near, total, arrive, store, late=1, count=8):
+    rows, width = hidden.shape
+    block = width // count
     part = rows // 3
     parts = [slice(first, first + part) for first in range(0, rows, part)]
 
@@ -83,12 +82,7 @@
         cols = slice(k * block, (k + 1) * block)
         scale = jnp.concatenate([inv[here, :]] * (block // 128), axis=1)
         normed = (hidden[here, cols].astype(F32) * scale * gain[:, cols]).astype(BF16)
-        return dot(normed, near[cols, :])
-
-    def arrive(k):
-        for copy in lines[k : k + 1]:
-            copy.wait()
-        weights[k].wait()
+        return dot(normed, near(cols))
 
     for k in range(count - late):
         arrive(k)
@@ -108,7 +102,7 @@
 
 def state_kernel(
     hidden_hbm, gain_hbm, w_hbm, taps_hbm, rates_hbm,
-    prod_ref, inv_ref, edge_ref, own_ref,
+    prod_ref, inv_ref, edge_ref, own_ref, ahead_ref,
     hidden, near, gain, taps, rates, total, ext, little, sems,
 ):
     rows, width = hidden.shape
@@ -161,7 +155,20 @@
         prod_ref[here, :] = product
         crossed.append(dot(high[:, here], product) + dot(low[:, here], product))
 
-    multiply(hidden, inv_ref, gain, near, total, weights, store, late=4)
+    deep = ahead_ref.shape[0]
+    ahead = pltpu.make_async_copy(
+        w_hbm.at[pl.ds(0, deep), pl.ds(0, chan)], ahead_ref, sems.at[2, 7]
+    )
+
+    def arrive(k):
+        weights[k].wait()
+        if k == 6:
+            ahead.start()
+
+    def weight_rows(cols):
+        return near[cols, :]
+
+    multiply(hidden, inv_ref, gain, weight_rows, total, arrive, store, late=4)
 
     edge_ref[0:HALO, :] = ext[HALO : 2 * HALO, :]
     edge_ref[HALO:, :] = ext[rows : rows + HALO, :]
@@ -171,6 +178,7 @@
     tail_v = feature(taps, little, EDGE, 2 * chan, chan, chan)
     state = fold(sum(crossed[1:], crossed[0]), modes, chan // rates.shape[0])
     own_ref[...] = jnp.concatenate([state] + heads + [tail_k, tail_v], axis=0)
+    ahead.wait()
 
 
 def joined(tail_k, head_k, tail_v, head_v):
@@ -236,23 +244,38 @@
 
 
 def query_kernel(
-    after_ref, hidden_hbm, gain_ref, w_hbm, taps_ref, inv_ref, edge_ref,
+    after_ref, hidden_hbm, gain_ref, w_hbm, taps_ref, inv_ref, edge_ref, ahead_ref,
     query_ref, head_ref, tail_ref, hidden, near, total, ext, sems,
 ):
-    rows, _ = hidden.shape
+    rows, width = hidden.shape
     chan = query_ref.shape[1]
-    lines = copies(hidden_hbm, hidden, 1, 8, sems.at[0])
-    weights = copies(w_hbm.at[:, pl.ds(0, chan)], near, 0, 8, sems.at[1])
-    for line, weight in zip(lines, weights):
+    deep, rest = ahead_ref.shape[0], near.shape[0]
+    count = 8
+    known = count * deep // width
+    lines = copies(hidden_hbm, hidden, 1, count, sems.at[0])
+    source = w_hbm.at[pl.ds(deep, rest), pl.ds(0, chan)]
+    weights = copies(source, near, 0, count - known, sems.at[1])
+    for k, line in enumerate(lines):
         line.start()
-        weight.start()
+        if k >= known:
+            weights[k - known].start()
+
+    def arrive(k):
+        lines[k].wait()
+        if k >= known:
+            weights[k - known].wait()
+
+    def weight_rows(cols):
+        if cols.stop <= deep:
+            return ahead_ref[cols, :]
+        return near[cols.start - deep : cols.stop - deep, :]
 
     def store(here, value):
         ext[HALO + here.start : HALO + here.stop, :] = value.astype(F32)
         query_ref[here, :] = feature(taps_ref, ext, here, 0, chan, 0)
 
     ext[0:HALO, :] = jnp.zeros((HALO, chan), F32)
-    multiply(hidden, inv_ref, gain_ref, near, total, weights, store, lines)
+    multiply(hidden, inv_ref, gain_ref, weight_rows, total, arrive, store)
     head_ref[:, :chan] = ext[HALO : 2 * HALO, :]
     head_ref[:, chan:] = edge_ref[0:HALO, :]
     tail = jnp.concatenate([ext[rows : rows + HALO, :], edge_ref[HALO:, :]], axis=1)
@@ -458,7 +481,8 @@
     skips = skip[None, :]
     vmem, sem = pltpu.VMEM, pltpu.SemaphoreType.DMA
 
-    product, inv, edges, own = call(
+    deep = width // 2
+    product, inv, edges, own, ahead = call(
         state_kernel,
         "state",
         [ANY] * 5,
@@ -467,6 +491,7 @@
             vmem((rows, 128), F32),
             vmem((2 * HALO, 2 * chan), F32),
             vmem((modes + 4 * HALO, chan), F32),
+            vmem((deep, chan), BF16),
         ],
         [
             vmem((rows, width), BF16),
@@ -499,18 +524,18 @@
     query, head, tail = call(
         query_kernel,
         "query",
-        [VMEM, ANY, VMEM, ANY] + [VMEM] * 3,
+        [VMEM, ANY, VMEM, ANY] + [VMEM] * 4,
         [vmem((rows, chan), F32), vmem((HALO, columns), F32), vmem((HALO, columns), BF16)],
         [
             vmem((rows, width), BF16),
-            vmem((width, chan), BF16),
+            vmem((width - deep, chan), BF16),
             vmem((rows, chan), F32),
             vmem((HALO + rows, chan), F32),
             sem((2, 8)),
         ],
         flops=2 * rows * width * chan,
         size=2 * width * (rows + chan),
-    )(first, in_hbm(hidden), gain, in_hbm(w_in), taps, inv, edges)
+    )(first, in_hbm(hidden), gain, in_hbm(w_in), taps, inv, edges, ahead)
     spread, inner, early, tail = call(
         functools.partial(line_kernel, hop=float(rows), reach=reach, per=per, along=along),
         "line",

time: 42.9 us -> 42.6 us (level)
  transfers between devices with their start and end apart: 6 -> 6, of which waited for: 2 -> 2; matrix products, arithmetic and copies ran while one was open for 1% -> 1% of each run, Pallas kernels for 17% -> 16%
where the time goes in v6:
time: 42.6 us; the launch traced here: 42.3 us
  Pallas kernels  21.2 us (50%)
  starting transfers between devices  13.9 us (33%)
  waiting for transfers between devices  6.61 us (16%)
    pallas_call x1, Pallas kernels, on_device(): call(state_kernel, 'state', [ANY] * 5, [vmem((rows, chan), BF16), vmem((r...  8.71 us
    all_to_all x1, starting transfers between devices, on_device(): lax.all_to_all(spread, 'tm', 0, 0, tiled=True, axis_index_groups=members)  8.15 us
    all_to_all x1, waiting for transfers between devices, on_device(): lax.all_to_all(spread, 'tm', 0, 0, tiled=True, axis_index_groups=members)  5.49 us
    pallas_call x1, Pallas kernels, on_device(): call(mix_kernel, 'mix', [VMEM] * 12 + [ANY], jax.ShapeDtypeStruct((rows,...  4.75 us
    pallas_call x1, Pallas kernels, on_device(): call(query_kernel, 'query', [VMEM, ANY, VMEM, ANY] + [VMEM] * 4, [vmem((r...  4.53 us
    ppermute x3, starting transfers between devices, on_device(): lax.ppermute(chip, 'tm', [(i, i ^ 2 * m) for i in range(devices)])  4.17 us
    pallas_call x1, Pallas kernels, on_device(): call(local_kernel, 'local', [VMEM] * 7 + [ANY], [vmem((rows, chan), F32),...  1.88 us
    ppermute x1, starting transfers between devices, on_device(): halo = lax.ppermute(tail, 'tm', [(i, i + 1) for i in range(devices - 1)])  1.47 us
  transfers between devices with their start and end apart: 6, of which 2 were waited for; matrix products, arithmetic and copies ran while one was open for 1% of the time, Pallas kernels for 16%

profile of v6, /device:TPU:0, one launch (start us, length us, event | category | flops | bytes accessed | tf_op | source)
XLA Modules:
  0.0 42.3 jit_solution(16645598272266373188)
XLA Ops:
  0.0 0.0 copy-start
  0.0 0.0 copy-start.1
  0.0 0.0 copy-start.2
  0.0 8.7 %state.1 = (bf16[384,256]{1,0:T(8,128)(2,1)S(1)}, f32[384,128]{1,0:T(8,128)S(1)}, f32[16,512]{1,0:T(8,128)S(1)}, f32[48,256]{1,0:T(8,128)S(1)}, bf16[4096,256]{1,0:T(8,128)(2,1)S(1)}) custom-call(bf16[384,8192]{1,0:T(8,128)(2,1)} %hidden_hbm.3, f32[1,8192]{1,0:T(1,128)} %bitcast.9, bf16[8192,768]{1,0:T(8,128)(2,1)} %w_hbm.5, f32[7,768]{1,0:T(8,128)} %bitcast.6, ...), custom_call_target="tpu_custom_call" | custom-call | flops 3221225472 | bytes 14680064 | tf_op jit(solution)/shard_map/state/pallas_call | solution.py:485
  8.7 0.1 collective-permute-start
  8.9 0.1 pad_add_fusion
  8.9 1.1 %collective-permute-done.got_ref = f32[48,256]{1,0:T(8,128)S(1)} collective-permute-done((f32[48,256]{1,0:T(8,128)S(1)}, f32[48,256]{1,0:T(8,128)S(1)}, u32[]{:S(2)}, u32[]{:S(2)}) %collective-permute-start) | collective-permute-done | bytes 49184 | tf_op jit(solution)/shard_map/ppermute | solution.py:512
  10.0 0.1 broadcast_in_dim.12.place_ref
  10.1 0.0 copy-done
  10.1 0.1 chip.1
  10.2 2.9 %collective-permute-start.3 = (f32[48,256]{1,0:T(8,128)S(1)}, f32[48,256]{1,0:T(8,128)S(1)}, u32[]{:S(2)}, u32[]{:S(2)}) collective-permute-start(f32[48,256]{1,0:T(8,128)S(1)} %get-tuple-element.29.own_ref), channel_id=1, source_target_pairs={{0,6},{1,7},{2,4},{3,5},{4,2},{5,3},{6,0},{7,1},{8,14},{9,15},{10,... | collective-permute-start | bytes 147464 | tf_op jit(solution)/shard_map/ppermute | solution.py:520
  13.2 0.8 %collective-permute-start.2 = (f32[48,256]{1,0:T(8,128)S(1)}, f32[48,256]{1,0:T(8,128)S(1)}, u32[]{:S(2)}, u32[]{:S(2)}) collective-permute-start(f32[48,256]{1,0:T(8,128)S(1)} %get-tuple-element.29.own_ref), channel_id=1, source_target_pairs={{0,4},{1,5},{2,6},{3,7},{4,0},{5,1},{6,2},{7,3},{8,12},{9,13},{10,... | collective-permute-start | bytes 147464 | tf_op jit(solution)/shard_map/ppermute | solution.py:520
  14.0 0.4 %collective-permute-start.1 = (f32[48,256]{1,0:T(8,128)S(1)}, f32[48,256]{1,0:T(8,128)S(1)}, u32[]{:S(2)}, u32[]{:S(2)}) collective-permute-start(f32[48,256]{1,0:T(8,128)S(1)} %get-tuple-element.29.own_ref), channel_id=1, source_target_pairs={{0,2},{1,3},{2,0},{3,1},{4,6},{5,7},{6,4},{7,5},{8,10},{9,11},{10,... | collective-permute-start | bytes 147464 | tf_op jit(solution)/shard_map/ppermute | solution.py:520
  14.4 0.0 copy-done.1
  14.4 0.0 copy-done.2
  14.4 0.0 copy-start.3
  14.4 0.0 copy-start.4
  14.4 4.5 %query.1 = (f32[384,256]{1,0:T(8,128)S(1)}, f32[8,768]{1,0:T(8,128)S(1)}, bf16[8,768]{1,0:T(8,128)(2,1)S(1)}) custom-call(f32[16,256]{1,0:T(8,128)S(1)} %get-tuple-element.24.after_ref.first_ref, bf16[384,8192]{1,0:T(8,128)(2,1)} %hidden_hbm.3, f32[1,8192]{1,0:T(1,128)S(1)} %bitcast.10, bf16[8192,768]{1,0:T(8,128)(2,1)} %w_hbm.5, f32[7,768]{1,0:T(8,128)S(1)} %bitcast.7, ...), custom_call_target="tpu_custom_call" | custom-call | flops 1610612736 | bytes 10485760 | tf_op jit(solution)/shard_map/query/pallas_call | solution.py:524
  19.0 0.0 collective-permute-done.3.refs_2_
  19.0 0.0 collective-permute-done.2.refs_1_
  19.0 0.0 collective-permute-done.1.refs_0_
  19.0 0.9 %line.1 = (bf16[16,40,256]{2,1,0:T(8,128)(2,1)}, f32[48,256]{1,0:T(8,128)S(1)}, f32[16,256]{1,0:T(8,128)S(1)}, bf16[8,768]{1,0:T(8,128)(2,1)S(1)}) custom-call(s32[3,256]{1,0:T(4,128)S(1)} %broadcast_in_dim.12.place_ref, f32[48,256]{1,0:T(8,128)S(1)} %get-tuple-element.29.own_ref, f32[48,256]{1,0:T(8,128)S(1)} %collective-permute-done.1.refs_0_, ...), custom_call_target="tpu_custom_call" | custom-call | tf_op jit(solution)/shard_map/line/pallas_call | solution.py:539
  19.9 8.1 %all-to-all-start = ((bf16[16,40,256]{2,1,0:T(8,128)(2,1)}), bf16[16,40,256]{2,1,0:T(8,128)(2,1)S(1)}, u32[]{:S(2)}, u32[]{:S(2)}) async-start(bf16[16,40,256]{2,1,0:T(8,128)(2,1)} %get-tuple-element.34), calls=%async_computation | async-start | bytes 655360 | tf_op jit(solution)/shard_map/all_to_all | solution.py:551
  28.0 1.5 %collective-permute-start.4 = (bf16[8,768]{1,0:T(8,128)(2,1)S(1)}, bf16[8,768]{1,0:T(8,128)(2,1)S(1)}, u32[]{:S(2)}, u32[]{:S(2)}) collective-permute-start(bf16[8,768]{1,0:T(8,128)(2,1)S(1)} %get-tuple-element.31.after_ref), channel_id=1, source_target_pairs={{0,1},{1,2},{2,3},{3,4},{4,5},{5,6},{6,7},{7,8},{8,9},{9,10},{10,1... | collective-permute-start | bytes 36872 | tf_op jit(solution)/shard_map/ppermute | solution.py:552
  29.5 0.0 copy-done.3
  29.5 0.1 reshape.7.rrow_ref
  29.6 0.1 reshape.8.wrow_ref
  29.7 0.0 copy-done.4
  29.7 1.9 %local.1 = (f32[384,256]{1,0:T(8,128)S(1)}, bf16[384,128]{1,0:T(8,128)(2,1)S(1)}, bf16[384,128]{1,0:T(8,128)(2,1)S(1)}, bf16[256,3072]{1,0:T(8,128)(2,1)S(1)}) custom-call(bf16[8,768]{1,0:T(8,128)(2,1)S(1)} %get-tuple-element.31.after_ref, bf16[384,256]{1,0:T(8,128)(2,1)S(1)} %get-tuple-element.32.prod_ref, f32[1,256]{1,0:T(1,128)S(1)} %bitcast.11, ...), custom_call_target="tpu_custom_call" | custom-call | flops 75497472 | bytes 589824 | tf_op jit(solution)/shard_map/local/pallas_call | solution.py:556
  31.6 5.5 %all-to-all-done.all_ref = bf16[16,40,256]{2,1,0:T(8,128)(2,1)S(1)} async-done(((bf16[16,40,256]{2,1,0:T(8,128)(2,1)}), bf16[16,40,256]{2,1,0:T(8,128)(2,1)S(1)}, u32[]{:S(2)}, u32[]{:S(2)}) %all-to-all-start) | async-done | bytes 327712 | tf_op jit(solution)/shard_map/all_to_all | solution.py:551
  37.1 0.3 prefix.1.state_ref
  37.4 0.0 collective-permute-done.4.halo_ref
  37.4 4.7 %mix.1 = bf16[384,8192]{1,0:T(8,128)(2,1)} custom-call(f32[384,256]{1,0:T(8,128)S(1)} %get-tuple-element.28.query_ref, f32[384,256]{1,0:T(8,128)S(1)} %get-tuple-element.33.base_ref, f32[16,256]{1,0:T(8,128)S(1)} %prefix.1.state_ref, bf16[384,128]{1,0:T(8,128)(2,1)S(1)} %get-tuple-element.38.high_ref, ...), custom_call_target="tpu_custom_call" | custom-call | tf_op jit(solution)/shard_map/mix/pallas_call | solution.py:585
  (1 shorter events, 0.0 us)
Async XLA Ops:
  0.0 10.1 %copy-start = (f32[8,16]{1,0:T(8,128)S(1)}, f32[8,16]{1,0:T(8,128)}, u32[]{:S(2)}) copy-start(f32[8,16]{1,0:T(8,128)} %rates_ref.7) | copy-start | bytes 1540
  0.0 14.4 %copy-start.1 = (f32[768,7]{0,1:T(8,128)S(1)}, f32[768,7]{0,1:T(8,128)}, u32[]{:S(2)}) copy-start(f32[768,7]{0,1:T(8,128)} %param.11) | copy-start | bytes 64516
  0.0 14.4 %copy-start.2 = (f32[8192]{0:T(1024)S(1)}, f32[8192]{0:T(1024)}, u32[]{:S(2)}) copy-start(f32[8192]{0:T(1024)} %param.9) | copy-start | bytes 98308
  8.7 1.3 %collective-permute-start = (f32[48,256]{1,0:T(8,128)S(1)}, f32[48,256]{1,0:T(8,128)S(1)}, u32[]{:S(2)}, u32[]{:S(2)}) collective-permute-start(f32[48,256]{1,0:T(8,128)S(1)} %get-tuple-element.23.own_ref), channel_id=1, source_target_pairs={{0,1},{1,0},{2,3},{3,2},{4,5},{5,4},{6,7},{7,6},{8,9},{9,8},{10,11... | collective-permute-start | bytes 147464 | tf_op jit(solution)/shard_map/ppermute | solution.py:512
  10.2 8.7 %collective-permute-start.3 = (f32[48,256]{1,0:T(8,128)S(1)}, f32[48,256]{1,0:T(8,128)S(1)}, u32[]{:S(2)}, u32[]{:S(2)}) collective-permute-start(f32[48,256]{1,0:T(8,128)S(1)} %get-tuple-element.29.own_ref), channel_id=1, source_target_pairs={{0,6},{1,7},{2,4},{3,5},{4,2},{5,3},{6,0},{7,1},{8,14},{9,15},{10,... | collective-permute-start | bytes 147464 | tf_op jit(solution)/shard_map/ppermute | solution.py:520
  13.2 5.8 %collective-permute-start.2 = (f32[48,256]{1,0:T(8,128)S(1)}, f32[48,256]{1,0:T(8,128)S(1)}, u32[]{:S(2)}, u32[]{:S(2)}) collective-permute-start(f32[48,256]{1,0:T(8,128)S(1)} %get-tuple-element.29.own_ref), channel_id=1, source_target_pairs={{0,4},{1,5},{2,6},{3,7},{4,0},{5,1},{6,2},{7,3},{8,12},{9,13},{10,... | collective-permute-start | bytes 147464 | tf_op jit(solution)/shard_map/ppermute | solution.py:520
  14.0 5.0 %collective-permute-start.1 = (f32[48,256]{1,0:T(8,128)S(1)}, f32[48,256]{1,0:T(8,128)S(1)}, u32[]{:S(2)}, u32[]{:S(2)}) collective-permute-start(f32[48,256]{1,0:T(8,128)S(1)} %get-tuple-element.29.own_ref), channel_id=1, source_target_pairs={{0,2},{1,3},{2,0},{3,1},{4,6},{5,7},{6,4},{7,5},{8,10},{9,11},{10,... | collective-permute-start | bytes 147464 | tf_op jit(solution)/shard_map/ppermute | solution.py:520
  14.4 15.1 %copy-start.3 = (f32[8,16]{1,0:T(8,128)S(1)}, f32[8,16]{1,0:T(8,128)}, u32[]{:S(2)}) copy-start(f32[8,16]{1,0:T(8,128)} %residues_ref.3) | copy-start | bytes 1540
  14.4 15.3 %copy-start.4 = (f32[256]{0:T(256)S(1)}, f32[256]{0:T(256)}, u32[]{:S(2)}) copy-start(f32[256]{0:T(256)} %param.14) | copy-start | bytes 3076
  19.9 17.2 %all-to-all-start = ((bf16[16,40,256]{2,1,0:T(8,128)(2,1)}), bf16[16,40,256]{2,1,0:T(8,128)(2,1)S(1)}, u32[]{:S(2)}, u32[]{:S(2)}) async-start(bf16[16,40,256]{2,1,0:T(8,128)(2,1)} %get-tuple-element.34), calls=%async_computation | async-start | bytes 655360 | tf_op jit(solution)/shard_map/all_to_all | solution.py:551
  28.0 9.4 %collective-permute-start.4 = (bf16[8,768]{1,0:T(8,128)(2,1)S(1)}, bf16[8,768]{1,0:T(8,128)(2,1)S(1)}, u32[]{:S(2)}, u32[]{:S(2)}) collective-permute-start(bf16[8,768]{1,0:T(8,128)(2,1)S(1)} %get-tuple-element.31.after_ref), channel_id=1, source_target_pairs={{0,1},{1,2},{2,3},{3,4},{4,5},{5,6},{6,7},{7,8},{8,9},{9,10},{10,1... | collective-permute-start | bytes 36872 | tf_op jit(solution)/shard_map/ppermute | solution.py:552

commit v7 on v6

--- a/solution.py
+++ b/solution.py
@@ -284,7 +284,7 @@
 
 def local_kernel(
     after_ref, prod_ref, skip_ref, rates_ref, residues_ref, rrow_ref, wrow_ref, w_hbm,
-    base_ref, high_ref, low_ref, near_ref, sem,
+    base_ref, high_ref, low_ref, near_ref, rise_ref, above_ref, sem,
 ):
     fetch = pltpu.make_async_copy(w_hbm.at[:, pl.ds(0, near_ref.shape[1])], near_ref, sem)
     fetch.start()
@@ -327,6 +327,14 @@
         cols = slice(g * per, (g + 1) * per)
         for here in places:
             base_ref[here, cols] += dot(square, prod_ref[here, cols])
+    rate = by_channel(rcol, modes, per, chan)
+    weight = by_channel(wcol, modes, per, chan)
+    reach = rise_ref.shape[0] // modes
+    for s in range(reach):
+        rise_ref[s * modes : (s + 1) * modes, :] = jnp.exp(rate * (s + 1.0))
+    for s in range(HALO):
+        above = jnp.sum(weight * jnp.exp(rate * float(s)), axis=0, keepdims=True)
+        above_ref[s : s + 1, :] = above
     fetch.wait()
 
 
@@ -389,7 +397,7 @@
 
 def mix_kernel(
     query_ref, base_ref, state_ref, high_ref, low_ref, head_ref, halo_ref,
-    taps_ref, skip_ref, rates_ref, residues_ref, near_ref, w_hbm,
+    taps_ref, skip_ref, lift_ref, above_ref, near_ref, w_hbm,
     out_hbm, w_ref, staged, gated, ext, shift, sums, sems,
 ):
     steps = sems.shape[1]
@@ -400,7 +408,8 @@
     for copy in weights:
         copy.start()
     rows, chan = query_ref.shape
-    groups, modes = rates_ref.shape
+    modes = state_ref.shape[0]
+    groups = high_ref.shape[1] // modes
     per = chan // groups
     reach = taps_ref.shape[0] - 1
     ext[0:HALO, :] = halo_ref[...].astype(F32)
@@ -409,14 +418,9 @@
     product = jnp.where(spot(0, HALO) < reach, key * value, 0.0).astype(BF16).astype(F32)
     shift[0:HALO, :] = product
     shift[HALO:, :] = jnp.zeros((HALO, chan), F32)
-    rcol = column(rates_ref[...])
-    wcol = column(residues_ref[...]) * jnp.sqrt(2.0 * rcol)
-    rate = by_channel(rcol, modes, per, chan)
-    weight = by_channel(wcol, modes, per, chan)
-
     state = state_ref[...]
     for s in range(reach):
-        state += jnp.exp(rate * (s + 1.0)) * product[s : s + 1, :]
+        state += lift_ref[s * modes : (s + 1) * modes, :] * product[s : s + 1, :]
     owner = spot(1, chan) // per
     spread = jnp.concatenate([jnp.where(owner == g, state, 0.0) for g in range(groups)], axis=0)
     high, low = split(spread)
@@ -424,8 +428,7 @@
     sums[...] = base_ref[...] + (dot(rise, high) + dot(low_ref[...], high) + dot(rise, low))
     start = sums[0:HALO, :] + skip_ref[...] * product
     for ahead in range(1, reach):
-        above = jnp.sum(weight * jnp.exp(rate * float(ahead)), axis=0, keepdims=True)
-        start -= above * shift[ahead : ahead + HALO, :]
+        start -= above_ref[ahead : ahead + 1, :] * shift[ahead : ahead + HALO, :]
     sums[...] = query_ref[...] * sums[...]
     sums[0:HALO, :] = query * start
     gated[...] = sums[...].astype(BF16)
@@ -553,7 +556,7 @@
 
     weights = residues * jnp.sqrt(2.0 * rates)
     kept = w_out.shape[1] * 3 // 8
-    base, high, low, w_near = call(
+    base, high, low, w_near, lift, above = call(
         local_kernel,
         "local",
         [VMEM] * 7 + [ANY],
@@ -562,6 +565,8 @@
             vmem((rows, groups * modes), BF16),
             vmem((rows, groups * modes), BF16),
             vmem((chan, kept), BF16),
+            vmem((reach * modes, chan), F32),
+            vmem((HALO, chan), F32),
         ],
         [sem],
         flops=2 * rows * rows * chan,
@@ -598,7 +603,7 @@
         ],
         out_specs=ANY,
     )(
-        query, base, state, high, low, head, halo, taps, skips, rates, residues,
+        query, base, state, high, low, head, halo, taps, skips, lift, above,
         w_near, in_hbm(w_out),
     )
 

time: 42.6 us -> 42.5 us (level)
  no operation moved by 1% of the time
where the time goes in v7:
time: 42.5 us; the launch traced here: 42.2 us
  Pallas kernels  21.1 us (50%)
  starting transfers between devices  13.9 us (33%)
  waiting for transfers between devices  6.56 us (15%)
    pallas_call x1, Pallas kernels, on_device(): call(state_kernel, 'state', [ANY] * 5, [vmem((rows, chan), BF16), vmem((r...  8.71 us
    all_to_all x1, starting transfers between devices, on_device(): lax.all_to_all(spread, 'tm', 0, 0, tiled=True, axis_index_groups=members)  8.15 us
    all_to_all x1, waiting for transfers between devices, on_device(): lax.all_to_all(spread, 'tm', 0, 0, tiled=True, axis_index_groups=members)  5.45 us
    pallas_call x1, Pallas kernels, on_device(): call(mix_kernel, 'mix', [VMEM] * 12 + [ANY], jax.ShapeDtypeStruct((rows,...  4.65 us
    pallas_call x1, Pallas kernels, on_device(): call(query_kernel, 'query', [VMEM, ANY, VMEM, ANY] + [VMEM] * 4, [vmem((r...  4.53 us
    ppermute x3, starting transfers between devices, on_device(): lax.ppermute(chip, 'tm', [(i, i ^ 2 * m) for i in range(devices)])  4.17 us
    pallas_call x1, Pallas kernels, on_device(): call(local_kernel, 'local', [VMEM] * 7 + [ANY], [vmem((rows, chan), F32),...  1.92 us
    ppermute x1, starting transfers between devices, on_device(): halo = lax.ppermute(tail, 'tm', [(i, i + 1) for i in range(devices - 1)])  1.47 us
  transfers between devices with their start and end apart: 6, of which 2 were waited for; matrix products, arithmetic and copies ran while one was open for 1% of the time, Pallas kernels for 16%

profile of v7, /device:TPU:0, one launch (start us, length us, event | category | flops | bytes accessed | tf_op | source)
XLA Modules:
  0.0 42.2 jit_solution(13139785037492719346)
XLA Ops:
  0.0 0.0 copy-start.1
  0.0 0.0 copy-start
  0.0 0.0 copy-start.2
  0.0 8.7 %state.1 = (bf16[384,256]{1,0:T(8,128)(2,1)S(1)}, f32[384,128]{1,0:T(8,128)S(1)}, f32[16,512]{1,0:T(8,128)S(1)}, f32[48,256]{1,0:T(8,128)S(1)}, bf16[4096,256]{1,0:T(8,128)(2,1)S(1)}) custom-call(bf16[384,8192]{1,0:T(8,128)(2,1)} %hidden_hbm.3, f32[1,8192]{1,0:T(1,128)} %bitcast.9, bf16[8192,768]{1,0:T(8,128)(2,1)} %w_hbm.5, f32[7,768]{1,0:T(8,128)} %bitcast.6, ...), custom_call_target="tpu_custom_call" | custom-call | flops 3221225472 | bytes 14680064 | tf_op jit(solution)/shard_map/state/pallas_call | solution.py:488
  8.7 0.1 collective-permute-start
  8.9 0.1 pad_add_fusion
  8.9 1.1 %collective-permute-done.got_ref = f32[48,256]{1,0:T(8,128)S(1)} collective-permute-done((f32[48,256]{1,0:T(8,128)S(1)}, f32[48,256]{1,0:T(8,128)S(1)}, u32[]{:S(2)}, u32[]{:S(2)}) %collective-permute-start) | collective-permute-done | bytes 49184 | tf_op jit(solution)/shard_map/ppermute | solution.py:515
  10.0 0.1 broadcast_in_dim.12.place_ref
  10.1 0.0 copy-done.1
  10.1 0.1 chip.1
  10.2 2.9 %collective-permute-start.3 = (f32[48,256]{1,0:T(8,128)S(1)}, f32[48,256]{1,0:T(8,128)S(1)}, u32[]{:S(2)}, u32[]{:S(2)}) collective-permute-start(f32[48,256]{1,0:T(8,128)S(1)} %get-tuple-element.31.own_ref), channel_id=1, source_target_pairs={{0,6},{1,7},{2,4},{3,5},{4,2},{5,3},{6,0},{7,1},{8,14},{9,15},{10,... | collective-permute-start | bytes 147464 | tf_op jit(solution)/shard_map/ppermute | solution.py:523
  13.2 0.8 %collective-permute-start.2 = (f32[48,256]{1,0:T(8,128)S(1)}, f32[48,256]{1,0:T(8,128)S(1)}, u32[]{:S(2)}, u32[]{:S(2)}) collective-permute-start(f32[48,256]{1,0:T(8,128)S(1)} %get-tuple-element.31.own_ref), channel_id=1, source_target_pairs={{0,4},{1,5},{2,6},{3,7},{4,0},{5,1},{6,2},{7,3},{8,12},{9,13},{10,... | collective-permute-start | bytes 147464 | tf_op jit(solution)/shard_map/ppermute | solution.py:523
  14.0 0.4 %collective-permute-start.1 = (f32[48,256]{1,0:T(8,128)S(1)}, f32[48,256]{1,0:T(8,128)S(1)}, u32[]{:S(2)}, u32[]{:S(2)}) collective-permute-start(f32[48,256]{1,0:T(8,128)S(1)} %get-tuple-element.31.own_ref), channel_id=1, source_target_pairs={{0,2},{1,3},{2,0},{3,1},{4,6},{5,7},{6,4},{7,5},{8,10},{9,11},{10,... | collective-permute-start | bytes 147464 | tf_op jit(solution)/shard_map/ppermute | solution.py:523
  14.4 0.0 copy-done
  14.4 0.0 copy-done.2
  14.4 0.0 copy-start.3
  14.4 0.0 copy-start.4
  14.4 4.5 %query.1 = (f32[384,256]{1,0:T(8,128)S(1)}, f32[8,768]{1,0:T(8,128)S(1)}, bf16[8,768]{1,0:T(8,128)(2,1)S(1)}) custom-call(f32[16,256]{1,0:T(8,128)S(1)} %get-tuple-element.26.after_ref.first_ref, bf16[384,8192]{1,0:T(8,128)(2,1)} %hidden_hbm.3, f32[1,8192]{1,0:T(1,128)S(1)} %bitcast.10, bf16[8192,768]{1,0:T(8,128)(2,1)} %w_hbm.5, f32[7,768]{1,0:T(8,128)S(1)} %bitcast.7, ...), custom_call_target="tpu_custom_call" | custom-call | flops 1610612736 | bytes 10485760 | tf_op jit(solution)/shard_map/query/pallas_call | solution.py:527
  19.0 0.0 collective-permute-done.3.refs_2_
  19.0 0.0 collective-permute-done.2.refs_1_
  19.0 0.0 collective-permute-done.1.refs_0_
  19.0 0.9 %line.1 = (bf16[16,40,256]{2,1,0:T(8,128)(2,1)}, f32[48,256]{1,0:T(8,128)S(1)}, f32[16,256]{1,0:T(8,128)S(1)}, bf16[8,768]{1,0:T(8,128)(2,1)S(1)}) custom-call(s32[3,256]{1,0:T(4,128)S(1)} %broadcast_in_dim.12.place_ref, f32[48,256]{1,0:T(8,128)S(1)} %get-tuple-element.31.own_ref, f32[48,256]{1,0:T(8,128)S(1)} %collective-permute-done.1.refs_0_, ...), custom_call_target="tpu_custom_call" | custom-call | tf_op jit(solution)/shard_map/line/pallas_call | solution.py:542
  19.9 8.1 %all-to-all-start = ((bf16[16,40,256]{2,1,0:T(8,128)(2,1)}), bf16[16,40,256]{2,1,0:T(8,128)(2,1)S(1)}, u32[]{:S(2)}, u32[]{:S(2)}) async-start(bf16[16,40,256]{2,1,0:T(8,128)(2,1)} %get-tuple-element.36), calls=%async_computation | async-start | bytes 655360 | tf_op jit(solution)/shard_map/all_to_all | solution.py:554
  28.0 1.5 %collective-permute-start.4 = (bf16[8,768]{1,0:T(8,128)(2,1)S(1)}, bf16[8,768]{1,0:T(8,128)(2,1)S(1)}, u32[]{:S(2)}, u32[]{:S(2)}) collective-permute-start(bf16[8,768]{1,0:T(8,128)(2,1)S(1)} %get-tuple-element.33.after_ref), channel_id=1, source_target_pairs={{0,1},{1,2},{2,3},{3,4},{4,5},{5,6},{6,7},{7,8},{8,9},{9,10},{10,1... | collective-permute-start | bytes 36872 | tf_op jit(solution)/shard_map/ppermute | solution.py:555
  29.5 0.0 copy-done.3
  29.5 0.1 reshape.7.rrow_ref
  29.6 0.1 reshape.8.wrow_ref
  29.7 0.0 copy-done.4
  29.7 1.9 %local.1 = (f32[384,256]{1,0:T(8,128)S(1)}, bf16[384,128]{1,0:T(8,128)(2,1)S(1)}, bf16[384,128]{1,0:T(8,128)(2,1)S(1)}, bf16[256,3072]{1,0:T(8,128)(2,1)S(1)}, f...) custom-call(bf16[8,768]{1,0:T(8,128)(2,1)S(1)} %get-tuple-element.33.after_ref, ...), custom_call_target="tpu_custom_call" | custom-call | flops 75497472 | bytes 589824 | tf_op jit(solution)/shard_map/local/pallas_call | solution.py:559
  31.6 5.4 %all-to-all-done.all_ref = bf16[16,40,256]{2,1,0:T(8,128)(2,1)S(1)} async-done(((bf16[16,40,256]{2,1,0:T(8,128)(2,1)}), bf16[16,40,256]{2,1,0:T(8,128)(2,1)S(1)}, u32[]{:S(2)}, u32[]{:S(2)}) %all-to-all-start) | async-done | bytes 327712 | tf_op jit(solution)/shard_map/all_to_all | solution.py:554
  37.1 0.3 prefix.1.state_ref
  37.4 0.0 collective-permute-done.4.halo_ref
  37.4 4.7 %mix.1 = bf16[384,8192]{1,0:T(8,128)(2,1)} custom-call(f32[384,256]{1,0:T(8,128)S(1)} %get-tuple-element.30.query_ref, f32[384,256]{1,0:T(8,128)S(1)} %get-tuple-element.35.base_ref, f32[16,256]{1,0:T(8,128)S(1)} %prefix.1.state_ref, bf16[384,128]{1,0:T(8,128)(2,1)S(1)} %get-tuple-element.40.high_ref, ...), custom_call_target="tpu_custom_call" | custom-call | tf_op jit(solution)/shard_map/mix/pallas_call | solution.py:590
  (1 shorter events, 0.0 us)
Async XLA Ops:
  0.0 10.1 %copy-start.1 = (f32[8,16]{1,0:T(8,128)S(1)}, f32[8,16]{1,0:T(8,128)}, u32[]{:S(2)}) copy-start(f32[8,16]{1,0:T(8,128)} %rates_ref.5) | copy-start | bytes 1540
  0.0 14.4 %copy-start = (f32[768,7]{0,1:T(8,128)S(1)}, f32[768,7]{0,1:T(8,128)}, u32[]{:S(2)}) copy-start(f32[768,7]{0,1:T(8,128)} %param.11) | copy-start | bytes 64516
  0.0 14.4 %copy-start.2 = (f32[8192]{0:T(1024)S(1)}, f32[8192]{0:T(1024)}, u32[]{:S(2)}) copy-start(f32[8192]{0:T(1024)} %param.9) | copy-start | bytes 98308
  8.7 1.3 %collective-permute-start = (f32[48,256]{1,0:T(8,128)S(1)}, f32[48,256]{1,0:T(8,128)S(1)}, u32[]{:S(2)}, u32[]{:S(2)}) collective-permute-start(f32[48,256]{1,0:T(8,128)S(1)} %get-tuple-element.25.own_ref), channel_id=1, source_target_pairs={{0,1},{1,0},{2,3},{3,2},{4,5},{5,4},{6,7},{7,6},{8,9},{9,8},{10,11... | collective-permute-start | bytes 147464 | tf_op jit(solution)/shard_map/ppermute | solution.py:515
  10.2 8.7 %collective-permute-start.3 = (f32[48,256]{1,0:T(8,128)S(1)}, f32[48,256]{1,0:T(8,128)S(1)}, u32[]{:S(2)}, u32[]{:S(2)}) collective-permute-start(f32[48,256]{1,0:T(8,128)S(1)} %get-tuple-element.31.own_ref), channel_id=1, source_target_pairs={{0,6},{1,7},{2,4},{3,5},{4,2},{5,3},{6,0},{7,1},{8,14},{9,15},{10,... | collective-permute-start | bytes 147464 | tf_op jit(solution)/shard_map/ppermute | solution.py:523
  13.2 5.8 %collective-permute-start.2 = (f32[48,256]{1,0:T(8,128)S(1)}, f32[48,256]{1,0:T(8,128)S(1)}, u32[]{:S(2)}, u32[]{:S(2)}) collective-permute-start(f32[48,256]{1,0:T(8,128)S(1)} %get-tuple-element.31.own_ref), channel_id=1, source_target_pairs={{0,4},{1,5},{2,6},{3,7},{4,0},{5,1},{6,2},{7,3},{8,12},{9,13},{10,... | collective-permute-start | bytes 147464 | tf_op jit(solution)/shard_map/ppermute | solution.py:523
  14.0 5.0 %collective-permute-start.1 = (f32[48,256]{1,0:T(8,128)S(1)}, f32[48,256]{1,0:T(8,128)S(1)}, u32[]{:S(2)}, u32[]{:S(2)}) collective-permute-start(f32[48,256]{1,0:T(8,128)S(1)} %get-tuple-element.31.own_ref), channel_id=1, source_target_pairs={{0,2},{1,3},{2,0},{3,1},{4,6},{5,7},{6,4},{7,5},{8,10},{9,11},{10,... | collective-permute-start | bytes 147464 | tf_op jit(solution)/shard_map/ppermute | solution.py:523
  14.4 15.1 %copy-start.3 = (f32[8,16]{1,0:T(8,128)S(1)}, f32[8,16]{1,0:T(8,128)}, u32[]{:S(2)}) copy-start(f32[8,16]{1,0:T(8,128)} %residues_ref.1) | copy-start | bytes 1540
  14.4 15.3 %copy-start.4 = (f32[256]{0:T(256)S(1)}, f32[256]{0:T(256)}, u32[]{:S(2)}) copy-start(f32[256]{0:T(256)} %param.14) | copy-start | bytes 3076
  19.9 17.2 %all-to-all-start = ((bf16[16,40,256]{2,1,0:T(8,128)(2,1)}), bf16[16,40,256]{2,1,0:T(8,128)(2,1)S(1)}, u32[]{:S(2)}, u32[]{:S(2)}) async-start(bf16[16,40,256]{2,1,0:T(8,128)(2,1)} %get-tuple-element.36), calls=%async_computation | async-start | bytes 655360 | tf_op jit(solution)/shard_map/all_to_all | solution.py:554
  28.0 9.4 %collective-permute-start.4 = (bf16[8,768]{1,0:T(8,128)(2,1)S(1)}, bf16[8,768]{1,0:T(8,128)(2,1)S(1)}, u32[]{:S(2)}, u32[]{:S(2)}) collective-permute-start(bf16[8,768]{1,0:T(8,128)(2,1)S(1)} %get-tuple-element.33.after_ref), channel_id=1, source_target_pairs={{0,1},{1,2},{2,3},{3,4},{4,5},{5,6},{6,7},{7,8},{8,9},{9,10},{10,1... | collective-permute-start | bytes 36872 | tf_op jit(solution)/shard_map/ppermute | solution.py:555
